TPU v7x, 128 devices: a whole 4x4x4 slice. The times are simulated.
128 devices in a mesh: seq: 64 (over x, z, y), head: 2 (over core).
Axes of the slice: x: 4, y: 4, z: 4, core: 2. Of those that a mesh axis runs over, the one named last changes fastest.
Arguments:
- video_query: bfloat16 [32768, 3072], P('seq', 'head'), as said below
- video_value: bfloat16 [32768, 3072], P('seq', 'head'), may hold values from -12 to 12
- audio_key: bfloat16 [16384, 3072], P('seq', 'head'), as said below
- audio_value: bfloat16 [16384, 3072], P('seq', 'head'), may hold values from -12 to 12
- video_proj: bfloat16 [3072, 3072], P('head'), may hold values from -0.109375 to 0.109375
- audio_proj: bfloat16 [3072, 3072], P('head'), may hold values from -0.109375 to 0.109375
- pair_first: int32 [64], replicated, may hold values from 0 to 63, as said below
- pair_count: int32 [64], replicated, may hold values from 1 to 5, as said below
Outputs:
- video_out: bfloat16 [32768, 3072], P('seq', 'head')
- audio_out: bfloat16 [16384, 3072], P('seq', 'head')
Inputs may be any that keep to these rules, and one draw needn't show every extreme that they name: Video block b pairs with the audio blocks pair_first[b] to pair_first[b] + pair_count[b] - 1; these lie within b - 2 to b + 2, inside 0 to 63, and always include block b. `pair_count`: some video block pairs with 5 audio blocks in every draw. `video_query`: entries lie within -8 to 8. `audio_key`: entries lie within -8 to 8.
All inputs are finite; a program needn't handle non-finite values.
Results may differ from a plain program's by a relative error of at most 0.0052.
Values may be sent and summed in bfloat16 or wider, within the bound.
No kernel may reach another device: no remote copies, remote signals or barrier semaphores. Data moves between devices by JAX's collectives and lax.ppermute only.
A program may use at most 192 MiB of HBM per device.

v0:
```python
import math

import jax
import jax.numpy as jnp
from jax import lax
from jax.sharding import PartitionSpec as P

HEAD_DIM = 128
HALF = 2


NEG = -1e30


def shifted(x, axis, by):
    size = lax.axis_size(axis)
    pairs = [(i, i + by) for i in range(size) if 0 <= i + by < size]
    return lax.ppermute(x, axis, pairs)


def tile_scores(query, keys):
    return jnp.einsum("vhe,ahe->hva", query, keys, preferred_element_type=jnp.float32) / math.sqrt(
        HEAD_DIM
    )


def row_piece(scores, values):
    top = jnp.max(scores, axis=2)
    expo = jnp.exp(scores - top[:, :, None])
    total = jnp.sum(expo, axis=2)
    out = jnp.einsum(
        "hva,ahe->vhe", expo.astype(jnp.bfloat16), values, preferred_element_type=jnp.float32
    )
    return (top, total, out)


def col_piece(scores, values):
    top = jnp.max(scores, axis=1)
    expo = jnp.exp(scores - top[:, None, :])
    total = jnp.sum(expo, axis=1)
    out = jnp.einsum(
        "hva,vhe->ahe", expo.astype(jnp.bfloat16), values, preferred_element_type=jnp.float32
    )
    return (top, total, out)


def combine(acc, part):
    top_a, total_a, out_a = acc
    top_b, total_b, out_b = part
    top = jnp.maximum(top_a, top_b)
    old = jnp.exp(top_a - top)
    new = jnp.exp(top_b - top)
    return (
        top,
        total_a * old + total_b * new,
        out_a * old.T[:, :, None] + out_b * new.T[:, :, None],
    )


def empty_acc(heads, rows):
    return (
        jnp.full((heads, rows), NEG, jnp.float32),
        jnp.zeros((heads, rows), jnp.float32),
        jnp.zeros((rows, heads, HEAD_DIM), jnp.float32),
    )


def finish(acc):
    top, total, out = acc
    result = (out / total.T[:, :, None]).astype(jnp.bfloat16)
    return result.reshape(result.shape[0], result.shape[1] * result.shape[2])


def shards(
    video_query, video_value, audio_key, audio_value, video_proj, audio_proj, pair_first, pair_count
):
    heads = video_query.shape[1] // HEAD_DIM
    vid = video_query.shape[0]
    aud = audio_key.shape[0]
    nblocks = lax.axis_size("seq")
    me = lax.axis_index("seq")
    first = pair_first[me]
    count = pair_count[me]
    query = video_query.reshape(vid, heads, HEAD_DIM)
    own_keys = audio_key.reshape(aud, heads, HEAD_DIM)
    audio_pair = jnp.stack([audio_key, audio_value])
    video_pair = jnp.stack([video_query, video_value])
    video_acc = empty_acc(heads, vid)
    audio_acc = empty_acc(heads, aud)
    for offset in range(-HALF, HALF + 1):
        if offset == 0:
            arrived = audio_pair
        else:
            arrived = shifted(audio_pair, "seq", -offset)
        keys = arrived[0].reshape(aud, heads, HEAD_DIM)
        aud_vals = arrived[1].reshape(aud, heads, HEAD_DIM)
        target = me + offset
        valid = (target >= first) & (target < first + count)
        source = me - offset
        clipped = jnp.clip(source, 0, nblocks - 1)
        from_source = (
            (source >= 0)
            & (source < nblocks)
            & (pair_first[clipped] <= me)
            & (me < pair_first[clipped] + pair_count[clipped])
        )

        def video_side(unused):
            return row_piece(tile_scores(query, keys), aud_vals)

        def no_video(unused):
            return empty_acc(heads, vid)

        video_acc = combine(video_acc, lax.cond(valid, video_side, no_video, 0))
        if offset == 0:
            visiting = video_pair
        else:
            visiting = shifted(video_pair, "seq", offset)

        def audio_side(unused):
            visit_query = visiting[0].reshape(vid, heads, HEAD_DIM)
            visit_vals = visiting[1].reshape(vid, heads, HEAD_DIM)
            return col_piece(tile_scores(visit_query, own_keys), visit_vals)

        def no_audio(unused):
            return empty_acc(heads, aud)

        audio_acc = combine(audio_acc, lax.cond(from_source, audio_side, no_audio, 0))
    video_attn = finish(video_acc)
    audio_attn = finish(audio_acc)
    video_term = jnp.dot(video_attn, video_proj, preferred_element_type=jnp.float32)
    audio_term = jnp.dot(audio_attn, audio_proj, preferred_element_type=jnp.float32)
    video_sum, audio_sum = (
        lax.psum_scatter(video_term, "head", scatter_dimension=1, tiled=True),
        lax.psum_scatter(audio_term, "head", scatter_dimension=1, tiled=True),
    )
    return (video_sum.astype(jnp.bfloat16), audio_sum.astype(jnp.bfloat16))


def solution(mesh):
    in_specs = (
        P("seq", "head"),
        P("seq", "head"),
        P("seq", "head"),
        P("seq", "head"),
        P("head", None),
        P("head", None),
        P(),
        P(),
    )
    out_specs = (P("seq", "head"), P("seq", "head"))
    return jax.shard_map(shards, mesh=mesh, in_specs=in_specs, out_specs=out_specs, check_vma=False)
```

profile of v0, /device:TPU:1, one launch (start us, length us, event | category | flops | bytes accessed | tf_op | source)
XLA Modules:
  0.0 527.0 jit_solution(5992770864245962287)
XLA Ops:
  10.6 3.4 pad_maximum_fusion
  14.1 7.3 %collective-permute-start.7 = (bf16[2,512,1536]{1,2,0:T(8,128)(2,1)}, bf16[2,512,1536]{1,2,0:T(8,128)(2,1)}, u32[]{:S(2)}, u32[]{:S(2)}) collective-permute-start(bf16[2,512,1536]{1,2,0:T(8,128)(2,1)} %pad_maximum_fusion), channel_id=1, source_target_pairs={{0,4},{2,6},{4,8},{6,10},{8,12},{10,14},{12,16},{14,18},{16,20},{1... | collective-permute-start | bytes 9437192 | tf_op jit(solution)/shard_map/ppermute | solution.py:18
  21.4 4.0 collective-permute-start.6
  38.3 19.2 %conditional.17 = (f32[12,256]{1,0:T(8,128)S(1)}, f32[12,256]{1,0:T(8,128)S(1)}, f32[256,12,128]{0,2,1:T(8,128)}) conditional(s32[]{:T(128)} %convert_element_type.81, () %tuple.102, (bf16[512,1536]{1,0:T(8,128)(2,1)}, bf16[256,12,128]{0,2,1:T(8,128)(2,1)S(1)}, bf16[512,1536]{1,0:T(8,128)(2,1)}) %tuple.222), branch_computations={%region_29.30_spmd, %region_30.33_spmd} | conditional | flops 817883136 | bytes 59129964 | solution.py:128
  38.4 2.6 copy.74
  41.0 2.4 multiply_reduce_fusion.7
  46.1 2.6 copy.76
  48.7 5.8 %fusion.76 = f32[256,12,128]{2,0,1:T(8,128)} fusion(bf16[512,12,128]{0,2,1:T(8,128)(2,1)} %bitcast.154, f32[12,512,256]{2,1,0:T(8,128)} %copy-done, f32[12,256]{1,0:T(8,128)S(1)} %get-tuple-element.304), kind=kOutput, calls=%fused_computation.70 | convolution fusion | flops 407371776 | bytes 9449472 | tf_op jit(solution)/shard_map/cond/branch_1_fun/hva,vhe->ahe/dot_general | solution.py:41
  54.5 3.1 copy.137
  57.6 29.3 %collective-permute-done.7 = bf16[2,512,1536]{1,2,0:T(8,128)(2,1)} collective-permute-done((bf16[2,512,1536]{1,2,0:T(8,128)(2,1)}, bf16[2,512,1536]{1,2,0:T(8,128)(2,1)}, u32[]{:S(2)}, u32[]{:S(2)}) %collective-permute-start.7) | collective-permute-done | bytes 3145760 | tf_op jit(solution)/shard_map/ppermute | solution.py:18
  88.1 66.1 %collective-permute-done.6 = bf16[2,512,1536]{1,2,0:T(8,128)(2,1)} collective-permute-done((bf16[2,512,1536]{1,2,0:T(8,128)(2,1)}, bf16[2,512,1536]{1,2,0:T(8,128)(2,1)}, u32[]{:S(2)}, u32[]{:S(2)}) %collective-permute-start.6) | collective-permute-done | bytes 3145760 | tf_op jit(solution)/shard_map/ppermute | solution.py:18
  155.8 134.3 %collective-permute-done.5 = bf16[2,512,1536]{1,2,0:T(8,128)(2,1)} collective-permute-done((bf16[2,512,1536]{1,2,0:T(8,128)(2,1)}, bf16[2,512,1536]{1,2,0:T(8,128)(2,1)}, u32[]{:S(2)}, u32[]{:S(2)}) %collective-permute-start.5) | collective-permute-done | bytes 3145760 | tf_op jit(solution)/shard_map/ppermute | solution.py:18
  293.2 4.8 divide_convert_fusion.1
  297.9 8.0 %fusion.147 = f32[256,3072]{1,0:T(8,128)} fusion(bf16[256,1536]{0,1:T(8,128)(2,1)S(1)} %bitcast.161, bf16[1536,3072]{1,0:T(8,128)(2,1)} %param.33), kind=kOutput, calls=%fused_computation.163 | convolution fusion | flops 2415919104 | bytes 13369344 | tf_op jit(solution)/shard_map/dot_general | solution.py:132
  308.3 2.4 pad_maximum_fusion.1
  313.3 11.6 %collective-permute-start.1 = (bf16[2,256,1536]{1,2,0:T(8,128)(2,1)}, bf16[2,256,1536]{1,2,0:T(8,128)(2,1)}, u32[]{:S(2)}, u32[]{:S(2)}) collective-permute-start(bf16[2,256,1536]{1,2,0:T(8,128)(2,1)} %pad_maximum_fusion.1), channel_id=1, source_target_pairs={{0,2},{2,4},{4,6},{6,8},{8,10},{10,12},{12,14},{14,16},{16,18},{18... | collective-permute-start | bytes 4718600 | tf_op jit(solution)/shard_map/ppermute | solution.py:18
  324.8 6.1 %collective-permute-start = (bf16[2,256,1536]{1,2,0:T(8,128)(2,1)}, bf16[2,256,1536]{1,2,0:T(8,128)(2,1)}, u32[]{:S(2)}, u32[]{:S(2)}) collective-permute-start(bf16[2,256,1536]{1,2,0:T(8,128)(2,1)} %pad_maximum_fusion.1), channel_id=1, source_target_pairs={{0,4},{2,6},{4,8},{6,10},{8,12},{10,14},{12,16},{14,18},{16,20},{1... | collective-permute-start | bytes 4718600 | tf_op jit(solution)/shard_map/ppermute | solution.py:18
  335.3 13.6 %conditional.12 = (f32[12,512]{1,0:T(8,128)S(1)}, f32[12,512]{1,0:T(8,128)S(1)}, f32[512,12,128]{0,2,1:T(8,128)}) conditional(s32[]{:T(128)} %convert_element_type.74, () %tuple.92, (bf16[512,12,128]{0,2,1:T(8,128)(2,1)S(1)}, bf16[256,12,128]{0,2,1:T(8,128)(2,1)S(1)}, bf16[256,1536]{1,0:T(8,128)(2,1)S(1)}) %tuple.228), branch_computations={%region_8.9_spmd, %region_9.12_spmd} | conditional | flops 817876992 | bytes 58490988 | solution.py:114
  339.4 5.9 %fusion.26 = f32[512,12,128]{2,0,1:T(8,128)} fusion(bf16[256,12,128]{0,2,1:T(8,128)(2,1)S(1)} %bitcast.162, f32[12,512,256]{1,2,0:T(8,128)} %copy-done.1, f32[12,512]{1,0:T(8,128)S(1)} %get-tuple-element.274), kind=kOutput, calls=%fused_computation.25 | convolution fusion | flops 407371776 | bytes 10248192 | tf_op jit(solution)/shard_map/cond/branch_1_fun/hva,ahe->vhe/dot_general | solution.py:31
  345.3 3.5 copy.127
  348.9 2.1 conditional.14
  350.9 39.3 %collective-permute-done.2 = bf16[2,256,1536]{1,2,0:T(8,128)(2,1)} collective-permute-done((bf16[2,256,1536]{1,2,0:T(8,128)(2,1)}, bf16[2,256,1536]{1,2,0:T(8,128)(2,1)}, u32[]{:S(2)}, u32[]{:S(2)}) %collective-permute-start.2) | collective-permute-done | bytes 1572896 | tf_op jit(solution)/shard_map/ppermute | solution.py:18
  390.2 2.3 conditional.13
  392.5 2.1 conditional.11
  392.5 2.1 broadcast.144.clone
  394.6 29.3 %collective-permute-done = bf16[2,256,1536]{1,2,0:T(8,128)(2,1)} collective-permute-done((bf16[2,256,1536]{1,2,0:T(8,128)(2,1)}, bf16[2,256,1536]{1,2,0:T(8,128)(2,1)}, u32[]{:S(2)}, u32[]{:S(2)}) %collective-permute-start) | collective-permute-done | bytes 1572896 | tf_op jit(solution)/shard_map/ppermute | solution.py:18
  423.9 2.3 conditional.10
  426.3 7.0 %divide_convert_fusion = bf16[512,12,128]{0,2,1:T(8,128)(2,1)S(1)} fusion(f32[512,12,128]{0,2,1:T(8,128)} %get-tuple-element.175, f32[512,12,128]{0,2,1:T(8,128)} %get-tuple-element.174, f32[512,12,128]{0,2,1:T(8,128)} %get-tuple-element.173, f32[512,12,128]{0,2,1:T(8,128)} %get-tuple-element.172, f32[512,12,128]{0,2,1:T(8,128)} %get-tuple-element.171, ...), kind=kLoop, calls=%fused_computation.91 | loop fusion | flops 12582912 | bytes 17571840 | tf_op jit(solution)/shard_map/convert_element_type | solution.py:70
  433.4 10.7 %fusion.146 = f32[512,3072]{1,0:T(8,128)} fusion(bf16[512,1536]{0,1:T(8,128)(2,1)S(1)} %bitcast.172, bf16[1536,3072]{1,0:T(8,128)(2,1)} %param.32), kind=kOutput, calls=%fused_computation.162 | convolution fusion | flops 4831838208 | bytes 17301504 | tf_op jit(solution)/shard_map/dot_general | solution.py:131
  444.2 2.4 convert_element_type.85
  446.6 70.0 %reduce-scatter.3.cloned.1.call-done = f32[512,1536]{1,0:T(8,128)} async-done(((f32[512,3072]{1,0:T(8,128)}), f32[512,1536]{1,0:T(8,128)}) %reduce-scatter.3.cloned.1.call-update) | async-done | bytes 3145744 | tf_op jit(solution)/shard_map/reduce_scatter | solution.py:134
  516.5 3.2 convert_element_type.78
  (74 shorter events, 35.8 us)
Async XLA Ops:
  7.2 1.9 copy-start.2
  7.2 437.0 %reduce-scatter.5.cloned.1.call-start = ((), (), s32[]{:S(2)}) async-start(), calls=%async_computation.3 | async-start | bytes 4718592 | tf_op jit(solution)/shard_map/reduce_scatter | solution.py:135
  10.6 17.3 %copy-start.10 = (bf16[256,1536]{1,0:T(8,128)(2,1)S(1)}, bf16[256,1536]{1,0:T(8,128)(2,1)}, u32[]{:S(2)}) copy-start(bf16[256,1536]{1,0:T(8,128)(2,1)} %param.30) | copy-start | bytes 2359300
  10.6 17.6 %copy-start.25 = (s32[64]{0:T(128)S(1)}, s32[64]{0:T(128)}, u32[]{:S(2)}) copy-start(s32[64]{0:T(128)} %param.35) | copy-start | bytes 772
  10.6 17.6 %copy-start.26 = (s32[64]{0:T(128)S(1)}, s32[64]{0:T(128)}, u32[]{:S(2)}) copy-start(s32[64]{0:T(128)} %param.34) | copy-start | bytes 772
  14.1 72.8 %collective-permute-start.7 = (bf16[2,512,1536]{1,2,0:T(8,128)(2,1)}, bf16[2,512,1536]{1,2,0:T(8,128)(2,1)}, u32[]{:S(2)}, u32[]{:S(2)}) collective-permute-start(bf16[2,512,1536]{1,2,0:T(8,128)(2,1)} %pad_maximum_fusion), channel_id=1, source_target_pairs={{0,4},{2,6},{4,8},{6,10},{8,12},{10,14},{12,16},{14,18},{16,20},{1... | collective-permute-start | bytes 9437192 | tf_op jit(solution)/shard_map/ppermute | solution.py:18
  21.4 132.8 %collective-permute-start.6 = (bf16[2,512,1536]{1,2,0:T(8,128)(2,1)}, bf16[2,512,1536]{1,2,0:T(8,128)(2,1)}, u32[]{:S(2)}, u32[]{:S(2)}) collective-permute-start(bf16[2,512,1536]{1,2,0:T(8,128)(2,1)} %pad_maximum_fusion), channel_id=1, source_target_pairs={{0,2},{2,4},{4,6},{6,8},{8,10},{10,12},{12,14},{14,16},{16,18},{18... | collective-permute-start | bytes 9437192 | tf_op jit(solution)/shard_map/ppermute | solution.py:18
  25.4 264.7 %collective-permute-start.5 = (bf16[2,512,1536]{1,2,0:T(8,128)(2,1)}, bf16[2,512,1536]{1,2,0:T(8,128)(2,1)}, u32[]{:S(2)}, u32[]{:S(2)}) collective-permute-start(bf16[2,512,1536]{1,2,0:T(8,128)(2,1)} %pad_maximum_fusion), channel_id=1, source_target_pairs={{2,0},{4,2},{6,4},{8,6},{10,8},{12,10},{14,12},{16,14},{18,16},{20... | collective-permute-start | bytes 9437192 | tf_op jit(solution)/shard_map/ppermute | solution.py:18
  26.6 264.8 %collective-permute-start.4 = (bf16[2,512,1536]{1,2,0:T(8,128)(2,1)}, bf16[2,512,1536]{1,2,0:T(8,128)(2,1)}, u32[]{:S(2)}, u32[]{:S(2)}) collective-permute-start(bf16[2,512,1536]{1,2,0:T(8,128)(2,1)} %pad_maximum_fusion), channel_id=1, source_target_pairs={{4,0},{6,2},{8,4},{10,6},{12,8},{14,10},{16,12},{18,14},{20,16},{2... | collective-permute-start | bytes 9437192 | tf_op jit(solution)/shard_map/ppermute | solution.py:18
  43.4 2.7 copy-start
  43.4 5.2 copy-start.15
  54.5 3.1 copy-start.16
  306.0 1.1 copy-start.3
  306.0 210.5 %reduce-scatter.3.cloned.1.call-start = ((), (), s32[]{:S(2)}) async-start(), calls=%async_computation.2 | async-start | bytes 9437184 | tf_op jit(solution)/shard_map/reduce_scatter | solution.py:134
  310.7 38.2 %collective-permute-start.3 = (bf16[2,256,1536]{1,2,0:T(8,128)(2,1)}, bf16[2,256,1536]{1,2,0:T(8,128)(2,1)}, u32[]{:S(2)}, u32[]{:S(2)}) collective-permute-start(bf16[2,256,1536]{1,2,0:T(8,128)(2,1)} %pad_maximum_fusion.1), channel_id=1, source_target_pairs={{4,0},{6,2},{8,4},{10,6},{12,8},{14,10},{16,12},{18,14},{20,16},{2... | collective-permute-start | bytes 4718600 | tf_op jit(solution)/shard_map/ppermute | solution.py:18
  312.0 78.3 %collective-permute-start.2 = (bf16[2,256,1536]{1,2,0:T(8,128)(2,1)}, bf16[2,256,1536]{1,2,0:T(8,128)(2,1)}, u32[]{:S(2)}, u32[]{:S(2)}) collective-permute-start(bf16[2,256,1536]{1,2,0:T(8,128)(2,1)} %pad_maximum_fusion.1), channel_id=1, source_target_pairs={{2,0},{4,2},{6,4},{8,6},{10,8},{12,10},{14,12},{16,14},{18,16},{20... | collective-permute-start | bytes 4718600 | tf_op jit(solution)/shard_map/ppermute | solution.py:18
  313.3 79.2 %collective-permute-start.1 = (bf16[2,256,1536]{1,2,0:T(8,128)(2,1)}, bf16[2,256,1536]{1,2,0:T(8,128)(2,1)}, u32[]{:S(2)}, u32[]{:S(2)}) collective-permute-start(bf16[2,256,1536]{1,2,0:T(8,128)(2,1)} %pad_maximum_fusion.1), channel_id=1, source_target_pairs={{0,2},{2,4},{4,6},{6,8},{8,10},{10,12},{12,14},{14,16},{16,18},{18... | collective-permute-start | bytes 4718600 | tf_op jit(solution)/shard_map/ppermute | solution.py:18
  324.8 99.1 %collective-permute-start = (bf16[2,256,1536]{1,2,0:T(8,128)(2,1)}, bf16[2,256,1536]{1,2,0:T(8,128)(2,1)}, u32[]{:S(2)}, u32[]{:S(2)}) collective-permute-start(bf16[2,256,1536]{1,2,0:T(8,128)(2,1)} %pad_maximum_fusion.1), channel_id=1, source_target_pairs={{0,4},{2,6},{4,8},{6,10},{8,12},{10,14},{12,16},{14,18},{16,20},{1... | collective-permute-start | bytes 4718600 | tf_op jit(solution)/shard_map/ppermute | solution.py:18
  336.5 2.7 copy-start.1
  336.5 2.9 copy-start.4
  345.3 3.5 copy-start.5
Sparse Core Ops, SparseCore 0:
  306.1 60.9 reduce-scatter.4
  444.3 72.2 reduce-scatter.2
where the time goes:
time: 536 us; the launch traced here: 527 us
  waiting for transfers between devices  368 us (69%)
  local copies, waits for them, and re-layouts  35.3 us (7%)
  starting transfers between devices  34.2 us (6%)
  matrix products  33.9 us (6%)
  between operations  28.4 us (5%)
  other arithmetic  25.5 us (5%)
    ppermute x8, waiting for transfers between devices, shifted(): return lax.ppermute(x, axis, pairs)  298 us
    reduce_scatter x1, waiting for transfers between devices, shards(): lax.psum_scatter(video_term, 'head', scatter_dimension=1, tiled=True)  70 us
    ppermute x8, starting transfers between devices, shifted(): return lax.ppermute(x, axis, pairs)  34.1 us
    another operation x27, local copies, waits for them, and re-layouts  18.9 us
    convert_element_type x2, other arithmetic, finish(): result = (out / total.T[:, :, None]).astype(jnp.bfloat16)  11.8 us
    dot_general x1, matrix products, shards(): jnp.dot(video_attn, video_proj, preferred_element_type=jnp.float32)  10.7 us
  transfers between devices with their start and end apart: 10, of which 6 were waited for; matrix products, arithmetic and copies ran while one was open for 13% of the time, Pallas kernels for 0%

commit v1 on v0

v1 whole, which is shorter than its diff:
```python
import functools
import math

import jax
import jax.numpy as jnp
from jax import lax
from jax.experimental import pallas as pl
from jax.experimental.pallas import tpu as pltpu
from jax.sharding import PartitionSpec as P

HD = 128
LINE = 4
GH = 3
GW = GH * HD
VID = 512
AUD = 256
NEG = -1e30
SCALE = math.log2(math.e) / math.sqrt(HD)
EXTRA = 16
BF = jnp.bfloat16
F32 = jnp.float32
ANY = pl.BlockSpec(memory_space=pl.ANY)
SMEM = pl.BlockSpec(memory_space=pltpu.SMEM)
VMEM = pl.BlockSpec(memory_space=pltpu.VMEM)


def group_cols(g):
    return pl.ds(pl.multiple_of(g * GW, HD), GW)


def run_copies(copies):
    for copy in copies:
        copy.start()
    for copy in copies:
        copy.wait()


def pack_kernel(me, a, b, out1, out2, out3, sem):
    y = lax.rem(me[0], LINE)
    copies = []
    for d, out in ((1, out1), (3, out3), (2, out2)):
        cols = group_cols(lax.rem(y + d, LINE))
        copies.append(pltpu.make_async_copy(a.at[:, cols], out.at[0], sem.at[2 * d]))
        copies.append(pltpu.make_async_copy(b.at[:, cols], out.at[1], sem.at[2 * d + 1]))
    run_copies(copies)


def pack(me, a, b):
    piece = jax.ShapeDtypeStruct((2, a.shape[0], GW), BF)
    return pl.pallas_call(
        pack_kernel,
        out_shape=(piece,) * 3,
        in_specs=[SMEM, ANY, ANY],
        out_specs=(ANY,) * 3,
        scratch_shapes=[pltpu.SemaphoreType.DMA((8,))],
        name="pack",
    )(me, a, b)


def line_kernel(me, k, v, kv1, kv2, kv3, low, high, sem):
    y = lax.rem(me[0], LINE)
    cols = group_cols(y)
    for d, got in ((0, None), (1, kv1), (2, kv2), (3, kv3)):
        j = lax.rem(y + LINE - d, LINE)

        def place(out, at):
            if d == 0:
                pltpu.make_async_copy(k.at[:, cols], out.at[at, 0], sem.at[0]).start()
                pltpu.make_async_copy(v.at[:, cols], out.at[at, 1], sem.at[4]).start()
            else:
                pltpu.make_async_copy(got, out.at[at], sem.at[d]).start()

        @pl.when(j < 2)
        def _():
            place(low, j)

        @pl.when(j >= 2)
        def _():
            place(high, j - 2)

    pltpu.make_async_copy(k.at[:, cols], low.at[0, 0], sem.at[0]).wait()
    pltpu.make_async_copy(v.at[:, cols], low.at[0, 1], sem.at[4]).wait()
    for d, got in ((1, kv1), (2, kv2), (3, kv3)):
        pltpu.make_async_copy(got, low.at[0], sem.at[d]).wait()


def line_blocks(me, k, v, kv1, kv2, kv3):
    half = jax.ShapeDtypeStruct((2, 2, AUD, GW), BF)
    return pl.pallas_call(
        line_kernel,
        out_shape=(half, half),
        in_specs=[SMEM] + [ANY] * 5,
        out_specs=(ANY, ANY),
        scratch_shapes=[pltpu.SemaphoreType.DMA((5,))],
        name="line_blocks",
    )(me, k, v, kv1, kv2, kv3)


def attend_kernel(steps, own, carried, last, *refs):
    refs = list(refs)

    def take(n):
        part = refs[:n]
        del refs[:n]
        return part

    me, first, count = take(3)
    kvs = take(4)
    q_own, v_own = take(2) if own else (None, None)
    arrived = take(len(steps) - (1 if own else 0))
    u_in, c_in = take(2) if carried else (None, None)
    outs = take(len(steps))
    if last:
        before, after, u_out, c_out = take(4)
    else:
        u_out, c_out = take(2)
    kbuf, qbuf, obuf, tbuf, mbuf, cbuf, abuf, vtbuf, ubuf, csum, sem = refs

    y = lax.rem(me[0], LINE)
    base = me[0] - y
    copies = []

    def copy(src, dst):
        copies.append(pltpu.make_async_copy(src, dst, sem.at[len(copies)]))

    for i, part in enumerate(kvs):
        copy(part, kbuf.at[pl.ds(2 * i, 2)])
    if own:
        copy(q_own.at[:, group_cols(y)], qbuf.at[0, 0])
        copy(v_own.at[:, group_cols(y)], qbuf.at[0, 1])
    for i, part in enumerate(arrived):
        copy(part, qbuf.at[i + (1 if own else 0)])
    if carried:
        copy(u_in, ubuf)
        copy(c_in, csum)
    for c in copies:
        c.start()
    if not carried:
        ubuf[...] = jnp.zeros_like(ubuf)
        csum[...] = jnp.full_like(csum, NEG)
    for c in copies:
        c.wait()

    def video(i, carry):
        step = jnp.int32(steps[0])
        for n in range(1, len(steps)):
            step = jnp.where(i == n, steps[n], step)
        v = lax.rem(y + LINE - step, LINE)
        lo = first[base + v] - base + 2
        hi = lo + count[base + v]
        mbuf[...] = jnp.full_like(mbuf, NEG)

        def scores(a, carry):
            slot = a - lo
            for h in range(GH):
                cols = slice(h * HD, (h + 1) * HD)
                t = lax.dot_general(
                    qbuf[i, 0, :, cols], kbuf[a, 0, :, cols], (((1,), (1,)), ((), ())), preferred_element_type=F32
                )
                t = t * SCALE
                tbuf[h, slot] = t
                mbuf[h] = jnp.maximum(mbuf[h], jnp.maximum(t[:, :HD], t[:, HD:]))
                cbuf[h, slot] = jnp.broadcast_to(jnp.max(t, axis=0, keepdims=True), (8, AUD))
            return carry

        lax.fori_loop(lo, hi, scores, 0)
        for h in range(GH):
            cols = slice(h * HD, (h + 1) * HD)
            mbuf[h] = jnp.broadcast_to(jnp.max(mbuf[h], axis=1, keepdims=True), (VID, HD))
            abuf[h] = jnp.zeros((VID, 2 * HD), F32)
            vtbuf[h, :HD] = qbuf[i, 1, :, cols].T
            vtbuf[h, HD:] = jnp.ones((EXTRA, VID), BF)

        def weights(a, carry):
            slot = a - lo
            for h in range(GH):
                cols = slice(h * HD, (h + 1) * HD)
                t = tbuf[h, slot]
                r = mbuf[h]
                c = cbuf[h, slot, 0:1]
                by_row = jnp.exp2(t - jnp.concatenate([r, r], axis=1)).astype(BF)
                values = jnp.concatenate([kbuf[a, 1, :, cols], jnp.ones((AUD, HD), BF)], axis=1)
                abuf[h] += jnp.dot(by_row, values, preferred_element_type=F32)
                by_col = jnp.exp2(t - c).astype(BF)
                u = jnp.dot(vtbuf[h], by_col, preferred_element_type=F32)
                old = csum[h, a, 0:1]
                new = jnp.maximum(old, c)
                ubuf[h, a] = ubuf[h, a] * jnp.exp2(old - new) + u * jnp.exp2(c - new)
                csum[h, a] = jnp.broadcast_to(new, (8, AUD))
            return carry

        lax.fori_loop(lo, hi, weights, 0)
        for h in range(GH):
            obuf[i, :, h * HD : (h + 1) * HD] = (abuf[h, :, :HD] / abuf[h, :, HD:]).astype(BF)
        return carry

    lax.fori_loop(0, len(steps), video, 0)

    copies = [pltpu.make_async_copy(obuf.at[i], out, sem.at[i]) for i, out in enumerate(outs)]
    for c in copies:
        c.start()
    if last:
        row = lax.broadcasted_iota(jnp.int32, (EXTRA, AUD), 0)
        for place, out in ((0, before), (6, after)):
            for j in range(2):
                for h in range(GH):
                    u = ubuf[h, place + j, :HD]
                    n = ubuf[h, place + j, HD : HD + 1]
                    some = n > 0.0
                    safe = jnp.where(some, n, 1.0)
                    out[j, h, :HD] = (u / safe).astype(BF)
                    level = jnp.where(some, csum[h, place + j, 0:1] + jnp.log2(safe), NEG)
                    hi = level.astype(BF).astype(F32)
                    mid = (level - hi).astype(BF).astype(F32)
                    lo = level - hi - mid
                    parts = jnp.where(row == 0, hi, jnp.where(row == 1, mid, jnp.where(row == 2, lo, 0.0)))
                    out[j, h, HD:] = parts.astype(BF)
        for h in range(GH):
            u_out[h] = ubuf[h, 2:6]
            c_out[h] = csum[h, 2:6]
    else:
        more = [
            pltpu.make_async_copy(ubuf, u_out, sem.at[len(outs)]),
            pltpu.make_async_copy(csum, c_out, sem.at[len(outs) + 1]),
        ]
        for c in more:
            c.start()
        copies += more
    for c in copies:
        c.wait()


def attend(steps, info, kvs, own, arrived, sums, last):
    n = len(steps)
    n_idx = 2 * LINE
    out_shape = [jax.ShapeDtypeStruct((VID, GW), BF)] * n
    out_specs = [ANY] * n
    if last:
        halo = jax.ShapeDtypeStruct((2, GH, HD + EXTRA, AUD), BF)
        out_shape += [halo, halo]
        out_shape += [
            jax.ShapeDtypeStruct((GH, LINE, HD + EXTRA, AUD), F32),
            jax.ShapeDtypeStruct((GH, LINE, 8, AUD), F32),
        ]
        out_specs += [VMEM] * 4
    else:
        out_shape += [
            jax.ShapeDtypeStruct((GH, n_idx, HD + EXTRA, AUD), F32),
            jax.ShapeDtypeStruct((GH, n_idx, 8, AUD), F32),
        ]
        out_specs += [ANY] * 2
    operands = [*info, *kvs, *own, *arrived, *sums]
    tiles = 4 * n * GH
    return pl.pallas_call(
        functools.partial(attend_kernel, steps, bool(own), bool(sums), last),
        out_shape=tuple(out_shape),
        in_specs=[SMEM] * 3 + [ANY] * (len(operands) - 3),
        out_specs=tuple(out_specs),
        scratch_shapes=[
            pltpu.VMEM((n_idx, 2, AUD, GW), BF),
            pltpu.VMEM((n, 2, VID, GW), BF),
            pltpu.VMEM((n, VID, GW), BF),
            pltpu.VMEM((GH, 5, VID, AUD), F32),
            pltpu.VMEM((GH, VID, HD), F32),
            pltpu.VMEM((GH, 5, 8, AUD), F32),
            pltpu.VMEM((GH, VID, 2 * HD), F32),
            pltpu.VMEM((GH, HD + EXTRA, VID), BF),
            pltpu.VMEM((GH, n_idx, HD + EXTRA, AUD), F32),
            pltpu.VMEM((GH, n_idx, 8, AUD), F32),
            pltpu.SemaphoreType.DMA((12,)),
        ],
        compiler_params=pltpu.CompilerParams(vmem_limit_bytes=40 * 2**20),
        cost_estimate=pl.CostEstimate(
            flops=tiles * 6 * VID * AUD * HD, bytes_accessed=8 * 2**20, transcendentals=tiles * 2 * VID * AUD
        ),
        name="attend_last" if last else "attend",
    )(*operands)


def merge_kernel(me, u, c, prev, nxt, out0, out1, out2, out3):
    y = lax.rem(me[0], LINE)
    for d, out in enumerate((out0, out1, out2, out3)):
        j = lax.rem(y + d, LINE)
        for h in range(GH):
            low = j < 2
            at = lax.rem(j, 2)
            got = jnp.where(low, prev[at, h].astype(F32), nxt[at, h].astype(F32))
            level = got[HD : HD + 1] + got[HD + 1 : HD + 2] + got[HD + 2 : HD + 3]
            n = u[h, j, HD : HD + 1]
            own = c[h, j, 0:1] + jnp.log2(n)
            top = jnp.maximum(own, level)
            own_w = jnp.exp2(own - top)
            got_w = jnp.exp2(level - top)
            total = own_w + got_w
            mixed = u[h, j, :HD] * (own_w / (n * total)) + got[:HD] * (got_w / total)
            out[:, h * HD : (h + 1) * HD] = mixed.T.astype(BF)


def merge(me, u, c, prev, nxt):
    return pl.pallas_call(
        merge_kernel,
        out_shape=(jax.ShapeDtypeStruct((AUD, GW), BF),) * LINE,
        in_specs=[SMEM] + [VMEM] * 4,
        out_specs=(VMEM,) * LINE,
        name="merge",
        compiler_params=pltpu.CompilerParams(vmem_limit_bytes=24 * 2**20),
    )(me, u, c, prev, nxt)


def project_kernel(place, *refs):
    mine, theirs = refs[:LINE], refs[LINE : 2 * LINE]
    w_mine, w_theirs, out, left, right = refs[2 * LINE :]
    y = place[0]

    @pl.when(pl.program_id(0) == 0)
    def _():
        for d in range(LINE):
            cols = group_cols(lax.rem(y + d, LINE))
            left[:, cols] = mine[d][...]
            right[:, cols] = theirs[d][...]

    total = jnp.dot(left[...], w_mine[...], preferred_element_type=F32)
    total += jnp.dot(right[...], w_theirs[...], preferred_element_type=F32)
    out[...] = total.astype(BF)


def project(place, mine, theirs, w, w_theirs):
    rows = mine[0].shape[0]
    width = w_theirs.shape[1]
    tile = 256
    full = pl.BlockSpec((rows, GW), lambda n, s: (0, 0))
    return pl.pallas_call(
        project_kernel,
        out_shape=jax.ShapeDtypeStruct((rows, width), BF),
        grid_spec=pltpu.PrefetchScalarGridSpec(
            num_scalar_prefetch=1,
            grid=(width // tile,),
            in_specs=[full] * (2 * LINE)
            + [
                pl.BlockSpec((w.shape[0], tile), lambda n, s: (0, s[1] * (width // tile) + n)),
                pl.BlockSpec((w.shape[0], tile), lambda n, s: (0, n)),
            ],
            out_specs=pl.BlockSpec((rows, tile), lambda n, s: (0, n)),
            scratch_shapes=[pltpu.VMEM((rows, LINE * GW), BF), pltpu.VMEM((rows, LINE * GW), BF)],
        ),
        compiler_params=pltpu.CompilerParams(vmem_limit_bytes=32 * 2**20),
        cost_estimate=pl.CostEstimate(
            flops=4 * rows * w.shape[0] * width, bytes_accessed=4 * w.shape[0] * width, transcendentals=0
        ),
        name="project",
    )(place, *mine, *theirs, w, w_theirs)


def shards(
    video_query, video_value, audio_key, audio_value, video_proj, audio_proj, pair_first, pair_count
):
    nblocks = lax.axis_size("seq")
    me = lax.axis_index("seq").astype(jnp.int32)
    core = lax.axis_index("head").astype(jnp.int32)
    me_arr = me[None]
    place = jnp.stack([lax.rem(me, LINE), core])

    def along_line(x, d):
        return lax.ppermute(
            x, "seq", [(s, s // LINE * LINE + (s + d) % LINE) for s in range(nblocks)]
        )

    def across_lines(x, d):
        return lax.ppermute(x, "seq", [(s, (s + d * LINE) % nblocks) for s in range(nblocks)])

    def swap(x):
        return lax.ppermute(x, "head", [(0, 1), (1, 0)])

    kv_out = pack(me_arr, audio_key, audio_value)
    kv = [along_line(kv_out[d - 1], d) for d in (1, 2, 3)]
    qv_out = pack(me_arr, video_query, video_value)
    qv = [along_line(qv_out[d - 1], d) for d in (1, 2, 3)]
    low, high = line_blocks(me_arr, audio_key, audio_value, *kv)
    before, after = across_lines(high, 1), across_lines(low, -1)

    width = video_proj.shape[1] // 2
    v_other = swap(lax.dynamic_slice_in_dim(video_proj, (1 - core) * width, width, 1))
    a_other = swap(lax.dynamic_slice_in_dim(audio_proj, (1 - core) * width, width, 1))

    info = (me_arr, pair_first, pair_count)
    kvs = (before, low, high, after)
    o0, o1, o3, u, c = attend(
        (0, 1, 3), info, kvs, (video_query, video_value), (qv[0], qv[2]), (), False
    )
    o2, to_prev, to_next, u, c = attend((2,), info, kvs, (), (qv[1],), (u, c), True)
    from_next, from_prev = across_lines(to_prev, -1), across_lines(to_next, 1)

    v1, v3, v2 = along_line(o1, -1), along_line(o3, -3), along_line(o2, -2)
    v_mine = (o0, v1, v2, v3)
    near = swap(jnp.stack([o0, v1, v3]))
    far = swap(v2)
    v_theirs = (near[0], near[1], far, near[2])
    video_out = project(place, v_mine, v_theirs, video_proj, v_other)

    m0, m1, m2, m3 = merge(me_arr, u, c, from_prev, from_next)
    a_mine = (m0, along_line(m3, 3), along_line(m2, 2), along_line(m1, 1))
    a_all = swap(jnp.stack(a_mine))
    audio_out = project(place, a_mine, tuple(a_all[d] for d in range(LINE)), audio_proj, a_other)
    return video_out, audio_out


def solution(mesh):
    in_specs = (
        P("seq", "head"),
        P("seq", "head"),
        P("seq", "head"),
        P("seq", "head"),
        P("head", None),
        P("head", None),
        P(),
        P(),
    )
    out_specs = (P("seq", "head"), P("seq", "head"))
    return jax.shard_map(shards, mesh=mesh, in_specs=in_specs, out_specs=out_specs, check_vma=False)
```

time: 536 us -> 323 us (0.60); the launches traced: 527 us -> 321 us
  waiting for transfers between devices: 368 us -> 60.4 us
  Pallas kernels: 0 us -> 195 us
  matrix products: 33.9 us -> 0 us
  between operations: 28.4 us -> 0.87 us
  other arithmetic: 25.5 us -> 2.25 us
  local copies, waits for them, and re-layouts: 35.3 us -> 17.1 us
  starting transfers between devices: 34.2 us -> 45.4 us
    ppermute x8 -> x21, waiting for transfers between devices: 298 us -> 60.4 us  [the longest x12 41.2 us: along_line(): lax.ppermute(x, 'seq', [(s, s // LINE * LINE + (s + d) % LINE) for s in r...]
    pallas_call x0 -> x8, Pallas kernels: none -> 195 us  [the longest x2 110 us: pack(): pl.pallas_call(pack_kernel, out_shape=(piece,) * 3, in_specs=[SMEM, ANY,...]
    reduce_scatter x2 -> x0, waiting for transfers between devices: 70 us -> none  [the longest x1 70 us: shards(): lax.psum_scatter(video_term, 'head', scatter_dimension=1, tiled=True)]
    dot_general x6 -> x0, matrix products: 33.9 us -> none  [the longest x1 10.7 us: shards(): jnp.dot(video_attn, video_proj, preferred_element_type=jnp.float32)]
    another operation x27 -> x0, local copies, waits for them, and re-layouts: 18.9 us -> none
    convert_element_type x4 -> x0, other arithmetic: 17.4 us -> none  [the longest x2 11.8 us: finish(): result = (out / total.T[:, :, None]).astype(jnp.bfloat16)]
    ppermute x8 -> x21, starting transfers between devices: 34.1 us -> 45.4 us  [the longest x12 18.7 us: along_line(): lax.ppermute(x, 'seq', [(s, s // LINE * LINE + (s + d) % LINE) for s in r...]
    cond x14 -> x0, local copies, waits for them, and re-layouts: 9.8 us -> none  [the longest x1 3.53 us: shards(): video_acc = combine(video_acc, lax.cond(valid, video_side, no_video, 0))]
  transfers between devices with their start and end apart: 10 -> 21, of which waited for: 6 -> 5; matrix products, arithmetic and copies ran while one was open for 13% -> 4% of each run, Pallas kernels for 0% -> 46%
where the time goes in v1:
time: 323 us; the launch traced here: 321 us
  Pallas kernels  195 us (60%)
  waiting for transfers between devices  60.4 us (19%)
  starting transfers between devices  45.4 us (14%)
  local copies, waits for them, and re-layouts  17.1 us (5%)
    pallas_call x2, Pallas kernels, pack(): pl.pallas_call(pack_kernel, out_shape=(piece,) * 3, in_specs=[SMEM, ANY,...  110 us
    pallas_call x1, Pallas kernels, line_blocks(): pl.pallas_call(line_kernel, out_shape=(half, half), in_specs=[SMEM] + [AN...  48.8 us
    ppermute x12, waiting for transfers between devices, along_line(): lax.ppermute(x, 'seq', [(s, s // LINE * LINE + (s + d) % LINE) for s in r...  41.2 us
    ppermute x4, waiting for transfers between devices, across_lines(): lax.ppermute(x, 'seq', [(s, (s + d * LINE) % nblocks) for s in range(nblo...  19.2 us
    ppermute x12, starting transfers between devices, along_line(): lax.ppermute(x, 'seq', [(s, s // LINE * LINE + (s + d) % LINE) for s in r...  18.7 us
    pallas_call x2, Pallas kernels, attend(): pl.pallas_call(functools.partial(attend_kernel, steps, bool(own), bool(su...  18.2 us
    pallas_call x2, Pallas kernels, project(): pl.pallas_call(project_kernel, out_shape=jax.ShapeDtypeStruct((rows, widt...  17.5 us
    ppermute x5, starting transfers between devices, swap(): return lax.ppermute(x, 'head', [(0, 1), (1, 0)])  14.8 us
  transfers between devices with their start and end apart: 21, of which 5 were waited for; matrix products, arithmetic and copies ran while one was open for 4% of the time, Pallas kernels for 46%

profile of v1, /device:TPU:1, one launch (start us, length us, event | category | flops | bytes accessed | tf_op | source)
XLA Modules:
  0.0 320.5 jit_solution(7906298874148063945)
XLA Ops:
  0.6 36.9 %pack.2 = (bf16[2,256,384]{2,1,0:T(8,128)(2,1)}, bf16[2,256,384]{2,1,0:T(8,128)(2,1)}, bf16[2,256,384]{2,1,0:T(8,128)(2,1)}) custom-call(s32[1]{0:T(128)} %bitcast.2.me.refs_0_, bf16[256,1536]{1,0:T(8,128)(2,1)} %k.1, bf16[256,1536]{1,0:T(8,128)(2,1)} %v.1), custom_call_target="tpu_custom_call" | custom-call | tf_op jit(solution)/shard_map/pack/pallas_call | solution.py:50
  37.6 2.2 collective-permute-start
  39.8 5.2 %constant_dynamic-slice_fusion = bf16[1536,1536]{1,0:T(8,128)(2,1)} fusion(bf16[1536,3072]{1,0:T(8,128)(2,1)} %refs_8_.5, s32[]{:T(128)S(6)} %select_n.4), kind=kLoop, calls=%fused_computation.10 | loop fusion | bytes 9437188 | tf_op jit(solution)/shard_map/dynamic_slice | solution.py:383
  46.6 2.6 constant_dynamic-slice_fusion.1
  50.1 2.6 collective-permute-start.1
  52.7 72.6 %pack.3 = (bf16[2,512,384]{2,1,0:T(8,128)(2,1)}, bf16[2,512,384]{2,1,0:T(8,128)(2,1)}, bf16[2,512,384]{2,1,0:T(8,128)(2,1)}) custom-call(s32[1]{0:T(128)} %bitcast.2.me.refs_0_, bf16[512,1536]{1,0:T(8,128)(2,1)} %refs_7_.1, bf16[512,1536]{1,0:T(8,128)(2,1)} %refs_8_.3), custom_call_target="tpu_custom_call" | custom-call | tf_op jit(solution)/shard_map/pack/pallas_call | solution.py:50
  125.5 2.6 collective-permute-start.6
  128.2 25.0 %collective-permute-done.2.kv3 = bf16[2,256,384]{2,1,0:T(8,128)(2,1)} collective-permute-done((bf16[2,256,384]{2,1,0:T(8,128)(2,1)}, bf16[2,256,384]{2,1,0:T(8,128)(2,1)}, u32[]{:S(2)}, u32[]{:S(2)}) %collective-permute-start.2) | collective-permute-done | bytes 393248 | tf_op jit(solution)/shard_map/ppermute | solution.py:364
  153.2 48.8 %line_blocks.1 = (bf16[2,2,256,384]{3,2,1,0:T(8,128)(2,1)}, bf16[2,2,256,384]{3,2,1,0:T(8,128)(2,1)}) custom-call(s32[1]{0:T(128)} %bitcast.2.me.refs_0_, bf16[256,1536]{1,0:T(8,128)(2,1)} %k.1, bf16[256,1536]{1,0:T(8,128)(2,1)} %v.1, bf16[2,256,384]{2,1,0:T(8,128)(2,1)} %copy-done.10, bf16[2,256,384]{2,1,0:T(8,128)(2,1)} %collective-permute-done.1.kv2, ...), custom_call_target="tpu_custom_call" | custom-call | tf_op jit(solution)/shard_map/line_blocks/pallas_call | solution.py:89
  202.0 1.7 collective-permute-start.3
  203.7 4.4 %collective-permute-start.4 = (bf16[2,2,256,384]{3,2,1,0:T(8,128)(2,1)}, bf16[2,2,256,384]{3,2,1,0:T(8,128)(2,1)S(1)}, u32[]{:S(2)}, u32[]{:S(2)}) collective-permute-start(bf16[2,2,256,384]{3,2,1,0:T(8,128)(2,1)} %get-tuple-element.28.refs_4_), channel_id=1, source_target_pairs={{0,120},{2,122},{4,124},{6,126},{8,0},{10,2},{12,4},{14,6},{16,8},... | collective-permute-start | bytes 2359304 | tf_op jit(solution)/shard_map/ppermute | solution.py:369
  208.1 2.1 collective-permute-start.8
  210.2 14.5 %collective-permute-done.3.refs_3_ = bf16[2,2,256,384]{3,2,1,0:T(8,128)(2,1)S(1)} collective-permute-done((bf16[2,2,256,384]{3,2,1,0:T(8,128)(2,1)}, bf16[2,2,256,384]{3,2,1,0:T(8,128)(2,1)S(1)}, u32[]{:S(2)}, u32[]{:S(2)}) %collective-permute-start.3) | collective-permute-done | bytes 786464 | tf_op jit(solution)/shard_map/ppermute | solution.py:369
  224.7 1.1 copy-done.4
  225.9 1.1 copy-done.6
  227.0 11.3 %attend.1 = (bf16[512,384]{1,0:T(8,128)(2,1)S(1)}, bf16[512,384]{1,0:T(8,128)(2,1)S(1)}, bf16[512,384]{1,0:T(8,128)(2,1)S(1)}, f32[3,8,144,256]{3,2,1,0:T(8,128)S(1)}, f32[3,8,8,256]{3,2,1,0:T(8,128)S(1)}) custom-call(s32[1]{0:T(128)} %bitcast.2.me.refs_0_, s32[64]{0:T(128)S(1)} %copy-done.8, s32[64]{0:T(128)S(1)} %copy-done.9, ...), custom_call_target="tpu_custom_call" | custom-call | flops 3623878656 | bytes 8388608 | tf_op jit(solution)/shard_map/attend/pallas_call | solution.py:254
  238.3 6.9 %attend_last.1 = (bf16[512,384]{1,0:T(8,128)(2,1)}, bf16[2,3,144,256]{3,2,1,0:T(8,128)(2,1)S(1)}, bf16[2,3,144,256]{3,2,1,0:T(8,128)(2,1)S(1)}, f32[3,4,144,256]{3,2,1,0:T(8,128)S(1)}, f32[3,4,8,256]{3,2,1,0:T(8,128)S(1)}) custom-call(s32[1]{0:T(128)} %bitcast.2.me.refs_0_, s32[64]{0:T(128)S(1)} %copy-done.8, s32[64]{0:T(128)S(1)} %copy-done.9, ...), custom_call_target="tpu_custom_call" | custom-call | flops 1207959552 | bytes 8388608 | tf_op jit(solution)/shard_map/attend_last/pallas_call | solution.py:254
  245.5 5.5 %collective-permute-start.15 = (bf16[2,3,144,256]{3,2,1,0:T(8,128)(2,1)S(1)}, bf16[2,3,144,256]{3,2,1,0:T(8,128)(2,1)S(1)}, u32[]{:S(2)}, u32[]{:S(2)}) collective-permute-start(bf16[2,3,144,256]{3,2,1,0:T(8,128)(2,1)S(1)} %get-tuple-element.41), channel_id=1, source_target_pairs={{0,120},{2,122},{4,124},{6,126},{8,0},{10,2},{12,4},{14,6},{16,8},... | collective-permute-start | bytes 1327112 | tf_op jit(solution)/shard_map/ppermute | solution.py:369
  251.0 3.4 %collective-permute-start.7 = (bf16[512,384]{1,0:T(8,128)(2,1)S(1)}, bf16[512,384]{1,0:T(8,128)(2,1)S(1)}, u32[]{:S(2)}, u32[]{:S(2)}) collective-permute-start(bf16[512,384]{1,0:T(8,128)(2,1)S(1)} %get-tuple-element.32), channel_id=1, source_target_pairs={{0,6},{2,0},{4,2},{6,4},{8,14},{10,8},{12,10},{14,12},{16,22},{18,... | collective-permute-start | bytes 1179656 | tf_op jit(solution)/shard_map/ppermute | solution.py:364
  254.3 4.7 %collective-permute-done.14.prev = bf16[2,3,144,256]{3,2,1,0:T(8,128)(2,1)S(1)} collective-permute-done((bf16[2,3,144,256]{3,2,1,0:T(8,128)(2,1)S(1)}, bf16[2,3,144,256]{3,2,1,0:T(8,128)(2,1)S(1)}, u32[]{:S(2)}, u32[]{:S(2)}) %collective-permute-start.14) | collective-permute-done | bytes 442400 | tf_op jit(solution)/shard_map/ppermute | solution.py:369
  260.5 2.6 collective-permute-start.16
  263.1 1.3 collective-permute-start.17
  264.4 4.5 %collective-permute-done.10.refs_3_ = bf16[512,384]{1,0:T(8,128)(2,1)S(1)} collective-permute-done((bf16[512,384]{1,0:T(8,128)(2,1)S(1)}, bf16[512,384]{1,0:T(8,128)(2,1)S(1)}, u32[]{:S(2)}, u32[]{:S(2)}) %collective-permute-start.10) | collective-permute-done | bytes 393248 | tf_op jit(solution)/shard_map/ppermute | solution.py:364
  268.9 1.2 pad_maximum_fusion
  270.1 6.4 %collective-permute-start.11 = (bf16[3,512,384]{2,1,0:T(8,128)(2,1)}, bf16[3,512,384]{2,1,0:T(8,128)(2,1)}, u32[]{:S(2)}, u32[]{:S(2)}) collective-permute-start(bf16[3,512,384]{2,1,0:T(8,128)(2,1)} %pad_maximum_fusion), channel_id=1, source_target_pairs={{0,1},{1,0},{2,3},{3,2},{4,5},{5,4},{6,7},{7,6},{8,9},{9,8},{10,11... | collective-permute-start | bytes 3538952 | tf_op jit(solution)/shard_map/ppermute | solution.py:372
  277.5 5.7 %collective-permute-start.19 = (bf16[4,256,384]{2,1,0:T(8,128)(2,1)}, bf16[4,256,384]{2,1,0:T(8,128)(2,1)}, u32[]{:S(2)}, u32[]{:S(2)}) collective-permute-start(bf16[4,256,384]{2,1,0:T(8,128)(2,1)} %pad_maximum_fusion.1), channel_id=1, source_target_pairs={{0,1},{1,0},{2,3},{3,2},{4,5},{5,4},{6,7},{7,6},{8,9},{9,8},{10,11... | collective-permute-start | bytes 2359304 | tf_op jit(solution)/shard_map/ppermute | solution.py:372
  284.2 11.6 %collective-permute-done.9.refs_2_ = bf16[512,384]{1,0:T(8,128)(2,1)} collective-permute-done((bf16[512,384]{1,0:T(8,128)(2,1)}, bf16[512,384]{1,0:T(8,128)(2,1)}, u32[]{:S(2)}, u32[]{:S(2)}) %collective-permute-start.9) | collective-permute-done | bytes 393248 | tf_op jit(solution)/shard_map/ppermute | solution.py:364
  296.6 1.3 slice_bitcast_fusion.3
  297.9 1.4 slice_bitcast_fusion
  299.3 3.7 %copy-done = bf16[1536,3072]{1,0:T(8,128)(2,1)S(1)} copy-done((bf16[1536,3072]{1,0:T(8,128)(2,1)S(1)}, bf16[1536,3072]{1,0:T(8,128)(2,1)}, u32[]{:S(2)}) %copy-start) | copy-done | bytes 9437208
  302.9 8.0 %project.3 = bf16[256,1536]{1,0:T(8,128)(2,1)} custom-call(s32[2]{0:T(128)S(1)} %pad_add_fusion.place, bf16[256,384]{1,0:T(8,128)(2,1)S(1)} %get-tuple-element.42.refs_0_, bf16[256,384]{1,0:T(8,128)(2,1)S(1)} %collective-permute-done.16.refs_1_, bf16[256,384]{1,0:T(8,128)(2,1)S(1)} %collective-permute-done.17.refs_2_, ...), custom_call_target="tpu_custom_call" | custom-call | flops 2415919104 | bytes 9437184 | tf_op jit(solution)/shard_map/project/pallas_call | solution.py:332
  311.0 9.5 %project.2 = bf16[512,1536]{1,0:T(8,128)(2,1)} custom-call(s32[2]{0:T(128)S(1)} %pad_add_fusion.place, bf16[512,384]{1,0:T(8,128)(2,1)S(1)} %get-tuple-element.31.refs_0_, bf16[512,384]{1,0:T(8,128)(2,1)S(1)} %collective-permute-done.7.refs_1_, bf16[512,384]{1,0:T(8,128)(2,1)} %collective-permute-done.9.refs_2_, ...), custom_call_target="tpu_custom_call" | custom-call | flops 4831838208 | bytes 9437184 | tf_op jit(solution)/shard_map/project/pallas_call | solution.py:332
  (54 shorter events, 7.3 us)
Async XLA Ops:
  37.6 87.9 %collective-permute-start = (bf16[2,256,384]{2,1,0:T(8,128)(2,1)}, bf16[2,256,384]{2,1,0:T(8,128)(2,1)S(1)}, u32[]{:S(2)}, u32[]{:S(2)}) collective-permute-start(bf16[2,256,384]{2,1,0:T(8,128)(2,1)} %get-tuple-element.24), channel_id=1, source_target_pairs={{0,2},{2,4},{4,6},{6,0},{8,10},{10,12},{12,14},{14,8},{16,18},{18,... | collective-permute-start | bytes 1179656 | tf_op jit(solution)/shard_map/ppermute | solution.py:364
  39.8 6.8 %copy-start.1 = (bf16[1536,3072]{1,0:T(8,128)(2,1)S(1)}, bf16[1536,3072]{1,0:T(8,128)(2,1)}, u32[]{:S(2)}) copy-start(bf16[1536,3072]{1,0:T(8,128)(2,1)} %refs_8_.4) | copy-start | bytes 28311556
  45.0 254.3 %collective-permute-start.20 = (bf16[1536,1536]{1,0:T(8,128)(2,1)}, bf16[1536,1536]{1,0:T(8,128)(2,1)}, u32[]{:S(2)}, u32[]{:S(2)}) collective-permute-start(bf16[1536,1536]{1,0:T(8,128)(2,1)} %constant_dynamic-slice_fusion), channel_id=1, source_target_pairs={{0,1},{1,0},{2,3},{3,2},{4,5},{5,4},{6,7},{7,6},{8,9},{9,8},{10,11... | collective-permute-start | bytes 14155784 | tf_op jit(solution)/shard_map/ppermute | solution.py:372
  49.1 261.8 %collective-permute-start.13 = (bf16[1536,1536]{1,0:T(8,128)(2,1)}, bf16[1536,1536]{1,0:T(8,128)(2,1)}, u32[]{:S(2)}, u32[]{:S(2)}) collective-permute-start(bf16[1536,1536]{1,0:T(8,128)(2,1)} %constant_dynamic-slice_fusion.1), channel_id=1, source_target_pairs={{0,1},{1,0},{2,3},{3,2},{4,5},{5,4},{6,7},{7,6},{8,9},{9,8},{10,11... | collective-permute-start | bytes 14155784 | tf_op jit(solution)/shard_map/ppermute | solution.py:372
  50.1 78.1 %collective-permute-start.1 = (bf16[2,256,384]{2,1,0:T(8,128)(2,1)}, bf16[2,256,384]{2,1,0:T(8,128)(2,1)}, u32[]{:S(2)}, u32[]{:S(2)}) collective-permute-start(bf16[2,256,384]{2,1,0:T(8,128)(2,1)} %get-tuple-element.25), channel_id=1, source_target_pairs={{0,4},{2,6},{4,0},{6,2},{8,12},{10,14},{12,8},{14,10},{16,20},{18,... | collective-permute-start | bytes 1179656 | tf_op jit(solution)/shard_map/ppermute | solution.py:364
  52.7 172.0 %copy-start.3 = (bf16[512,1536]{1,0:T(8,128)(2,1)S(1)}, bf16[512,1536]{1,0:T(8,128)(2,1)}, u32[]{:S(2)}) copy-start(bf16[512,1536]{1,0:T(8,128)(2,1)} %refs_8_.3) | copy-start | bytes 4718596
  125.4 99.3 %copy-start.2 = (bf16[512,1536]{1,0:T(8,128)(2,1)S(1)}, bf16[512,1536]{1,0:T(8,128)(2,1)}, u32[]{:S(2)}) copy-start(bf16[512,1536]{1,0:T(8,128)(2,1)} %refs_7_.1) | copy-start | bytes 4718596
  125.4 99.3 %copy-start.8 = (s32[64]{0:T(128)S(1)}, s32[64]{0:T(128)}, u32[]{:S(2)}) copy-start(s32[64]{0:T(128)} %refs_1_.3) | copy-start | bytes 772
  125.4 99.3 %copy-start.9 = (s32[64]{0:T(128)S(1)}, s32[64]{0:T(128)}, u32[]{:S(2)}) copy-start(s32[64]{0:T(128)} %refs_2_.3) | copy-start | bytes 772
  125.4 78.3 %collective-permute-start.5 = (bf16[2,512,384]{2,1,0:T(8,128)(2,1)}, bf16[2,512,384]{2,1,0:T(8,128)(2,1)}, u32[]{:S(2)}, u32[]{:S(2)}) collective-permute-start(bf16[2,512,384]{2,1,0:T(8,128)(2,1)} %get-tuple-element.29), channel_id=1, source_target_pairs={{0,2},{2,4},{4,6},{6,0},{8,10},{10,12},{12,14},{14,8},{16,18},{18,... | collective-permute-start | bytes 2359304 | tf_op jit(solution)/shard_map/ppermute | solution.py:364
  125.5 27.7 %copy-start.10 = (bf16[2,256,384]{2,1,0:T(8,128)(2,1)}, bf16[2,256,384]{2,1,0:T(8,128)(2,1)S(1)}, u32[]{:S(2)}) copy-start(bf16[2,256,384]{2,1,0:T(8,128)(2,1)S(1)} %collective-permute-done.kv1) | copy-start | bytes 1179652
  125.5 82.6 %collective-permute-start.6 = (bf16[2,512,384]{2,1,0:T(8,128)(2,1)}, bf16[2,512,384]{2,1,0:T(8,128)(2,1)}, u32[]{:S(2)}, u32[]{:S(2)}) collective-permute-start(bf16[2,512,384]{2,1,0:T(8,128)(2,1)} %get-tuple-element.30), channel_id=1, source_target_pairs={{0,6},{2,0},{4,2},{6,4},{8,14},{10,8},{12,10},{14,12},{16,22},{18,... | collective-permute-start | bytes 2359304 | tf_op jit(solution)/shard_map/ppermute | solution.py:364
  128.2 25.1 %collective-permute-start.2 = (bf16[2,256,384]{2,1,0:T(8,128)(2,1)}, bf16[2,256,384]{2,1,0:T(8,128)(2,1)}, u32[]{:S(2)}, u32[]{:S(2)}) collective-permute-start(bf16[2,256,384]{2,1,0:T(8,128)(2,1)} %get-tuple-element.26), channel_id=1, source_target_pairs={{0,6},{2,0},{4,2},{6,4},{8,14},{10,8},{12,10},{14,12},{16,22},{18,... | collective-permute-start | bytes 1179656 | tf_op jit(solution)/shard_map/ppermute | solution.py:364
  202.0 22.7 %collective-permute-start.3 = (bf16[2,2,256,384]{3,2,1,0:T(8,128)(2,1)}, bf16[2,2,256,384]{3,2,1,0:T(8,128)(2,1)S(1)}, u32[]{:S(2)}, u32[]{:S(2)}) collective-permute-start(bf16[2,2,256,384]{3,2,1,0:T(8,128)(2,1)} %get-tuple-element.27.refs_5_), channel_id=1, source_target_pairs={{0,8},{2,10},{4,12},{6,14},{8,16},{10,18},{12,20},{14,22},{16,24},... | collective-permute-start | bytes 2359304 | tf_op jit(solution)/shard_map/ppermute | solution.py:369
  203.7 21.0 %collective-permute-start.4 = (bf16[2,2,256,384]{3,2,1,0:T(8,128)(2,1)}, bf16[2,2,256,384]{3,2,1,0:T(8,128)(2,1)S(1)}, u32[]{:S(2)}, u32[]{:S(2)}) collective-permute-start(bf16[2,2,256,384]{3,2,1,0:T(8,128)(2,1)} %get-tuple-element.28.refs_4_), channel_id=1, source_target_pairs={{0,120},{2,122},{4,124},{6,126},{8,0},{10,2},{12,4},{14,6},{16,8},... | collective-permute-start | bytes 2359304 | tf_op jit(solution)/shard_map/ppermute | solution.py:369
  208.1 30.1 %collective-permute-start.8 = (bf16[2,512,384]{2,1,0:T(8,128)(2,1)}, bf16[2,512,384]{2,1,0:T(8,128)(2,1)S(1)}, u32[]{:S(2)}, u32[]{:S(2)}) collective-permute-start(bf16[2,512,384]{2,1,0:T(8,128)(2,1)} %get-tuple-element.33), channel_id=1, source_target_pairs={{0,4},{2,6},{4,0},{6,2},{8,12},{10,14},{12,8},{14,10},{16,20},{18,... | collective-permute-start | bytes 2359304 | tf_op jit(solution)/shard_map/ppermute | solution.py:364
  227.0 11.3 %copy-start.5 = (bf16[2,2,256,384]{3,2,1,0:T(8,128)(2,1)S(1)}, bf16[2,2,256,384]{3,2,1,0:T(8,128)(2,1)}, u32[]{:S(2)}) copy-start(bf16[2,2,256,384]{3,2,1,0:T(8,128)(2,1)} %get-tuple-element.28.refs_4_) | copy-start | bytes 2359300
  227.0 11.3 %copy-start.7 = (bf16[2,2,256,384]{3,2,1,0:T(8,128)(2,1)S(1)}, bf16[2,2,256,384]{3,2,1,0:T(8,128)(2,1)}, u32[]{:S(2)}) copy-start(bf16[2,2,256,384]{3,2,1,0:T(8,128)(2,1)} %get-tuple-element.27.refs_5_) | copy-start | bytes 2359300
  245.2 13.9 %collective-permute-start.14 = (bf16[2,3,144,256]{3,2,1,0:T(8,128)(2,1)S(1)}, bf16[2,3,144,256]{3,2,1,0:T(8,128)(2,1)S(1)}, u32[]{:S(2)}, u32[]{:S(2)}) collective-permute-start(bf16[2,3,144,256]{3,2,1,0:T(8,128)(2,1)S(1)} %get-tuple-element.40), channel_id=1, source_target_pairs={{0,8},{2,10},{4,12},{6,14},{8,16},{10,18},{12,20},{14,22},{16,24},... | collective-permute-start | bytes 1327112 | tf_op jit(solution)/shard_map/ppermute | solution.py:369
  245.5 14.5 %collective-permute-start.15 = (bf16[2,3,144,256]{3,2,1,0:T(8,128)(2,1)S(1)}, bf16[2,3,144,256]{3,2,1,0:T(8,128)(2,1)S(1)}, u32[]{:S(2)}, u32[]{:S(2)}) collective-permute-start(bf16[2,3,144,256]{3,2,1,0:T(8,128)(2,1)S(1)} %get-tuple-element.41), channel_id=1, source_target_pairs={{0,120},{2,122},{4,124},{6,126},{8,0},{10,2},{12,4},{14,6},{16,8},... | collective-permute-start | bytes 1327112 | tf_op jit(solution)/shard_map/ppermute | solution.py:369
  251.0 12.1 %collective-permute-start.7 = (bf16[512,384]{1,0:T(8,128)(2,1)S(1)}, bf16[512,384]{1,0:T(8,128)(2,1)S(1)}, u32[]{:S(2)}, u32[]{:S(2)}) collective-permute-start(bf16[512,384]{1,0:T(8,128)(2,1)S(1)} %get-tuple-element.32), channel_id=1, source_target_pairs={{0,6},{2,0},{4,2},{6,4},{8,14},{10,8},{12,10},{14,12},{16,22},{18,... | collective-permute-start | bytes 1179656 | tf_op jit(solution)/shard_map/ppermute | solution.py:364
  259.1 9.8 %collective-permute-start.10 = (bf16[512,384]{1,0:T(8,128)(2,1)S(1)}, bf16[512,384]{1,0:T(8,128)(2,1)S(1)}, u32[]{:S(2)}, u32[]{:S(2)}) collective-permute-start(bf16[512,384]{1,0:T(8,128)(2,1)S(1)} %get-tuple-element.37), channel_id=1, source_target_pairs={{0,2},{2,4},{4,6},{6,0},{8,10},{10,12},{12,14},{14,8},{16,18},{18,... | collective-permute-start | bytes 1179656 | tf_op jit(solution)/shard_map/ppermute | solution.py:364
  260.5 9.5 %collective-permute-start.16 = (bf16[256,384]{1,0:T(8,128)(2,1)S(1)}, bf16[256,384]{1,0:T(8,128)(2,1)S(1)}, u32[]{:S(2)}, u32[]{:S(2)}) collective-permute-start(bf16[256,384]{1,0:T(8,128)(2,1)S(1)} %get-tuple-element.43), channel_id=1, source_target_pairs={{0,6},{2,0},{4,2},{6,4},{8,14},{10,8},{12,10},{14,12},{16,22},{18,... | collective-permute-start | bytes 589832 | tf_op jit(solution)/shard_map/ppermute | solution.py:364
  263.1 13.4 %collective-permute-start.17 = (bf16[256,384]{1,0:T(8,128)(2,1)S(1)}, bf16[256,384]{1,0:T(8,128)(2,1)S(1)}, u32[]{:S(2)}, u32[]{:S(2)}) collective-permute-start(bf16[256,384]{1,0:T(8,128)(2,1)S(1)} %get-tuple-element.44), channel_id=1, source_target_pairs={{0,4},{2,6},{4,0},{6,2},{8,12},{10,14},{12,8},{14,10},{16,20},{18,... | collective-permute-start | bytes 589832 | tf_op jit(solution)/shard_map/ppermute | solution.py:364
  268.9 7.6 %collective-permute-start.18 = (bf16[256,384]{1,0:T(8,128)(2,1)S(1)}, bf16[256,384]{1,0:T(8,128)(2,1)S(1)}, u32[]{:S(2)}, u32[]{:S(2)}) collective-permute-start(bf16[256,384]{1,0:T(8,128)(2,1)S(1)} %get-tuple-element.45), channel_id=1, source_target_pairs={{0,2},{2,4},{4,6},{6,0},{8,10},{10,12},{12,14},{14,8},{16,18},{18,... | collective-permute-start | bytes 589832 | tf_op jit(solution)/shard_map/ppermute | solution.py:364
  270.1 27.8 %collective-permute-start.11 = (bf16[3,512,384]{2,1,0:T(8,128)(2,1)}, bf16[3,512,384]{2,1,0:T(8,128)(2,1)}, u32[]{:S(2)}, u32[]{:S(2)}) collective-permute-start(bf16[3,512,384]{2,1,0:T(8,128)(2,1)} %pad_maximum_fusion), channel_id=1, source_target_pairs={{0,1},{1,0},{2,3},{3,2},{4,5},{5,4},{6,7},{7,6},{8,9},{9,8},{10,11... | collective-permute-start | bytes 3538952 | tf_op jit(solution)/shard_map/ppermute | solution.py:372
  276.5 34.5 %slice-start = ((s8[9437184]{0:T(1024)(128)(4,1)}), s8[1048576]{0:T(1024)(128)(4,1)S(1)}, s32[]{:S(2)}) async-start(s8[9437184]{0:T(1024)(128)(4,1)} %bitcast.24), calls=%async_computation | async-start | bytes 2097152
  277.5 19.0 %collective-permute-start.19 = (bf16[4,256,384]{2,1,0:T(8,128)(2,1)}, bf16[4,256,384]{2,1,0:T(8,128)(2,1)}, u32[]{:S(2)}, u32[]{:S(2)}) collective-permute-start(bf16[4,256,384]{2,1,0:T(8,128)(2,1)} %pad_maximum_fusion.1), channel_id=1, source_target_pairs={{0,1},{1,0},{2,3},{3,2},{4,5},{5,4},{6,7},{7,6},{8,9},{9,8},{10,11... | collective-permute-start | bytes 2359304 | tf_op jit(solution)/shard_map/ppermute | solution.py:372
  283.2 12.6 %collective-permute-start.9 = (bf16[512,384]{1,0:T(8,128)(2,1)}, bf16[512,384]{1,0:T(8,128)(2,1)}, u32[]{:S(2)}, u32[]{:S(2)}) collective-permute-start(bf16[512,384]{1,0:T(8,128)(2,1)} %get-tuple-element.36), channel_id=1, source_target_pairs={{0,4},{2,6},{4,0},{6,2},{8,12},{10,14},{12,8},{14,10},{16,20},{18,... | collective-permute-start | bytes 1179656 | tf_op jit(solution)/shard_map/ppermute | solution.py:364
  295.8 15.2 %collective-permute-start.12 = (bf16[512,384]{1,0:T(8,128)(2,1)}, bf16[512,384]{1,0:T(8,128)(2,1)S(1)}, u32[]{:S(2)}, u32[]{:S(2)}) collective-permute-start(bf16[512,384]{1,0:T(8,128)(2,1)} %collective-permute-done.9.refs_2_), channel_id=1, source_target_pairs={{0,1},{1,0},{2,3},{3,2},{4,5},{5,4},{6,7},{7,6},{8,9},{9,8},{10,11... | collective-permute-start | bytes 1179656 | tf_op jit(solution)/shard_map/ppermute | solution.py:372
  302.9 8.0 %slice-start.1 = ((s8[9437184]{0:T(1024)(128)(4,1)}), s8[4194304]{0:T(1024)(128)(4,1)S(1)}, s32[]{:S(2)}) async-start(s8[9437184]{0:T(1024)(128)(4,1)} %bitcast.24), calls=%async_computation.1 | async-start | bytes 8388608
  302.9 8.1 %slice-start.2 = ((s8[9437184]{0:T(1024)(128)(4,1)}), s8[4194304]{0:T(1024)(128)(4,1)S(1)}, s32[]{:S(2)}) async-start(s8[9437184]{0:T(1024)(128)(4,1)} %bitcast.24), calls=%async_computation.2 | async-start | bytes 8388608
  (3 other events, 6.0 us)

commit v2 on v1

v2 whole, which is shorter than its diff:
```python
import functools
import math

import jax
import jax.numpy as jnp
from jax import lax
from jax.experimental import pallas as pl
from jax.experimental.pallas import tpu as pltpu
from jax.sharding import PartitionSpec as P

HD = 128
LINE = 4
GH = 3
GW = GH * HD
VID = 512
AUD = 256
NEG = -1e30
SCALE = math.log2(math.e) / math.sqrt(HD)
EXTRA = 16
BF = jnp.bfloat16
F32 = jnp.float32
MIB = 2**20


def cost(us):
    return pl.CostEstimate(flops=int(us * 1e9), bytes_accessed=1000, transcendentals=0)


TINY = cost(0.001)
ANY = pl.BlockSpec(memory_space=pl.ANY)
SMEM = pl.BlockSpec(memory_space=pltpu.SMEM)
VMEM = pl.BlockSpec(memory_space=pltpu.VMEM)


def group_cols(g):
    return pl.ds(pl.multiple_of(g * GW, HD), GW)


def through(pieces, held, sem):
    ins = [pltpu.make_async_copy(src, held.at[at], sem.at[0, i]) for i, (src, at, _) in enumerate(pieces)]
    outs = [pltpu.make_async_copy(held.at[at], dst, sem.at[1, i]) for i, (_, at, dst) in enumerate(pieces)]
    for copy in ins:
        copy.start()
    for copy, out in zip(ins, outs):
        copy.wait()
        out.start()
    for copy in outs:
        copy.wait()


def pack_kernel(steps, me, a, b, *refs):
    outs, held, sem = refs[-len(steps) - 2 : -2], refs[-2], refs[-1]
    y = lax.rem(me[0], LINE)
    pieces = []
    for d, out in zip(steps, outs):
        cols = group_cols(lax.rem(y + d, LINE))
        pieces.append((a.at[:, cols], len(pieces), out.at[0]))
        pieces.append((b.at[:, cols], len(pieces), out.at[1]))
    through(pieces, held, sem)


def pack(steps, me, a, b, *after, limit=60):
    n = len(steps)
    return pl.pallas_call(
        functools.partial(pack_kernel, steps),
        out_shape=(jax.ShapeDtypeStruct((2, a.shape[0], GW), BF),) * n,
        in_specs=[SMEM] + [ANY] * (2 + len(after)),
        out_specs=(ANY,) * n,
        scratch_shapes=[pltpu.VMEM((2 * n, a.shape[0], GW), BF), pltpu.SemaphoreType.DMA((2, 2 * n))],
        compiler_params=pltpu.CompilerParams(vmem_limit_bytes=limit * MIB),
        cost_estimate=TINY,
        name="pack",
    )(me, a, b, *after)


def load_kernel(place, v, a, after, v_own, v_other, a_own, a_send, held, sem):
    width = v_own.shape[1]
    rows = held.shape[1]
    own = pl.ds(pl.multiple_of(place[1] * width, HD), width)
    other = pl.ds(pl.multiple_of((1 - place[1]) * width, HD), width)
    whole = [
        pltpu.make_async_copy(a.at[:, own], a_own, sem.at[2, 0]),
        pltpu.make_async_copy(v.at[:, other], v_other, sem.at[2, 1]),
        pltpu.make_async_copy(v.at[:, own], v_own, sem.at[2, 2]),
    ]
    through([(a.at[pl.ds(i * rows, rows), other], i, a_send.at[pl.ds(i * rows, rows)]) for i in range(4)], held, sem)
    for copy in whole:
        copy.start()
    for copy in whole:
        copy.wait()


def load_projections(place, v, a, after):
    rows, width = v.shape[0], v.shape[1] // 2
    half = jax.ShapeDtypeStruct((rows, width), BF)
    return pl.pallas_call(
        load_kernel,
        out_shape=(half,) * 4,
        in_specs=[SMEM, ANY, ANY, ANY],
        out_specs=(VMEM, VMEM, VMEM, ANY),
        scratch_shapes=[pltpu.VMEM((4, rows // 4, width), BF), pltpu.SemaphoreType.DMA((3, 4))],
        compiler_params=pltpu.CompilerParams(vmem_limit_bytes=46 * MIB),
        cost_estimate=cost(6),
        name="load_projections",
    )(place, v, a, after)


def line_kernel(me, k, v, kv1, kv2, kv3, low, high, held, sem):
    y = lax.rem(me[0], LINE)
    cols = group_cols(y)
    copies = [
        pltpu.make_async_copy(k.at[:, cols], held.at[y, 0], sem.at[0]),
        pltpu.make_async_copy(v.at[:, cols], held.at[y, 1], sem.at[4]),
    ]
    for d, got in ((1, kv1), (2, kv2), (3, kv3)):
        copies.append(pltpu.make_async_copy(got, held.at[lax.rem(y + LINE - d, LINE)], sem.at[d]))
    for copy in copies:
        copy.start()
    for copy in copies:
        copy.wait()
    copies = [
        pltpu.make_async_copy(held.at[pl.ds(0, 2)], low, sem.at[0]),
        pltpu.make_async_copy(held.at[pl.ds(2, 2)], high, sem.at[1]),
    ]
    for copy in copies:
        copy.start()
    for copy in copies:
        copy.wait()


def line_blocks(me, k, v, kv1, kv2, kv3):
    half = jax.ShapeDtypeStruct((2, 2, AUD, GW), BF)
    return pl.pallas_call(
        line_kernel,
        out_shape=(half, half),
        in_specs=[SMEM] + [ANY] * 5,
        out_specs=(ANY, ANY),
        scratch_shapes=[pltpu.VMEM((LINE, 2, AUD, GW), BF), pltpu.SemaphoreType.DMA((5,))],
        compiler_params=pltpu.CompilerParams(vmem_limit_bytes=16 * MIB),
        cost_estimate=TINY,
        name="line_blocks",
    )(me, k, v, kv1, kv2, kv3)


def attend_kernel(steps, own, carried, last, *refs):
    refs = list(refs)

    def take(n):
        part = refs[:n]
        del refs[:n]
        return part

    me, first, count = take(3)
    kvs = [] if carried else take(4)
    q_own, v_own = take(2) if own else (None, None)
    arrived = take(len(steps) - (1 if own else 0))
    if carried:
        (kbuf,) = take(1)
        take(2)
    outs = take(len(steps))
    ubuf, csum = take(2)
    if not carried:
        (kbuf,) = take(1)
    if last:
        before, after = take(2)
    qbuf, obuf, tbuf, mbuf, cbuf, abuf, vtbuf, sem, qsem = refs

    y = lax.rem(me[0], LINE)
    base = me[0] - y
    copies = []

    def copy(src, dst):
        copies.append(pltpu.make_async_copy(src, dst, sem.at[len(copies)]))

    for i, part in enumerate(kvs):
        copy(part, kbuf.at[pl.ds(2 * i, 2)])
    if own:
        copy(q_own.at[:, group_cols(y)], qbuf.at[0, 0])
        copy(v_own.at[:, group_cols(y)], qbuf.at[0, 1])
    for c in copies:
        c.start()
    for i, part in enumerate(arrived):
        pltpu.make_async_copy(part, qbuf.at[i], qsem.at[i]).start()
    if not carried:
        csum[...] = jnp.full_like(csum, NEG)
    for c in copies:
        c.wait()

    def video(i, carry):
        if not own:
            pltpu.make_async_copy(qbuf.at[i], qbuf.at[i], qsem.at[i]).wait()
        step = jnp.int32(steps[0])
        for n in range(1, len(steps)):
            step = jnp.where(i == n, steps[n], step)
        v = lax.rem(y + LINE - step, LINE)
        lo = first[base + v] - base + 2
        hi = lo + count[base + v]
        mbuf[...] = jnp.full_like(mbuf, NEG)

        def scores(a, carry):
            slot = a - lo
            for h in range(GH):
                cols = slice(h * HD, (h + 1) * HD)
                t = lax.dot_general(
                    qbuf[i, 0, :, cols], kbuf[a, 0, :, cols], (((1,), (1,)), ((), ())), preferred_element_type=F32
                )
                t = t * SCALE
                tbuf[h, slot] = t
                mbuf[h] = jnp.maximum(mbuf[h], jnp.maximum(t[:, :HD], t[:, HD:]))
                cbuf[h, slot] = jnp.broadcast_to(jnp.max(t, axis=0, keepdims=True), (8, AUD))
            return carry

        lax.fori_loop(lo, hi, scores, 0)
        for h in range(GH):
            cols = slice(h * HD, (h + 1) * HD)
            mbuf[h] = jnp.broadcast_to(jnp.max(mbuf[h], axis=1, keepdims=True), (VID, HD))
            abuf[h] = jnp.zeros((VID, 2 * HD), F32)
            vtbuf[h, :HD] = qbuf[i, 1, :, cols].T
            vtbuf[h, HD:] = jnp.ones((EXTRA, VID), BF)

        def weights(a, carry):
            slot = a - lo
            for h in range(GH):
                cols = slice(h * HD, (h + 1) * HD)
                t = tbuf[h, slot]
                r = mbuf[h]
                c = cbuf[h, slot, 0:1]
                by_row = jnp.exp2(t - jnp.concatenate([r, r], axis=1)).astype(BF)
                values = jnp.concatenate([kbuf[a, 1, :, cols], jnp.ones((AUD, HD), BF)], axis=1)
                abuf[h] += jnp.dot(by_row, values, preferred_element_type=F32)
                by_col = jnp.exp2(t - c).astype(BF)
                u = jnp.dot(vtbuf[h], by_col, preferred_element_type=F32)
                old = csum[h, a, 0:1]
                new = jnp.maximum(old, c)
                kept = jnp.where(old > NEG, ubuf[h, a], 0.0)
                ubuf[h, a] = kept * jnp.exp2(old - new) + u * jnp.exp2(c - new)
                csum[h, a] = jnp.broadcast_to(new, (8, AUD))
            return carry

        lax.fori_loop(lo, hi, weights, 0)
        for h in range(GH):
            obuf[i, :, h * HD : (h + 1) * HD] = (abuf[h, :, :HD] / abuf[h, :, HD:]).astype(BF)
        return carry

    lax.fori_loop(0, len(steps), video, 0)

    copies = [pltpu.make_async_copy(obuf.at[i], out, sem.at[i]) for i, out in enumerate(outs)]
    for c in copies:
        c.start()
    if last:
        row = lax.broadcasted_iota(jnp.int32, (EXTRA, AUD), 0)
        for place, out in ((0, before), (6, after)):
            for j in range(2):
                for h in range(GH):
                    top = csum[h, place + j, 0:1]
                    some = top > NEG
                    n = jnp.where(some, ubuf[h, place + j, HD : HD + 1], 1.0)
                    u = jnp.where(some, ubuf[h, place + j, :HD], 0.0)
                    out[j, h, :HD] = (u / n).astype(BF)
                    level = jnp.where(some, top + jnp.log2(n), NEG)
                    hi = level.astype(BF).astype(F32)
                    mid = (level - hi).astype(BF).astype(F32)
                    lo = level - hi - mid
                    parts = jnp.where(row == 0, hi, jnp.where(row == 1, mid, jnp.where(row == 2, lo, 0.0)))
                    out[j, h, HD:] = parts.astype(BF)
    for c in copies:
        c.wait()


def attend(steps, info, kvs, own, arrived, sums, last):
    n = len(steps)
    n_idx = 2 * LINE
    sum_shapes = [
        jax.ShapeDtypeStruct((GH, n_idx, HD + EXTRA, AUD), F32),
        jax.ShapeDtypeStruct((GH, n_idx, 8, AUD), F32),
    ]
    out_shape = [jax.ShapeDtypeStruct((VID, GW), BF)] * n + sum_shapes
    out_specs = [ANY] * n + [VMEM] * 2
    if last:
        out_shape += [jax.ShapeDtypeStruct((2, GH, HD + EXTRA, AUD), BF)] * 2
        out_specs += [VMEM] * 2
    assert bool(own) != bool(sums)
    operands = [*info, *kvs, *own, *arrived, *sums]
    at = len(operands) - len(sums)
    if not sums:
        out_shape.append(jax.ShapeDtypeStruct((n_idx, 2, AUD, GW), BF))
        out_specs.append(VMEM)
    return pl.pallas_call(
        functools.partial(attend_kernel, steps, bool(own), bool(sums), last),
        out_shape=tuple(out_shape),
        in_specs=[SMEM] * 3 + [ANY] * (at - 3) + [VMEM] * len(sums),
        out_specs=tuple(out_specs),
        scratch_shapes=[
            pltpu.VMEM((n, 2, VID, GW), BF),
            pltpu.VMEM((n, VID, GW), BF),
            pltpu.VMEM((GH, 5, VID, AUD), F32),
            pltpu.VMEM((GH, VID, HD), F32),
            pltpu.VMEM((GH, 5, 8, AUD), F32),
            pltpu.VMEM((GH, VID, 2 * HD), F32),
            pltpu.VMEM((GH, HD + EXTRA, VID), BF),
            pltpu.SemaphoreType.DMA((8,)),
            pltpu.SemaphoreType.DMA((2,)),
        ],
        input_output_aliases={at + 1: n, at + 2: n + 1} if sums else {},
        compiler_params=pltpu.CompilerParams(vmem_limit_bytes=24 * MIB),
        cost_estimate=cost(6 * n),
        name="attend_last" if last else "attend",
    )(*operands)


def merge_kernel(me, u, c, prev, nxt, out0, out1, out2, out3):
    y = lax.rem(me[0], LINE)
    for d, out in enumerate((out0, out1, out2, out3)):
        j = lax.rem(y + d, LINE)
        for h in range(GH):
            low = j < 2
            at = lax.rem(j, 2)
            got = jnp.where(low, prev[at, h].astype(F32), nxt[at, h].astype(F32))
            level = got[HD : HD + 1] + got[HD + 1 : HD + 2] + got[HD + 2 : HD + 3]
            n = u[h, j + 2, HD : HD + 1]
            own = c[h, j + 2, 0:1] + jnp.log2(n)
            top = jnp.maximum(own, level)
            own_w = jnp.exp2(own - top)
            got_w = jnp.exp2(level - top)
            total = own_w + got_w
            mixed = u[h, j + 2, :HD] * (own_w / (n * total)) + got[:HD] * (got_w / total)
            out[:, h * HD : (h + 1) * HD] = mixed.T.astype(BF)


def merge(me, u, c, prev, nxt):
    return pl.pallas_call(
        merge_kernel,
        out_shape=(jax.ShapeDtypeStruct((AUD, GW), BF),) * LINE,
        in_specs=[SMEM] + [VMEM] * 4,
        out_specs=(VMEM,) * LINE,
        name="merge",
        cost_estimate=TINY,
        compiler_params=pltpu.CompilerParams(vmem_limit_bytes=24 * MIB),
    )(me, u, c, prev, nxt)


def near_kernel(place, o0, o1, o3, w_own, w_other, own, other, held, sem):
    y = place[0]
    copies = [pltpu.make_async_copy(o, held.at[i], sem.at[i]) for i, o in enumerate((o0, o1, o3))]
    for copy in copies:
        copy.start()
    for copy in copies:
        copy.wait()
    for w, out in ((w_other, other), (w_own, own)):
        for i, d in enumerate((0, 1, 3)):
            rows = group_cols(lax.rem(y + d, LINE))
            part = jnp.dot(held[i], w[rows, :], preferred_element_type=F32)
            out[...] = part if i == 0 else out[...] + part


def project_near(place, near, w_own, w_other):
    rows, width = near[0].shape[0], w_own.shape[1]
    return pl.pallas_call(
        near_kernel,
        out_shape=(jax.ShapeDtypeStruct((rows, width), F32),) * 2,
        in_specs=[SMEM] + [ANY] * 3 + [VMEM] * 2,
        out_specs=(VMEM,) * 2,
        scratch_shapes=[pltpu.VMEM((3, rows, GW), BF), pltpu.SemaphoreType.DMA((3,))],
        compiler_params=pltpu.CompilerParams(vmem_limit_bytes=16 * MIB),
        cost_estimate=cost(4),
        name="project_near",
    )(place, *near, w_own, w_other)


def far_kernel(n_add, place, piece, w, *refs):
    adds = refs[:n_add]
    out, held, sums, done, sem = refs[-5:]
    base, received = adds[0], adds[1:]
    tiles, _, tile = done.shape
    copies = [pltpu.make_async_copy(piece, held, sem.at[0, 0])]
    if received:
        copies.append(pltpu.make_async_copy(received[0], sums, sem.at[0, 1]))
    for copy in copies:
        copy.start()
    for copy in copies:
        copy.wait()
    rows = group_cols(lax.rem(place[0] + 2, LINE))
    outs = []
    for n in range(tiles):
        cols = slice(n * tile, (n + 1) * tile)
        total = base[:, cols] + jnp.dot(held[...], w[rows, cols], preferred_element_type=F32)
        if received:
            total += sums[:, cols].astype(F32)
        done[n] = total.astype(BF)
        outs.append(pltpu.make_async_copy(done.at[n], out.at[:, pl.ds(n * tile, tile)], sem.at[1, n]))
        outs[-1].start()
    for copy in outs:
        copy.wait()


def project_far(place, piece, w, base, received=(), after=()):
    rows, width = piece.shape[0], w.shape[1]
    tile = 384
    return pl.pallas_call(
        functools.partial(far_kernel, 1 + len(received)),
        out_shape=jax.ShapeDtypeStruct((rows, width), BF),
        in_specs=[SMEM, ANY, VMEM, VMEM] + [ANY] * (len(received) + len(after)),
        out_specs=ANY,
        scratch_shapes=[
            pltpu.VMEM((rows, GW), BF),
            pltpu.VMEM((rows, width), BF),
            pltpu.VMEM((width // tile, rows, tile), BF),
            pltpu.SemaphoreType.DMA((2, 8)),
        ],
        compiler_params=pltpu.CompilerParams(vmem_limit_bytes=16 * MIB),
        cost_estimate=cost(1),
        name="project_far",
    )(place, piece, w, base, *received, *after)


def project_kernel(place, *refs):
    mine, theirs = refs[:LINE], refs[LINE : 2 * LINE]
    w_mine, w_theirs, out, left, right, held, sem = refs[2 * LINE :]
    y = place[0]
    tiles, _, tile = held.shape
    ins = []
    for d in range(LINE):
        cols = group_cols(lax.rem(y + d, LINE))
        ins.append(pltpu.make_async_copy(mine[d], left.at[:, cols], sem.at[0, d]))
        ins.append(pltpu.make_async_copy(theirs[d], right.at[:, cols], sem.at[1, d]))
    for copy in ins:
        copy.start()
    for copy in ins:
        copy.wait()
    outs = []
    for n in range(tiles):
        cols = slice(n * tile, (n + 1) * tile)
        total = jnp.dot(left[...], w_mine[:, cols], preferred_element_type=F32)
        total += jnp.dot(right[...], w_theirs[:, cols], preferred_element_type=F32)
        held[n] = total.astype(BF)
        outs.append(pltpu.make_async_copy(held.at[n], out.at[:, pl.ds(n * tile, tile)], sem.at[2, n]))
        outs[-1].start()
    for copy in outs:
        copy.wait()


def project(place, mine, theirs, w, w_theirs):
    rows, width = mine[0].shape[0], w.shape[1]
    tile = 256
    return pl.pallas_call(
        project_kernel,
        out_shape=jax.ShapeDtypeStruct((rows, width), BF),
        in_specs=[SMEM] + [ANY] * (2 * LINE) + [VMEM] * 2,
        out_specs=ANY,
        scratch_shapes=[
            pltpu.VMEM((rows, LINE * GW), BF),
            pltpu.VMEM((rows, LINE * GW), BF),
            pltpu.VMEM((width // tile, rows, tile), BF),
            pltpu.SemaphoreType.DMA((3, 8)),
        ],
        compiler_params=pltpu.CompilerParams(vmem_limit_bytes=16 * MIB),
        cost_estimate=cost(4),
        name="project",
    )(place, *mine, *theirs, w, w_theirs)


def shards(
    video_query, video_value, audio_key, audio_value, video_proj, audio_proj, pair_first, pair_count
):
    nblocks = lax.axis_size("seq")
    me = lax.axis_index("seq").astype(jnp.int32)
    core = lax.axis_index("head").astype(jnp.int32)
    me_arr = me[None]
    place = jnp.stack([lax.rem(me, LINE), core])

    def along_line(x, d):
        return lax.ppermute(
            x, "seq", [(s, s // LINE * LINE + (s + d) % LINE) for s in range(nblocks)]
        )

    def across_lines(x, d):
        return lax.ppermute(x, "seq", [(s, (s + d * LINE) % nblocks) for s in range(nblocks)])

    def swap(x):
        return lax.ppermute(x, "head", [(0, 1), (1, 0)])

    kv_out = pack((1, 2, 3), me_arr, audio_key, audio_value)
    kv = [along_line(piece, d + 1) for d, piece in enumerate(kv_out)]
    near1, near3 = pack((1, 3), me_arr, video_query, video_value, kv_out[0])
    qv1, qv3 = along_line(near1, 1), along_line(near3, 3)
    (far,) = pack((2,), me_arr, video_query, video_value, qv1, qv3, limit=32)
    qv2 = along_line(far, 2)
    v_own, v_other, a_own, a_send = load_projections(place, video_proj, audio_proj, kv[0])
    a_other = swap(a_send)
    low, high = line_blocks(me_arr, audio_key, audio_value, *kv)
    before, after = across_lines(high, 1), across_lines(low, -1)

    info = (me_arr, pair_first, pair_count)
    kvs = (before, low, high, after)
    o0, u, c, kv_all = attend((0,), info, kvs, (video_query, video_value), (), (), False)
    o1, o3, u, c = attend((1, 3), info, (), (), (qv1, qv3), (kv_all, u, c), False)
    o2, u, c, to_prev, to_next = attend((2,), info, (), (), (qv2,), (kv_all, u, c), True)
    from_next, from_prev = across_lines(to_prev, -1), across_lines(to_next, 1)

    v1, v3, v2 = along_line(o1, -1), along_line(o3, -3), along_line(o2, -2)
    base, base_other = project_near(place, (o0, v1, v3), v_own, v_other)
    m0, m1, m2, m3 = merge(me_arr, u, c, from_prev, from_next)
    given = project_far(place, v2, v_other, base_other, after=(m0,))
    video_out = project_far(place, v2, v_own, base, received=(swap(given),))

    a_mine = (m0, along_line(m3, 3), along_line(m2, 2), along_line(m1, 1))
    audio_out = project(place, a_mine, tuple(swap(m) for m in a_mine), a_own, a_other)
    return video_out, audio_out


def solution(mesh):
    in_specs = (
        P("seq", "head"),
        P("seq", "head"),
        P("seq", "head"),
        P("seq", "head"),
        P("head", None),
        P("head", None),
        P(),
        P(),
    )
    out_specs = (P("seq", "head"), P("seq", "head"))
    return jax.shard_map(shards, mesh=mesh, in_specs=in_specs, out_specs=out_specs, check_vma=False)
```

time: 323 us -> 117 us (0.36); the launches traced: 321 us -> 118 us
  Pallas kernels: 195 us -> 54.3 us
  waiting for transfers between devices: 60.4 us -> 28.2 us
  local copies, waits for them, and re-layouts: 17.1 us -> 0.05 us
  starting transfers between devices: 45.4 us -> 34.4 us
    pallas_call x2 -> x7, Pallas kernels: 110 us -> 30.2 us  [the longest x1 13.3 us: load_projections(): pl.pallas_call(load_kernel, out_shape=(half,) * 4, in_specs=[SMEM, ANY, A...]
    pallas_call x1, Pallas kernels: 48.8 us -> 1.49 us  [line_blocks(): pl.pallas_call(line_kernel, out_shape=(half, half), in_specs=[SMEM] + [AN...]
    ppermute x4, waiting for transfers between devices: 19.2 us -> 3.02 us  [across_lines(): lax.ppermute(x, 'seq', [(s, (s + d * LINE) % nblocks) for s in range(nblo...]
    ppermute x12, waiting for transfers between devices: 41.2 us -> 25.2 us  [along_line(): lax.ppermute(x, 'seq', [(s, s // LINE * LINE + (s + d) % LINE) for s in r...]
    pallas_call x2 -> x1, Pallas kernels: 17.5 us -> 4.25 us  [project(): pl.pallas_call(project_kernel, out_shape=jax.ShapeDtypeStruct((rows, widt...]
    dynamic_slice x2 -> x0, local copies, waits for them, and re-layouts: 7.78 us -> none  [the longest x1 5.2 us: shards(): lax.dynamic_slice_in_dim(audio_proj, (1 - core) * width, width, 1)]
    unnamed x28 -> x20, local copies, waits for them, and re-layouts: 6.63 us -> 0.05 us
    ppermute x5 -> x6, starting transfers between devices: 14.8 us -> 8.77 us  [swap(): return lax.ppermute(x, 'head', [(0, 1), (1, 0)])]
  transfers between devices with their start and end apart: 21 -> 22, of which waited for: 5 -> 9; matrix products, arithmetic and copies ran while one was open for 4% -> 0% of each run, Pallas kernels for 46% -> 40%
where the time goes in v2:
time: 117 us; the launch traced here: 118 us
  Pallas kernels  54.3 us (46%)
  starting transfers between devices  34.4 us (29%)
  waiting for transfers between devices  28.2 us (24%)
    ppermute x12, waiting for transfers between devices, along_line(): lax.ppermute(x, 'seq', [(s, s // LINE * LINE + (s + d) % LINE) for s in r...  25.2 us
    pallas_call x3, Pallas kernels, attend(): pl.pallas_call(functools.partial(attend_kernel, steps, bool(own), bool(su...  17.8 us
    ppermute x12, starting transfers between devices, along_line(): lax.ppermute(x, 'seq', [(s, s // LINE * LINE + (s + d) % LINE) for s in r...  14.6 us
    pallas_call x1, Pallas kernels, load_projections(): pl.pallas_call(load_kernel, out_shape=(half,) * 4, in_specs=[SMEM, ANY, A...  13.3 us
    ppermute x4, starting transfers between devices, across_lines(): lax.ppermute(x, 'seq', [(s, (s + d * LINE) % nblocks) for s in range(nblo...  11 us
    ppermute x6, starting transfers between devices, swap(): return lax.ppermute(x, 'head', [(0, 1), (1, 0)])  8.77 us
    pallas_call x1, Pallas kernels, project_near(): pl.pallas_call(near_kernel, out_shape=(jax.ShapeDtypeStruct((rows, width)...  6.25 us
    pallas_call x2, Pallas kernels, project_far(): pl.pallas_call(functools.partial(far_kernel, 1 + len(received)), out_shap...  5.69 us
  transfers between devices with their start and end apart: 22, of which 9 were waited for; matrix products, arithmetic and copies ran while one was open for 0% of the time, Pallas kernels for 40%

profile of v2, /device:TPU:1, one launch (start us, length us, event | category | flops | bytes accessed | tf_op | source)
XLA Modules:
  0.0 118.1 jit_solution(16654694110519726545)
XLA Ops:
  0.7 2.3 %pack.3 = (bf16[2,256,384]{2,1,0:T(8,128)(2,1)}, bf16[2,256,384]{2,1,0:T(8,128)(2,1)}, bf16[2,256,384]{2,1,0:T(8,128)(2,1)}) custom-call(s32[1]{0:T(128)} %bitcast.2.me.refs_0_, bf16[256,1536]{1,0:T(8,128)(2,1)} %k.1, bf16[256,1536]{1,0:T(8,128)(2,1)} %v.2), custom_call_target="tpu_custom_call" | custom-call | flops 1000000 | bytes 1000 | tf_op jit(solution)/shard_map/pack/pallas_call | solution.py:64
  2.9 3.8 %collective-permute-start.4 = (bf16[2,256,384]{2,1,0:T(8,128)(2,1)}, bf16[2,256,384]{2,1,0:T(8,128)(2,1)}, u32[]{:S(2)}, u32[]{:S(2)}) collective-permute-start(bf16[2,256,384]{2,1,0:T(8,128)(2,1)} %get-tuple-element.35), channel_id=1, source_target_pairs={{0,4},{2,6},{4,0},{6,2},{8,12},{10,14},{12,8},{14,10},{16,20},{18,... | collective-permute-start | bytes 1179656 | tf_op jit(solution)/shard_map/ppermute | solution.py:472
  6.8 0.8 collective-permute-start.5
  7.5 0.7 collective-permute-start.3
  8.2 2.2 %pack.4 = (bf16[2,512,384]{2,1,0:T(8,128)(2,1)}, bf16[2,512,384]{2,1,0:T(8,128)(2,1)}) custom-call(s32[1]{0:T(128)} %bitcast.2.me.refs_0_, bf16[512,1536]{1,0:T(8,128)(2,1)} %refs_7_.1, bf16[512,1536]{1,0:T(8,128)(2,1)} %refs_8_.1, bf16[2,256,384]{2,1,0:T(8,128)(2,1)} %get-tuple-element.32.refs_0_), custom_call_target="tpu_custom_call" | custom-call | flops 1000000 | bytes 1000 | tf_op jit(solution)/shard_map/pack/pallas_call | solution.py:64
  10.9 2.3 %collective-permute-start.1 = (bf16[2,512,384]{2,1,0:T(8,128)(2,1)}, bf16[2,512,384]{2,1,0:T(8,128)(2,1)S(1)}, u32[]{:S(2)}, u32[]{:S(2)}) collective-permute-start(bf16[2,512,384]{2,1,0:T(8,128)(2,1)} %get-tuple-element.34), channel_id=1, source_target_pairs={{0,6},{2,0},{4,2},{6,4},{8,14},{10,8},{12,10},{14,12},{16,22},{18,... | collective-permute-start | bytes 2359304 | tf_op jit(solution)/shard_map/ppermute | solution.py:472
  13.2 2.5 %collective-permute-done.4.kv2 = bf16[2,256,384]{2,1,0:T(8,128)(2,1)} collective-permute-done((bf16[2,256,384]{2,1,0:T(8,128)(2,1)}, bf16[2,256,384]{2,1,0:T(8,128)(2,1)}, u32[]{:S(2)}, u32[]{:S(2)}) %collective-permute-start.4) | collective-permute-done | bytes 393248 | tf_op jit(solution)/shard_map/ppermute | solution.py:472
  15.7 8.8 %collective-permute-done.5.kv3 = bf16[2,256,384]{2,1,0:T(8,128)(2,1)} collective-permute-done((bf16[2,256,384]{2,1,0:T(8,128)(2,1)}, bf16[2,256,384]{2,1,0:T(8,128)(2,1)}, u32[]{:S(2)}, u32[]{:S(2)}) %collective-permute-start.5) | collective-permute-done | bytes 393248 | tf_op jit(solution)/shard_map/ppermute | solution.py:472
  25.0 1.5 %line_blocks.1 = (bf16[2,2,256,384]{3,2,1,0:T(8,128)(2,1)S(1)}, bf16[2,2,256,384]{3,2,1,0:T(8,128)(2,1)S(1)}) custom-call(s32[1]{0:T(128)} %bitcast.2.me.refs_0_, bf16[256,1536]{1,0:T(8,128)(2,1)S(1)} %copy-done.2, bf16[256,1536]{1,0:T(8,128)(2,1)S(1)} %copy-done.3, bf16[2,256,384]{2,1,0:T(8,128)(2,1)S(1)} %collective-permute-done.3.kv1.after, ...), custom_call_target="tpu_custom_call" | custom-call | flops 1000000 | bytes 1000 | tf_op jit(solution)/shard_map/line_blocks/pallas_call | solution.py:133
  26.5 1.8 %collective-permute-start.6 = (bf16[2,2,256,384]{3,2,1,0:T(8,128)(2,1)S(1)}, bf16[2,2,256,384]{3,2,1,0:T(8,128)(2,1)S(1)}, u32[]{:S(2)}, u32[]{:S(2)}) collective-permute-start(bf16[2,2,256,384]{3,2,1,0:T(8,128)(2,1)S(1)} %get-tuple-element.37.refs_5_), channel_id=1, source_target_pairs={{0,8},{2,10},{4,12},{6,14},{8,16},{10,18},{12,20},{14,22},{16,24},... | collective-permute-start | bytes 2359304 | tf_op jit(solution)/shard_map/ppermute | solution.py:477
  28.2 4.4 %collective-permute-start.7 = (bf16[2,2,256,384]{3,2,1,0:T(8,128)(2,1)S(1)}, bf16[2,2,256,384]{3,2,1,0:T(8,128)(2,1)S(1)}, u32[]{:S(2)}, u32[]{:S(2)}) collective-permute-start(bf16[2,2,256,384]{3,2,1,0:T(8,128)(2,1)S(1)} %get-tuple-element.38.refs_4_), channel_id=1, source_target_pairs={{0,120},{2,122},{4,124},{6,126},{8,0},{10,2},{12,4},{14,6},{16,8},... | collective-permute-start | bytes 2359304 | tf_op jit(solution)/shard_map/ppermute | solution.py:477
  32.7 13.3 %load_projections.1 = (bf16[1536,1536]{1,0:T(8,128)(2,1)S(1)}, bf16[1536,1536]{1,0:T(8,128)(2,1)}, bf16[1536,1536]{1,0:T(8,128)(2,1)}, bf16[1536,1536]{1,0:T(8,128)(2,1)}) custom-call(s32[2]{0:T(128)S(1)} %pad_add_fusion.place, bf16[1536,3072]{1,0:T(8,128)(2,1)} %v.3, bf16[1536,3072]{1,0:T(8,128)(2,1)} %a.7, ...), custom_call_target="tpu_custom_call" | custom-call | flops 6000000000 | bytes 1000 | tf_op jit(solution)/shard_map/load_projections/pallas_call | solution.py:96
  46.0 2.5 %collective-permute-start.21 = (bf16[1536,1536]{1,0:T(8,128)(2,1)}, bf16[1536,1536]{1,0:T(8,128)(2,1)S(1)}, u32[]{:S(2)}, u32[]{:S(2)}) collective-permute-start(bf16[1536,1536]{1,0:T(8,128)(2,1)} %get-tuple-element.61), channel_id=1, source_target_pairs={{0,1},{1,0},{2,3},{3,2},{4,5},{5,4},{6,7},{7,6},{8,9},{9,8},{10,11... | collective-permute-start | bytes 14155784 | tf_op jit(solution)/shard_map/ppermute | solution.py:480
  49.1 1.6 %collective-permute-start.2 = (bf16[2,512,384]{2,1,0:T(8,128)(2,1)S(1)}, bf16[2,512,384]{2,1,0:T(8,128)(2,1)S(1)}, u32[]{:S(2)}, u32[]{:S(2)}) collective-permute-start(bf16[2,512,384]{2,1,0:T(8,128)(2,1)S(1)} %pack.5), channel_id=1, source_target_pairs={{0,4},{2,6},{4,0},{6,2},{8,12},{10,14},{12,8},{14,10},{16,20},{18,... | collective-permute-start | bytes 2359304 | tf_op jit(solution)/shard_map/ppermute | solution.py:472
  50.8 2.7 %attend.2 = (bf16[512,384]{1,0:T(8,128)(2,1)S(1)}, f32[3,8,144,256]{3,2,1,0:T(8,128)S(1)}, f32[3,8,8,256]{3,2,1,0:T(8,128)S(1)}, bf16[8,2,256,384]{3,2,1,0:T(8,128)(2,1)S(1)}) custom-call(s32[1]{0:T(128)} %bitcast.2.me.refs_0_, s32[64]{0:T(128)S(1)} %copy-done.4, s32[64]{0:T(128)S(1)} %copy-done.5, ...), custom_call_target="tpu_custom_call" | custom-call | flops 6000000000 | bytes 1000 | tf_op jit(solution)/shard_map/attend/pallas_call | solution.py:288
  53.5 8.3 %attend.3 = (bf16[512,384]{1,0:T(8,128)(2,1)S(1)}, bf16[512,384]{1,0:T(8,128)(2,1)S(1)}, f32[3,8,144,256]{3,2,1,0:T(8,128)S(1)}, f32[3,8,8,256]{3,2,1,0:T(8,128)S(1)}) custom-call(s32[1]{0:T(128)} %bitcast.2.me.refs_0_, s32[64]{0:T(128)S(1)} %copy-done.4, s32[64]{0:T(128)S(1)} %copy-done.5, ...), custom_call_target="tpu_custom_call", output_to_operand_aliasing={{2}: (6, {}), {3}: (7, {})} | custom-call | flops 12000000000 | bytes 1000 | tf_op jit(solution)/shard_map/attend/pallas_call | solution.py:288
  61.9 3.1 %collective-permute-start.9 = (bf16[512,384]{1,0:T(8,128)(2,1)S(1)}, bf16[512,384]{1,0:T(8,128)(2,1)S(1)}, u32[]{:S(2)}, u32[]{:S(2)}) collective-permute-start(bf16[512,384]{1,0:T(8,128)(2,1)S(1)} %get-tuple-element.47), channel_id=1, source_target_pairs={{0,6},{2,0},{4,2},{6,4},{8,14},{10,8},{12,10},{14,12},{16,22},{18,... | collective-permute-start | bytes 1179656 | tf_op jit(solution)/shard_map/ppermute | solution.py:472
  65.3 4.5 %collective-permute-done.2.refs_3_ = bf16[2,512,384]{2,1,0:T(8,128)(2,1)S(1)} collective-permute-done((bf16[2,512,384]{2,1,0:T(8,128)(2,1)S(1)}, bf16[2,512,384]{2,1,0:T(8,128)(2,1)S(1)}, u32[]{:S(2)}, u32[]{:S(2)}) %collective-permute-start.2) | collective-permute-done | bytes 786464 | tf_op jit(solution)/shard_map/ppermute | solution.py:472
  69.8 6.7 %attend_last.1 = (bf16[512,384]{1,0:T(8,128)(2,1)S(1)}, f32[3,8,144,256]{3,2,1,0:T(8,128)S(1)}, f32[3,8,8,256]{3,2,1,0:T(8,128)S(1)}, bf16[2,3,144,256]{3,2,1,0:T(8,128)(2,1)S(1)}, bf16[2,3,144,256]{3,2,1,0:T(8,128)(2,1)S(1)}) custom-call(s32[1]{0:T(128)} %bitcast.2.me.refs_0_, s32[64]{0:T(128)S(1)} %copy-done.4, ...), custom_call_target="tpu_custom_call", output_to_operand_aliasing={{1}: (5, {}), {2}: (6, {})} | custom-call | flops 6000000000 | bytes 1000 | tf_op jit(solution)/shard_map/attend_last/pallas_call | solution.py:288
  76.6 4.8 %collective-permute-start.12 = (bf16[2,3,144,256]{3,2,1,0:T(8,128)(2,1)S(1)}, bf16[2,3,144,256]{3,2,1,0:T(8,128)(2,1)S(1)}, u32[]{:S(2)}, u32[]{:S(2)}) collective-permute-start(bf16[2,3,144,256]{3,2,1,0:T(8,128)(2,1)S(1)} %get-tuple-element.55), channel_id=1, source_target_pairs={{0,120},{2,122},{4,124},{6,126},{8,0},{10,2},{12,4},{14,6},{16,8},... | collective-permute-start | bytes 1327112 | tf_op jit(solution)/shard_map/ppermute | solution.py:477
  81.4 6.2 %project_near.1 = (f32[512,1536]{1,0:T(8,128)S(1)}, f32[512,1536]{1,0:T(8,128)S(1)}) custom-call(s32[2]{0:T(128)S(1)} %pad_add_fusion.place, bf16[512,384]{1,0:T(8,128)(2,1)S(1)} %get-tuple-element.46.o0, bf16[512,384]{1,0:T(8,128)(2,1)S(1)} %collective-permute-done.9.o1, bf16[512,384]{1,0:T(8,128)(2,1)S(1)} %collective-permute-done.10.o3, ...), custom_call_target="tpu_custom_call" | custom-call | flops 4000000000 | bytes 1000 | tf_op jit(solution)/shard_map/project_near/pallas_call | solution.py:358
  87.7 3.0 %collective-permute-done.11.prev = bf16[2,3,144,256]{3,2,1,0:T(8,128)(2,1)S(1)} collective-permute-done((bf16[2,3,144,256]{3,2,1,0:T(8,128)(2,1)S(1)}, bf16[2,3,144,256]{3,2,1,0:T(8,128)(2,1)S(1)}, u32[]{:S(2)}, u32[]{:S(2)}) %collective-permute-start.11) | collective-permute-done | bytes 442400 | tf_op jit(solution)/shard_map/ppermute | solution.py:477
  91.3 0.8 collective-permute-done.8.piece
  92.0 2.8 %project_far.2 = bf16[512,1536]{1,0:T(8,128)(2,1)S(1)} custom-call(s32[2]{0:T(128)S(1)} %pad_add_fusion.place, bf16[512,384]{1,0:T(8,128)(2,1)S(1)} %collective-permute-done.8.piece, bf16[1536,1536]{1,0:T(8,128)(2,1)S(1)} %bitcast.4, f32[512,1536]{1,0:T(8,128)S(1)} %get-tuple-element.51.refs_0_, bf16[256,384]{1,0:T(8,128)(2,1)S(1)} %get-tuple-element.56.refs_1_.refs_0_), custom_call_target="tpu_custom_call" | custom-call | flops 1000000000 | bytes 1000 | tf_op jit(solution)/shard_map/project_far/pallas_call | solution.py:399
  94.9 2.5 %collective-permute-start.13 = (bf16[512,1536]{1,0:T(8,128)(2,1)S(1)}, bf16[512,1536]{1,0:T(8,128)(2,1)S(1)}, u32[]{:S(2)}, u32[]{:S(2)}) collective-permute-start(bf16[512,1536]{1,0:T(8,128)(2,1)S(1)} %project_far.2), channel_id=1, source_target_pairs={{0,1},{1,0},{2,3},{3,2},{4,5},{5,4},{6,7},{7,6},{8,9},{9,8},{10,11... | collective-permute-start | bytes 4718600 | tf_op jit(solution)/shard_map/ppermute | solution.py:480
  97.7 1.1 collective-permute-start.16
  98.8 5.0 %collective-permute-done.14.refs_1_ = bf16[256,384]{1,0:T(8,128)(2,1)S(1)} collective-permute-done((bf16[256,384]{1,0:T(8,128)(2,1)S(1)}, bf16[256,384]{1,0:T(8,128)(2,1)S(1)}, u32[]{:S(2)}, u32[]{:S(2)}) %collective-permute-start.14) | collective-permute-done | bytes 196640 | tf_op jit(solution)/shard_map/ppermute | solution.py:472
  103.8 1.3 %collective-permute-start.17 = (bf16[256,384]{1,0:T(8,128)(2,1)S(1)}, bf16[256,384]{1,0:T(8,128)(2,1)S(1)}, u32[]{:S(2)}, u32[]{:S(2)}) collective-permute-start(bf16[256,384]{1,0:T(8,128)(2,1)S(1)} %get-tuple-element.56.refs_1_.refs_0_), channel_id=1, source_target_pairs={{0,1},{1,0},{2,3},{3,2},{4,5},{5,4},{6,7},{7,6},{8,9},{9,8},{10,11... | collective-permute-start | bytes 589832 | tf_op jit(solution)/shard_map/ppermute | solution.py:480
  105.4 2.0 %collective-permute-start.18 = (bf16[256,384]{1,0:T(8,128)(2,1)S(1)}, bf16[256,384]{1,0:T(8,128)(2,1)S(1)}, u32[]{:S(2)}, u32[]{:S(2)}) collective-permute-start(bf16[256,384]{1,0:T(8,128)(2,1)S(1)} %collective-permute-done.14.refs_1_), channel_id=1, source_target_pairs={{0,1},{1,0},{2,3},{3,2},{4,5},{5,4},{6,7},{7,6},{8,9},{9,8},{10,11... | collective-permute-start | bytes 589832 | tf_op jit(solution)/shard_map/ppermute | solution.py:480
  107.3 2.9 %collective-permute-done.16.refs_3_ = bf16[256,384]{1,0:T(8,128)(2,1)S(1)} collective-permute-done((bf16[256,384]{1,0:T(8,128)(2,1)S(1)}, bf16[256,384]{1,0:T(8,128)(2,1)S(1)}, u32[]{:S(2)}, u32[]{:S(2)}) %collective-permute-start.16) | collective-permute-done | bytes 196640 | tf_op jit(solution)/shard_map/ppermute | solution.py:472
  110.8 2.9 %project_far.3 = bf16[512,1536]{1,0:T(8,128)(2,1)} custom-call(s32[2]{0:T(128)S(1)} %pad_add_fusion.place, bf16[512,384]{1,0:T(8,128)(2,1)S(1)} %collective-permute-done.8.piece, bf16[1536,1536]{1,0:T(8,128)(2,1)S(1)} %get-tuple-element.45.w_own.w, f32[512,1536]{1,0:T(8,128)S(1)} %get-tuple-element.50.refs_0_, ...), custom_call_target="tpu_custom_call" | custom-call | flops 1000000000 | bytes 1000 | tf_op jit(solution)/shard_map/project_far/pallas_call | solution.py:399
  113.7 4.2 %project.1 = bf16[256,1536]{1,0:T(8,128)(2,1)} custom-call(s32[2]{0:T(128)S(1)} %pad_add_fusion.place, bf16[256,384]{1,0:T(8,128)(2,1)S(1)} %get-tuple-element.56.refs_1_.refs_0_, bf16[256,384]{1,0:T(8,128)(2,1)S(1)} %collective-permute-done.14.refs_1_, bf16[256,384]{1,0:T(8,128)(2,1)S(1)} %collective-permute-done.15.refs_2_, ...), custom_call_target="tpu_custom_call" | custom-call | flops 4000000000 | bytes 1000 | tf_op jit(solution)/shard_map/project/pallas_call | solution.py:445
  (48 shorter events, 3.8 us)
Async XLA Ops:
  0.6 24.4 %copy-start.3 = (bf16[256,1536]{1,0:T(8,128)(2,1)S(1)}, bf16[256,1536]{1,0:T(8,128)(2,1)}, u32[]{:S(2)}) copy-start(bf16[256,1536]{1,0:T(8,128)(2,1)} %v.2) | copy-start | bytes 2359300
  0.6 24.4 %copy-start.2 = (bf16[256,1536]{1,0:T(8,128)(2,1)S(1)}, bf16[256,1536]{1,0:T(8,128)(2,1)}, u32[]{:S(2)}) copy-start(bf16[256,1536]{1,0:T(8,128)(2,1)} %k.1) | copy-start | bytes 2359300
  2.9 12.7 %collective-permute-start.4 = (bf16[2,256,384]{2,1,0:T(8,128)(2,1)}, bf16[2,256,384]{2,1,0:T(8,128)(2,1)}, u32[]{:S(2)}, u32[]{:S(2)}) collective-permute-start(bf16[2,256,384]{2,1,0:T(8,128)(2,1)} %get-tuple-element.35), channel_id=1, source_target_pairs={{0,4},{2,6},{4,0},{6,2},{8,12},{10,14},{12,8},{14,10},{16,20},{18,... | collective-permute-start | bytes 1179656 | tf_op jit(solution)/shard_map/ppermute | solution.py:472
  6.8 17.7 %collective-permute-start.5 = (bf16[2,256,384]{2,1,0:T(8,128)(2,1)}, bf16[2,256,384]{2,1,0:T(8,128)(2,1)}, u32[]{:S(2)}, u32[]{:S(2)}) collective-permute-start(bf16[2,256,384]{2,1,0:T(8,128)(2,1)} %get-tuple-element.36), channel_id=1, source_target_pairs={{0,6},{2,0},{4,2},{6,4},{8,14},{10,8},{12,10},{14,12},{16,22},{18,... | collective-permute-start | bytes 1179656 | tf_op jit(solution)/shard_map/ppermute | solution.py:472
  7.5 17.4 %collective-permute-start.3 = (bf16[2,256,384]{2,1,0:T(8,128)(2,1)}, bf16[2,256,384]{2,1,0:T(8,128)(2,1)S(1)}, u32[]{:S(2)}, u32[]{:S(2)}) collective-permute-start(bf16[2,256,384]{2,1,0:T(8,128)(2,1)} %get-tuple-element.32.refs_0_), channel_id=1, source_target_pairs={{0,2},{2,4},{4,6},{6,0},{8,10},{10,12},{12,14},{14,8},{16,18},{18,... | collective-permute-start | bytes 1179656 | tf_op jit(solution)/shard_map/ppermute | solution.py:472
  10.4 38.1 %collective-permute-start = (bf16[2,512,384]{2,1,0:T(8,128)(2,1)}, bf16[2,512,384]{2,1,0:T(8,128)(2,1)S(1)}, u32[]{:S(2)}, u32[]{:S(2)}) collective-permute-start(bf16[2,512,384]{2,1,0:T(8,128)(2,1)} %get-tuple-element.33), channel_id=1, source_target_pairs={{0,2},{2,4},{4,6},{6,0},{8,10},{10,12},{12,14},{14,8},{16,18},{18,... | collective-permute-start | bytes 2359304 | tf_op jit(solution)/shard_map/ppermute | solution.py:472
  10.9 37.7 %collective-permute-start.1 = (bf16[2,512,384]{2,1,0:T(8,128)(2,1)}, bf16[2,512,384]{2,1,0:T(8,128)(2,1)S(1)}, u32[]{:S(2)}, u32[]{:S(2)}) collective-permute-start(bf16[2,512,384]{2,1,0:T(8,128)(2,1)} %get-tuple-element.34), channel_id=1, source_target_pairs={{0,6},{2,0},{4,2},{6,4},{8,14},{10,8},{12,10},{14,12},{16,22},{18,... | collective-permute-start | bytes 2359304 | tf_op jit(solution)/shard_map/ppermute | solution.py:472
  26.5 24.2 %collective-permute-start.6 = (bf16[2,2,256,384]{3,2,1,0:T(8,128)(2,1)S(1)}, bf16[2,2,256,384]{3,2,1,0:T(8,128)(2,1)S(1)}, u32[]{:S(2)}, u32[]{:S(2)}) collective-permute-start(bf16[2,2,256,384]{3,2,1,0:T(8,128)(2,1)S(1)} %get-tuple-element.37.refs_5_), channel_id=1, source_target_pairs={{0,8},{2,10},{4,12},{6,14},{8,16},{10,18},{12,20},{14,22},{16,24},... | collective-permute-start | bytes 2359304 | tf_op jit(solution)/shard_map/ppermute | solution.py:477
  28.2 22.5 %collective-permute-start.7 = (bf16[2,2,256,384]{3,2,1,0:T(8,128)(2,1)S(1)}, bf16[2,2,256,384]{3,2,1,0:T(8,128)(2,1)S(1)}, u32[]{:S(2)}, u32[]{:S(2)}) collective-permute-start(bf16[2,2,256,384]{3,2,1,0:T(8,128)(2,1)S(1)} %get-tuple-element.38.refs_4_), channel_id=1, source_target_pairs={{0,120},{2,122},{4,124},{6,126},{8,0},{10,2},{12,4},{14,6},{16,8},... | collective-permute-start | bytes 2359304 | tf_op jit(solution)/shard_map/ppermute | solution.py:477
  32.7 15.8 %copy-start = (bf16[512,1536]{1,0:T(8,128)(2,1)S(1)}, bf16[512,1536]{1,0:T(8,128)(2,1)}, u32[]{:S(2)}) copy-start(bf16[512,1536]{1,0:T(8,128)(2,1)} %refs_7_.1) | copy-start | bytes 4718596
  32.7 15.8 %copy-start.1 = (bf16[512,1536]{1,0:T(8,128)(2,1)S(1)}, bf16[512,1536]{1,0:T(8,128)(2,1)}, u32[]{:S(2)}) copy-start(bf16[512,1536]{1,0:T(8,128)(2,1)} %refs_8_.1) | copy-start | bytes 4718596
  46.0 4.7 %copy-start.4 = (s32[64]{0:T(128)S(1)}, s32[64]{0:T(128)}, u32[]{:S(2)}) copy-start(s32[64]{0:T(128)} %refs_1_.5) | copy-start | bytes 772
  46.0 4.7 %copy-start.5 = (s32[64]{0:T(128)S(1)}, s32[64]{0:T(128)}, u32[]{:S(2)}) copy-start(s32[64]{0:T(128)} %refs_2_.5) | copy-start | bytes 772
  46.0 67.7 %collective-permute-start.21 = (bf16[1536,1536]{1,0:T(8,128)(2,1)}, bf16[1536,1536]{1,0:T(8,128)(2,1)S(1)}, u32[]{:S(2)}, u32[]{:S(2)}) collective-permute-start(bf16[1536,1536]{1,0:T(8,128)(2,1)} %get-tuple-element.61), channel_id=1, source_target_pairs={{0,1},{1,0},{2,3},{3,2},{4,5},{5,4},{6,7},{7,6},{8,9},{9,8},{10,11... | collective-permute-start | bytes 14155784 | tf_op jit(solution)/shard_map/ppermute | solution.py:480
  49.1 20.7 %collective-permute-start.2 = (bf16[2,512,384]{2,1,0:T(8,128)(2,1)S(1)}, bf16[2,512,384]{2,1,0:T(8,128)(2,1)S(1)}, u32[]{:S(2)}, u32[]{:S(2)}) collective-permute-start(bf16[2,512,384]{2,1,0:T(8,128)(2,1)S(1)} %pack.5), channel_id=1, source_target_pairs={{0,4},{2,6},{4,0},{6,2},{8,12},{10,14},{12,8},{14,10},{16,20},{18,... | collective-permute-start | bytes 2359304 | tf_op jit(solution)/shard_map/ppermute | solution.py:472
  50.8 30.7 %slice-start = ((s8[4718592]{0:T(1024)(128)(4,1)}), s8[524288]{0:T(1024)(128)(4,1)S(1)}, s32[]{:S(2)}) async-start(s8[4718592]{0:T(1024)(128)(4,1)} %bitcast.3), calls=%async_computation | async-start | bytes 1048576
  53.5 27.9 %slice-start.1 = ((s8[4718592]{0:T(1024)(128)(4,1)}), s8[4194304]{0:T(1024)(128)(4,1)S(1)}, s32[]{:S(2)}) async-start(s8[4718592]{0:T(1024)(128)(4,1)} %bitcast.3), calls=%async_computation.1 | async-start | bytes 8388608
  61.9 19.5 %collective-permute-start.9 = (bf16[512,384]{1,0:T(8,128)(2,1)S(1)}, bf16[512,384]{1,0:T(8,128)(2,1)S(1)}, u32[]{:S(2)}, u32[]{:S(2)}) collective-permute-start(bf16[512,384]{1,0:T(8,128)(2,1)S(1)} %get-tuple-element.47), channel_id=1, source_target_pairs={{0,6},{2,0},{4,2},{6,4},{8,14},{10,8},{12,10},{14,12},{16,22},{18,... | collective-permute-start | bytes 1179656 | tf_op jit(solution)/shard_map/ppermute | solution.py:472
  65.0 16.4 %collective-permute-start.10 = (bf16[512,384]{1,0:T(8,128)(2,1)S(1)}, bf16[512,384]{1,0:T(8,128)(2,1)S(1)}, u32[]{:S(2)}, u32[]{:S(2)}) collective-permute-start(bf16[512,384]{1,0:T(8,128)(2,1)S(1)} %get-tuple-element.48), channel_id=1, source_target_pairs={{0,2},{2,4},{4,6},{6,0},{8,10},{10,12},{12,14},{14,8},{16,18},{18,... | collective-permute-start | bytes 1179656 | tf_op jit(solution)/shard_map/ppermute | solution.py:472
  76.5 14.2 %collective-permute-start.11 = (bf16[2,3,144,256]{3,2,1,0:T(8,128)(2,1)S(1)}, bf16[2,3,144,256]{3,2,1,0:T(8,128)(2,1)S(1)}, u32[]{:S(2)}, u32[]{:S(2)}) collective-permute-start(bf16[2,3,144,256]{3,2,1,0:T(8,128)(2,1)S(1)} %get-tuple-element.54), channel_id=1, source_target_pairs={{0,8},{2,10},{4,12},{6,14},{8,16},{10,18},{12,20},{14,22},{16,24},... | collective-permute-start | bytes 1327112 | tf_op jit(solution)/shard_map/ppermute | solution.py:477
  76.6 14.1 %collective-permute-start.12 = (bf16[2,3,144,256]{3,2,1,0:T(8,128)(2,1)S(1)}, bf16[2,3,144,256]{3,2,1,0:T(8,128)(2,1)S(1)}, u32[]{:S(2)}, u32[]{:S(2)}) collective-permute-start(bf16[2,3,144,256]{3,2,1,0:T(8,128)(2,1)S(1)} %get-tuple-element.55), channel_id=1, source_target_pairs={{0,120},{2,122},{4,124},{6,126},{8,0},{10,2},{12,4},{14,6},{16,8},... | collective-permute-start | bytes 1327112 | tf_op jit(solution)/shard_map/ppermute | solution.py:477
  81.4 10.6 %collective-permute-start.8 = (bf16[512,384]{1,0:T(8,128)(2,1)S(1)}, bf16[512,384]{1,0:T(8,128)(2,1)S(1)}, u32[]{:S(2)}, u32[]{:S(2)}) collective-permute-start(bf16[512,384]{1,0:T(8,128)(2,1)S(1)} %get-tuple-element.44), channel_id=1, source_target_pairs={{0,4},{2,6},{4,0},{6,2},{8,12},{10,14},{12,8},{14,10},{16,20},{18,... | collective-permute-start | bytes 1179656 | tf_op jit(solution)/shard_map/ppermute | solution.py:472
  92.0 21.7 %slice-start.2 = ((s8[4718592]{0:T(1024)(128)(4,1)}), s8[4194304]{0:T(1024)(128)(4,1)S(1)}, s32[]{:S(2)}) async-start(s8[4718592]{0:T(1024)(128)(4,1)} %bitcast.5), calls=%async_computation.2 | async-start | bytes 8388608
  94.9 15.9 %collective-permute-start.13 = (bf16[512,1536]{1,0:T(8,128)(2,1)S(1)}, bf16[512,1536]{1,0:T(8,128)(2,1)S(1)}, u32[]{:S(2)}, u32[]{:S(2)}) collective-permute-start(bf16[512,1536]{1,0:T(8,128)(2,1)S(1)} %project_far.2), channel_id=1, source_target_pairs={{0,1},{1,0},{2,3},{3,2},{4,5},{5,4},{6,7},{7,6},{8,9},{9,8},{10,11... | collective-permute-start | bytes 4718600 | tf_op jit(solution)/shard_map/ppermute | solution.py:480
  97.3 6.5 %collective-permute-start.14 = (bf16[256,384]{1,0:T(8,128)(2,1)S(1)}, bf16[256,384]{1,0:T(8,128)(2,1)S(1)}, u32[]{:S(2)}, u32[]{:S(2)}) collective-permute-start(bf16[256,384]{1,0:T(8,128)(2,1)S(1)} %get-tuple-element.57), channel_id=1, source_target_pairs={{0,6},{2,0},{4,2},{6,4},{8,14},{10,8},{12,10},{14,12},{16,22},{18,... | collective-permute-start | bytes 589832 | tf_op jit(solution)/shard_map/ppermute | solution.py:472
  97.7 7.7 %collective-permute-start.15 = (bf16[256,384]{1,0:T(8,128)(2,1)S(1)}, bf16[256,384]{1,0:T(8,128)(2,1)S(1)}, u32[]{:S(2)}, u32[]{:S(2)}) collective-permute-start(bf16[256,384]{1,0:T(8,128)(2,1)S(1)} %get-tuple-element.58), channel_id=1, source_target_pairs={{0,4},{2,6},{4,0},{6,2},{8,12},{10,14},{12,8},{14,10},{16,20},{18,... | collective-permute-start | bytes 589832 | tf_op jit(solution)/shard_map/ppermute | solution.py:472
  97.7 12.6 %collective-permute-start.16 = (bf16[256,384]{1,0:T(8,128)(2,1)S(1)}, bf16[256,384]{1,0:T(8,128)(2,1)S(1)}, u32[]{:S(2)}, u32[]{:S(2)}) collective-permute-start(bf16[256,384]{1,0:T(8,128)(2,1)S(1)} %get-tuple-element.59), channel_id=1, source_target_pairs={{0,2},{2,4},{4,6},{6,0},{8,10},{10,12},{12,14},{14,8},{16,18},{18,... | collective-permute-start | bytes 589832 | tf_op jit(solution)/shard_map/ppermute | solution.py:472
  103.8 9.8 %collective-permute-start.17 = (bf16[256,384]{1,0:T(8,128)(2,1)S(1)}, bf16[256,384]{1,0:T(8,128)(2,1)S(1)}, u32[]{:S(2)}, u32[]{:S(2)}) collective-permute-start(bf16[256,384]{1,0:T(8,128)(2,1)S(1)} %get-tuple-element.56.refs_1_.refs_0_), channel_id=1, source_target_pairs={{0,1},{1,0},{2,3},{3,2},{4,5},{5,4},{6,7},{7,6},{8,9},{9,8},{10,11... | collective-permute-start | bytes 589832 | tf_op jit(solution)/shard_map/ppermute | solution.py:480
  105.4 8.3 %collective-permute-start.18 = (bf16[256,384]{1,0:T(8,128)(2,1)S(1)}, bf16[256,384]{1,0:T(8,128)(2,1)S(1)}, u32[]{:S(2)}, u32[]{:S(2)}) collective-permute-start(bf16[256,384]{1,0:T(8,128)(2,1)S(1)} %collective-permute-done.14.refs_1_), channel_id=1, source_target_pairs={{0,1},{1,0},{2,3},{3,2},{4,5},{5,4},{6,7},{7,6},{8,9},{9,8},{10,11... | collective-permute-start | bytes 589832 | tf_op jit(solution)/shard_map/ppermute | solution.py:480
  110.3 3.4 %collective-permute-start.19 = (bf16[256,384]{1,0:T(8,128)(2,1)S(1)}, bf16[256,384]{1,0:T(8,128)(2,1)S(1)}, u32[]{:S(2)}, u32[]{:S(2)}) collective-permute-start(bf16[256,384]{1,0:T(8,128)(2,1)S(1)} %collective-permute-done.15.refs_2_), channel_id=1, source_target_pairs={{0,1},{1,0},{2,3},{3,2},{4,5},{5,4},{6,7},{7,6},{8,9},{9,8},{10,11... | collective-permute-start | bytes 589832 | tf_op jit(solution)/shard_map/ppermute | solution.py:480
  110.7 3.0 %collective-permute-start.20 = (bf16[256,384]{1,0:T(8,128)(2,1)S(1)}, bf16[256,384]{1,0:T(8,128)(2,1)S(1)}, u32[]{:S(2)}, u32[]{:S(2)}) collective-permute-start(bf16[256,384]{1,0:T(8,128)(2,1)S(1)} %collective-permute-done.16.refs_3_), channel_id=1, source_target_pairs={{0,1},{1,0},{2,3},{3,2},{4,5},{5,4},{6,7},{7,6},{8,9},{9,8},{10,11... | collective-permute-start | bytes 589832 | tf_op jit(solution)/shard_map/ppermute | solution.py:480
  110.8 2.9 %slice-start.3 = ((s8[4718592]{0:T(1024)(128)(4,1)}), s8[524288]{0:T(1024)(128)(4,1)S(1)}, s32[]{:S(2)}) async-start(s8[4718592]{0:T(1024)(128)(4,1)} %bitcast.5), calls=%async_computation.3 | async-start | bytes 1048576

commit v3 on v2

--- a/solution.py
+++ b/solution.py
@@ -73,20 +73,40 @@
     )(me, a, b, *after)
 
 
-def load_kernel(place, v, a, after, v_own, v_other, a_own, a_send, held, sem):
+def send_half_kernel(place, w, after, out, held, sem):
+    width = out.shape[1]
+    rows = held.shape[1]
+    other = pl.ds(pl.multiple_of((1 - place[1]) * width, HD), width)
+    through([(w.at[pl.ds(i * rows, rows), other], i, out.at[pl.ds(i * rows, rows)]) for i in range(4)], held, sem)
+
+
+def half_to_send(place, w, after):
+    rows, width = w.shape[0], w.shape[1] // 2
+    return pl.pallas_call(
+        send_half_kernel,
+        out_shape=jax.ShapeDtypeStruct((rows, width), BF),
+        in_specs=[SMEM, ANY, ANY],
+        out_specs=ANY,
+        scratch_shapes=[pltpu.VMEM((4, rows // 4, width), BF), pltpu.SemaphoreType.DMA((2, 4))],
+        compiler_params=pltpu.CompilerParams(vmem_limit_bytes=60 * MIB),
+        cost_estimate=cost(4),
+        name="half_to_send",
+    )(place, w, after)
+
+
+def load_kernel(place, v, a, after, v_own, v_other, a_own, token, sem):
     width = v_own.shape[1]
-    rows = held.shape[1]
     own = pl.ds(pl.multiple_of(place[1] * width, HD), width)
     other = pl.ds(pl.multiple_of((1 - place[1]) * width, HD), width)
-    whole = [
-        pltpu.make_async_copy(a.at[:, own], a_own, sem.at[2, 0]),
-        pltpu.make_async_copy(v.at[:, other], v_other, sem.at[2, 1]),
-        pltpu.make_async_copy(v.at[:, own], v_own, sem.at[2, 2]),
+    copies = [
+        pltpu.make_async_copy(v.at[:, other], v_other, sem.at[0]),
+        pltpu.make_async_copy(v.at[:, own], v_own, sem.at[1]),
+        pltpu.make_async_copy(a.at[:, own], a_own, sem.at[2]),
     ]
-    through([(a.at[pl.ds(i * rows, rows), other], i, a_send.at[pl.ds(i * rows, rows)]) for i in range(4)], held, sem)
-    for copy in whole:
-        copy.start()
-    for copy in whole:
+    for copy in copies:
+        copy.start()
+    token[...] = jnp.zeros_like(token)
+    for copy in copies:
         copy.wait()
 
 
@@ -95,17 +115,17 @@
     half = jax.ShapeDtypeStruct((rows, width), BF)
     return pl.pallas_call(
         load_kernel,
-        out_shape=(half,) * 4,
+        out_shape=(half,) * 3 + (jax.ShapeDtypeStruct((8, HD), F32),),
         in_specs=[SMEM, ANY, ANY, ANY],
-        out_specs=(VMEM, VMEM, VMEM, ANY),
-        scratch_shapes=[pltpu.VMEM((4, rows // 4, width), BF), pltpu.SemaphoreType.DMA((3, 4))],
-        compiler_params=pltpu.CompilerParams(vmem_limit_bytes=46 * MIB),
-        cost_estimate=cost(6),
+        out_specs=(VMEM,) * 4,
+        scratch_shapes=[pltpu.SemaphoreType.DMA((3,))],
+        compiler_params=pltpu.CompilerParams(vmem_limit_bytes=44 * MIB),
+        cost_estimate=cost(8),
         name="load_projections",
     )(place, v, a, after)
 
 
-def line_kernel(me, k, v, kv1, kv2, kv3, low, high, held, sem):
+def line_kernel(me, k, v, kv1, kv2, kv3, after, low, high, held, sem):
     y = lax.rem(me[0], LINE)
     cols = group_cols(y)
     copies = [
@@ -128,18 +148,18 @@
         copy.wait()
 
 
-def line_blocks(me, k, v, kv1, kv2, kv3):
+def line_blocks(me, k, v, kv1, kv2, kv3, after):
     half = jax.ShapeDtypeStruct((2, 2, AUD, GW), BF)
     return pl.pallas_call(
         line_kernel,
         out_shape=(half, half),
-        in_specs=[SMEM] + [ANY] * 5,
+        in_specs=[SMEM] + [ANY] * 6,
         out_specs=(ANY, ANY),
         scratch_shapes=[pltpu.VMEM((LINE, 2, AUD, GW), BF), pltpu.SemaphoreType.DMA((5,))],
         compiler_params=pltpu.CompilerParams(vmem_limit_bytes=16 * MIB),
         cost_estimate=TINY,
         name="line_blocks",
-    )(me, k, v, kv1, kv2, kv3)
+    )(me, k, v, kv1, kv2, kv3, after)
 
 
 def attend_kernel(steps, own, carried, last, *refs):
@@ -152,7 +172,7 @@
 
     me, first, count = take(3)
     kvs = [] if carried else take(4)
-    q_own, v_own = take(2) if own else (None, None)
+    q_own, v_own, _, _ = take(4) if own else (None,) * 4
     arrived = take(len(steps) - (1 if own else 0))
     if carried:
         (kbuf,) = take(1)
@@ -180,14 +200,20 @@
     for c in copies:
         c.start()
     for i, part in enumerate(arrived):
-        pltpu.make_async_copy(part, qbuf.at[i], qsem.at[i]).start()
+        pltpu.make_async_copy(part, qbuf.at[i + (1 if own else 0)], qsem.at[i]).start()
     if not carried:
         csum[...] = jnp.full_like(csum, NEG)
     for c in copies:
         c.wait()
 
     def video(i, carry):
-        if not own:
+        if own:
+
+            @pl.when(i > 0)
+            def _():
+                pltpu.make_async_copy(qbuf.at[i], qbuf.at[i], qsem.at[i - 1]).wait()
+
+        else:
             pltpu.make_async_copy(qbuf.at[i], qbuf.at[i], qsem.at[i]).wait()
         step = jnp.int32(steps[0])
         for n in range(1, len(steps)):
@@ -302,7 +328,7 @@
             pltpu.SemaphoreType.DMA((2,)),
         ],
         input_output_aliases={at + 1: n, at + 2: n + 1} if sums else {},
-        compiler_params=pltpu.CompilerParams(vmem_limit_bytes=24 * MIB),
+        compiler_params=pltpu.CompilerParams(vmem_limit_bytes=18 * MIB),
         cost_estimate=cost(6 * n),
         name="attend_last" if last else "attend",
     )(*operands)
@@ -335,7 +361,7 @@
         out_specs=(VMEM,) * LINE,
         name="merge",
         cost_estimate=TINY,
-        compiler_params=pltpu.CompilerParams(vmem_limit_bytes=24 * MIB),
+        compiler_params=pltpu.CompilerParams(vmem_limit_bytes=12 * MIB),
     )(me, u, c, prev, nxt)
 
 
@@ -408,7 +434,7 @@
             pltpu.SemaphoreType.DMA((2, 8)),
         ],
         compiler_params=pltpu.CompilerParams(vmem_limit_bytes=16 * MIB),
-        cost_estimate=cost(1),
+        cost_estimate=cost(0.5),
         name="project_far",
     )(place, piece, w, base, *received, *after)
 
@@ -483,17 +509,18 @@
     kv = [along_line(piece, d + 1) for d, piece in enumerate(kv_out)]
     near1, near3 = pack((1, 3), me_arr, video_query, video_value, kv_out[0])
     qv1, qv3 = along_line(near1, 1), along_line(near3, 3)
-    (far,) = pack((2,), me_arr, video_query, video_value, qv1, qv3, limit=32)
+    a_send = half_to_send(place, audio_proj, near1)
+    a_other = swap(a_send)
+    low, high = line_blocks(me_arr, audio_key, audio_value, *kv, a_send)
+    before, after = across_lines(high, 1), across_lines(low, -1)
+    v_own, v_other, a_own, token = load_projections(place, video_proj, audio_proj, low)
+    (far,) = pack((2,), me_arr, video_query, video_value, low, limit=32)
     qv2 = along_line(far, 2)
-    v_own, v_other, a_own, a_send = load_projections(place, video_proj, audio_proj, kv[0])
-    a_other = swap(a_send)
-    low, high = line_blocks(me_arr, audio_key, audio_value, *kv)
-    before, after = across_lines(high, 1), across_lines(low, -1)
 
     info = (me_arr, pair_first, pair_count)
     kvs = (before, low, high, after)
-    o0, u, c, kv_all = attend((0,), info, kvs, (video_query, video_value), (), (), False)
-    o1, o3, u, c = attend((1, 3), info, (), (), (qv1, qv3), (kv_all, u, c), False)
+    own = (video_query, video_value, far, token)
+    o0, o1, o3, u, c, kv_all = attend((0, 1, 3), info, kvs, own, (qv1, qv3), (), False)
     o2, u, c, to_prev, to_next = attend((2,), info, (), (), (qv2,), (kv_all, u, c), True)
     from_next, from_prev = across_lines(to_prev, -1), across_lines(to_next, 1)
 

time: 117 us -> 113 us (0.966); the launches traced: 118 us -> 113 us
  waiting for transfers between devices: 28.2 us -> 13.6 us
  starting transfers between devices: 34.4 us -> 45.4 us
  Pallas kernels: 54.3 us -> 52.1 us
    ppermute x12, waiting for transfers between devices: 25.2 us -> 12.4 us  [along_line(): lax.ppermute(x, 'seq', [(s, s // LINE * LINE + (s + d) % LINE) for s in r...]
    ppermute x12, starting transfers between devices: 14.6 us -> 21.9 us  [along_line(): lax.ppermute(x, 'seq', [(s, s // LINE * LINE + (s + d) % LINE) for s in r...]
    ppermute x6, starting transfers between devices: 8.77 us -> 12.5 us  [swap(): return lax.ppermute(x, 'head', [(0, 1), (1, 0)])]
    ppermute x4, waiting for transfers between devices: 3.02 us -> 1.17 us  [across_lines(): lax.ppermute(x, 'seq', [(s, (s + d * LINE) % nblocks) for s in range(nblo...]
    pallas_call x1 -> x2, Pallas kernels: 13.3 us -> 12.4 us  [the longest x1 7.86 us: load_projections(): pl.pallas_call(load_kernel, out_shape=(half,) * 3 + (jax.ShapeDtypeStruct...]
    pallas_call x3 -> x2, Pallas kernels: 17.8 us -> 17.2 us  [attend(): pl.pallas_call(functools.partial(attend_kernel, steps, bool(own), bool(su...]
  transfers between devices with their start and end apart: 22 -> 22, of which waited for: 9 -> 4; matrix products, arithmetic and copies ran while one was open for 0% -> 1% of each run, Pallas kernels for 40% -> 40%
where the time goes in v3:
time: 113 us
  Pallas kernels  52.1 us (46%)
  starting transfers between devices  45.4 us (40%)
  waiting for transfers between devices  13.6 us (12%)
    ppermute x12, starting transfers between devices, along_line(): lax.ppermute(x, 'seq', [(s, s // LINE * LINE + (s + d) % LINE) for s in r...  21.9 us
    pallas_call x2, Pallas kernels, attend(): pl.pallas_call(functools.partial(attend_kernel, steps, bool(own), bool(su...  17.2 us
    ppermute x6, starting transfers between devices, swap(): return lax.ppermute(x, 'head', [(0, 1), (1, 0)])  12.5 us
    ppermute x12, waiting for transfers between devices, along_line(): lax.ppermute(x, 'seq', [(s, s // LINE * LINE + (s + d) % LINE) for s in r...  12.4 us
    ppermute x4, starting transfers between devices, across_lines(): lax.ppermute(x, 'seq', [(s, (s + d * LINE) % nblocks) for s in range(nblo...  11 us
    pallas_call x1, Pallas kernels, load_projections(): pl.pallas_call(load_kernel, out_shape=(half,) * 3 + (jax.ShapeDtypeStruct...  7.86 us
    pallas_call x1, Pallas kernels, project_near(): pl.pallas_call(near_kernel, out_shape=(jax.ShapeDtypeStruct((rows, width)...  6.25 us
    pallas_call x2, Pallas kernels, project_far(): pl.pallas_call(functools.partial(far_kernel, 1 + len(received)), out_shap...  5.82 us
  transfers between devices with their start and end apart: 22, of which 4 were waited for; matrix products, arithmetic and copies ran while one was open for 1% of the time, Pallas kernels for 40%

profile of v3, /device:TPU:1, one launch (start us, length us, event | category | flops | bytes accessed | tf_op | source)
XLA Modules:
  0.0 112.9 jit_solution(13189352572621566571)
XLA Ops:
  0.6 2.2 %pack.3 = (bf16[2,256,384]{2,1,0:T(8,128)(2,1)}, bf16[2,256,384]{2,1,0:T(8,128)(2,1)}, bf16[2,256,384]{2,1,0:T(8,128)(2,1)}) custom-call(s32[1]{0:T(128)} %bitcast.2.me.refs_0_, bf16[256,1536]{1,0:T(8,128)(2,1)} %k.1, bf16[256,1536]{1,0:T(8,128)(2,1)} %v.2), custom_call_target="tpu_custom_call" | custom-call | flops 1000000 | bytes 1000 | tf_op jit(solution)/shard_map/pack/pallas_call | solution.py:64
  2.8 2.2 %collective-permute-start = (bf16[2,256,384]{2,1,0:T(8,128)(2,1)}, bf16[2,256,384]{2,1,0:T(8,128)(2,1)S(1)}, u32[]{:S(2)}, u32[]{:S(2)}) collective-permute-start(bf16[2,256,384]{2,1,0:T(8,128)(2,1)} %get-tuple-element.30.refs_0_), channel_id=1, source_target_pairs={{0,2},{2,4},{4,6},{6,0},{8,10},{10,12},{12,14},{14,8},{16,18},{18,... | collective-permute-start | bytes 1179656 | tf_op jit(solution)/shard_map/ppermute | solution.py:498
  5.0 2.6 %collective-permute-start.1 = (bf16[2,256,384]{2,1,0:T(8,128)(2,1)}, bf16[2,256,384]{2,1,0:T(8,128)(2,1)S(1)}, u32[]{:S(2)}, u32[]{:S(2)}) collective-permute-start(bf16[2,256,384]{2,1,0:T(8,128)(2,1)} %get-tuple-element.31), channel_id=1, source_target_pairs={{0,4},{2,6},{4,0},{6,2},{8,12},{10,14},{12,8},{14,10},{16,20},{18,... | collective-permute-start | bytes 1179656 | tf_op jit(solution)/shard_map/ppermute | solution.py:498
  7.6 1.1 collective-permute-start.2
  8.7 2.2 %pack.4 = (bf16[2,512,384]{2,1,0:T(8,128)(2,1)}, bf16[2,512,384]{2,1,0:T(8,128)(2,1)}) custom-call(s32[1]{0:T(128)} %bitcast.2.me.refs_0_, bf16[512,1536]{1,0:T(8,128)(2,1)} %refs_7_.1, bf16[512,1536]{1,0:T(8,128)(2,1)} %refs_8_.1, bf16[2,256,384]{2,1,0:T(8,128)(2,1)} %get-tuple-element.30.refs_0_), custom_call_target="tpu_custom_call" | custom-call | flops 1000000 | bytes 1000 | tf_op jit(solution)/shard_map/pack/pallas_call | solution.py:64
  11.4 2.3 %collective-permute-start.7 = (bf16[2,512,384]{2,1,0:T(8,128)(2,1)}, bf16[2,512,384]{2,1,0:T(8,128)(2,1)}, u32[]{:S(2)}, u32[]{:S(2)}) collective-permute-start(bf16[2,512,384]{2,1,0:T(8,128)(2,1)} %get-tuple-element.37), channel_id=1, source_target_pairs={{0,6},{2,0},{4,2},{6,4},{8,14},{10,8},{12,10},{14,12},{16,22},{18,... | collective-permute-start | bytes 2359304 | tf_op jit(solution)/shard_map/ppermute | solution.py:498
  13.7 0.6 pad_add_fusion.place
  14.3 4.5 %half_to_send.1.after = bf16[1536,1536]{1,0:T(8,128)(2,1)} custom-call(s32[2]{0:T(128)} %pad_add_fusion.place, bf16[1536,3072]{1,0:T(8,128)(2,1)} %a.7, bf16[2,512,384]{2,1,0:T(8,128)(2,1)} %get-tuple-element.33.after), custom_call_target="tpu_custom_call" | custom-call | flops 4000000000 | bytes 1000 | tf_op jit(solution)/shard_map/half_to_send/pallas_call | solution.py:85
  18.9 6.0 %collective-permute-done.1.kv2 = bf16[2,256,384]{2,1,0:T(8,128)(2,1)S(1)} collective-permute-done((bf16[2,256,384]{2,1,0:T(8,128)(2,1)}, bf16[2,256,384]{2,1,0:T(8,128)(2,1)S(1)}, u32[]{:S(2)}, u32[]{:S(2)}) %collective-permute-start.1) | collective-permute-done | bytes 393248 | tf_op jit(solution)/shard_map/ppermute | solution.py:498
  24.8 0.8 line_blocks.1
  25.6 1.7 %collective-permute-start.4 = (bf16[2,2,256,384]{3,2,1,0:T(8,128)(2,1)S(1)}, bf16[2,2,256,384]{3,2,1,0:T(8,128)(2,1)}, u32[]{:S(2)}, u32[]{:S(2)}) collective-permute-start(bf16[2,2,256,384]{3,2,1,0:T(8,128)(2,1)S(1)} %get-tuple-element.35.refs_5_), channel_id=1, source_target_pairs={{0,8},{2,10},{4,12},{6,14},{8,16},{10,18},{12,20},{14,22},{16,24},... | collective-permute-start | bytes 2359304 | tf_op jit(solution)/shard_map/ppermute | solution.py:503
  27.3 4.4 %collective-permute-start.5 = (bf16[2,2,256,384]{3,2,1,0:T(8,128)(2,1)S(1)}, bf16[2,2,256,384]{3,2,1,0:T(8,128)(2,1)}, u32[]{:S(2)}, u32[]{:S(2)}) collective-permute-start(bf16[2,2,256,384]{3,2,1,0:T(8,128)(2,1)S(1)} %get-tuple-element.34.refs_0_.after.refs_4_), channel_id=1, source_target_pairs={{0,120},{2,122},{4,124},{6,126},{8,0},{10,2},{12,4},{14,6},{16,8},... | collective-permute-start | bytes 2359304 | tf_op jit(solution)/shard_map/ppermute | solution.py:503
  31.8 3.0 %collective-permute-start.21 = (bf16[1536,1536]{1,0:T(8,128)(2,1)}, bf16[1536,1536]{1,0:T(8,128)(2,1)S(1)}, u32[]{:S(2)}, u32[]{:S(2)}) collective-permute-start(bf16[1536,1536]{1,0:T(8,128)(2,1)} %half_to_send.1.after), channel_id=1, source_target_pairs={{0,1},{1,0},{2,3},{3,2},{4,5},{5,4},{6,7},{7,6},{8,9},{9,8},{10,11... | collective-permute-start | bytes 14155784 | tf_op jit(solution)/shard_map/ppermute | solution.py:506
  34.7 7.9 %load_projections.1 = (bf16[1536,1536]{1,0:T(8,128)(2,1)S(1)}, bf16[1536,1536]{1,0:T(8,128)(2,1)S(1)}, bf16[1536,1536]{1,0:T(8,128)(2,1)}, f32[8,128]{1,0:T(8,128)S(1)}) custom-call(s32[2]{0:T(128)S(1)} %copy-done.4, bf16[1536,3072]{1,0:T(8,128)(2,1)} %v.3, bf16[1536,3072]{1,0:T(8,128)(2,1)} %a.7, ...), custom_call_target="tpu_custom_call" | custom-call | flops 8000000000 | bytes 1000 | tf_op jit(solution)/shard_map/load_projections/pallas_call | solution.py:116
  43.2 2.6 %collective-permute-start.3 = (bf16[2,512,384]{2,1,0:T(8,128)(2,1)S(1)}, bf16[2,512,384]{2,1,0:T(8,128)(2,1)S(1)}, u32[]{:S(2)}, u32[]{:S(2)}) collective-permute-start(bf16[2,512,384]{2,1,0:T(8,128)(2,1)S(1)} %pack.5.refs_9_), channel_id=1, source_target_pairs={{0,4},{2,6},{4,0},{6,2},{8,12},{10,14},{12,8},{14,10},{16,20},{18,... | collective-permute-start | bytes 2359304 | tf_op jit(solution)/shard_map/ppermute | solution.py:498
  45.8 1.2 %collective-permute-done.4.refs_3_ = bf16[2,2,256,384]{3,2,1,0:T(8,128)(2,1)} collective-permute-done((bf16[2,2,256,384]{3,2,1,0:T(8,128)(2,1)S(1)}, bf16[2,2,256,384]{3,2,1,0:T(8,128)(2,1)}, u32[]{:S(2)}, u32[]{:S(2)}) %collective-permute-start.4) | collective-permute-done | bytes 786464 | tf_op jit(solution)/shard_map/ppermute | solution.py:503
  46.9 12.5 %attend.1 = (bf16[512,384]{1,0:T(8,128)(2,1)S(1)}, bf16[512,384]{1,0:T(8,128)(2,1)S(1)}, bf16[512,384]{1,0:T(8,128)(2,1)S(1)}, f32[3,8,144,256]{3,2,1,0:T(8,128)...) custom-call(s32[1]{0:T(128)} %bitcast.2.me.refs_0_, s32[64]{0:T(128)S(1)} %copy-done.5, ...), custom_call_target="tpu_custom_call" | custom-call | flops 17999998976 | bytes 1000 | tf_op jit(solution)/shard_map/attend/pallas_call | solution.py:314
  59.4 0.8 collective-permute-start.10
  60.2 4.4 %collective-permute-start.9 = (bf16[512,384]{1,0:T(8,128)(2,1)S(1)}, bf16[512,384]{1,0:T(8,128)(2,1)S(1)}, u32[]{:S(2)}, u32[]{:S(2)}) collective-permute-start(bf16[512,384]{1,0:T(8,128)(2,1)S(1)} %get-tuple-element.44), channel_id=1, source_target_pairs={{0,6},{2,0},{4,2},{6,4},{8,14},{10,8},{12,10},{14,12},{16,22},{18,... | collective-permute-start | bytes 1179656 | tf_op jit(solution)/shard_map/ppermute | solution.py:498
  64.6 4.7 %attend_last.1 = (bf16[512,384]{1,0:T(8,128)(2,1)S(1)}, f32[3,8,144,256]{3,2,1,0:T(8,128)S(1)}, f32[3,8,8,256]{3,2,1,0:T(8,128)S(1)}, bf16[2,3,144,256]{3,2,1,0:T(8,128)(2,1)S(1)}, bf16[2,3,144,256]{3,2,1,0:T(8,128)(2,1)S(1)}) custom-call(s32[1]{0:T(128)} %bitcast.2.me.refs_0_, s32[64]{0:T(128)S(1)} %copy-done.5, ...), custom_call_target="tpu_custom_call", output_to_operand_aliasing={{1}: (5, {}), {2}: (6, {})} | custom-call | flops 6000000000 | bytes 1000 | tf_op jit(solution)/shard_map/attend_last/pallas_call | solution.py:314
  69.4 4.8 %collective-permute-start.12 = (bf16[2,3,144,256]{3,2,1,0:T(8,128)(2,1)S(1)}, bf16[2,3,144,256]{3,2,1,0:T(8,128)(2,1)S(1)}, u32[]{:S(2)}, u32[]{:S(2)}) collective-permute-start(bf16[2,3,144,256]{3,2,1,0:T(8,128)(2,1)S(1)} %get-tuple-element.52), channel_id=1, source_target_pairs={{0,120},{2,122},{4,124},{6,126},{8,0},{10,2},{12,4},{14,6},{16,8},... | collective-permute-start | bytes 1327112 | tf_op jit(solution)/shard_map/ppermute | solution.py:503
  74.2 2.4 %collective-permute-start.8 = (bf16[512,384]{1,0:T(8,128)(2,1)S(1)}, bf16[512,384]{1,0:T(8,128)(2,1)S(1)}, u32[]{:S(2)}, u32[]{:S(2)}) collective-permute-start(bf16[512,384]{1,0:T(8,128)(2,1)S(1)} %get-tuple-element.41), channel_id=1, source_target_pairs={{0,4},{2,6},{4,0},{6,2},{8,12},{10,14},{12,8},{14,10},{16,20},{18,... | collective-permute-start | bytes 1179656 | tf_op jit(solution)/shard_map/ppermute | solution.py:498
  76.6 6.3 %project_near.1 = (f32[512,1536]{1,0:T(8,128)S(1)}, f32[512,1536]{1,0:T(8,128)S(1)}) custom-call(s32[2]{0:T(128)S(1)} %copy-done.4, bf16[512,384]{1,0:T(8,128)(2,1)S(1)} %get-tuple-element.43.o0, bf16[512,384]{1,0:T(8,128)(2,1)S(1)} %collective-permute-done.9.o1, bf16[512,384]{1,0:T(8,128)(2,1)S(1)} %collective-permute-done.10.o3, ...), custom_call_target="tpu_custom_call" | custom-call | flops 4000000000 | bytes 1000 | tf_op jit(solution)/shard_map/project_near/pallas_call | solution.py:384
  82.9 0.6 merge.1
  83.5 2.8 %project_far.2 = bf16[512,1536]{1,0:T(8,128)(2,1)S(1)} custom-call(s32[2]{0:T(128)S(1)} %copy-done.4, bf16[512,384]{1,0:T(8,128)(2,1)S(1)} %collective-permute-done.8.piece, bf16[1536,1536]{1,0:T(8,128)(2,1)S(1)} %get-tuple-element.46.w_other.w, f32[512,1536]{1,0:T(8,128)S(1)} %get-tuple-element.48.refs_0_, ...), custom_call_target="tpu_custom_call" | custom-call | flops 500000000 | bytes 1000 | tf_op jit(solution)/shard_map/project_far/pallas_call | solution.py:425
  86.3 3.9 %collective-permute-start.13 = (bf16[512,1536]{1,0:T(8,128)(2,1)S(1)}, bf16[512,1536]{1,0:T(8,128)(2,1)S(1)}, u32[]{:S(2)}, u32[]{:S(2)}) collective-permute-start(bf16[512,1536]{1,0:T(8,128)(2,1)S(1)} %project_far.2), channel_id=1, source_target_pairs={{0,1},{1,0},{2,3},{3,2},{4,5},{5,4},{6,7},{7,6},{8,9},{9,8},{10,11... | collective-permute-start | bytes 4718600 | tf_op jit(solution)/shard_map/ppermute | solution.py:506
  90.3 2.1 %collective-permute-start.14 = (bf16[256,384]{1,0:T(8,128)(2,1)S(1)}, bf16[256,384]{1,0:T(8,128)(2,1)S(1)}, u32[]{:S(2)}, u32[]{:S(2)}) collective-permute-start(bf16[256,384]{1,0:T(8,128)(2,1)S(1)} %get-tuple-element.54), channel_id=1, source_target_pairs={{0,6},{2,0},{4,2},{6,4},{8,14},{10,8},{12,10},{14,12},{16,22},{18,... | collective-permute-start | bytes 589832 | tf_op jit(solution)/shard_map/ppermute | solution.py:498
  93.4 3.6 %collective-permute-done.14.refs_1_ = bf16[256,384]{1,0:T(8,128)(2,1)S(1)} collective-permute-done((bf16[256,384]{1,0:T(8,128)(2,1)S(1)}, bf16[256,384]{1,0:T(8,128)(2,1)S(1)}, u32[]{:S(2)}, u32[]{:S(2)}) %collective-permute-start.14) | collective-permute-done | bytes 196640 | tf_op jit(solution)/shard_map/ppermute | solution.py:498
  97.0 4.8 %collective-permute-start.17 = (bf16[256,384]{1,0:T(8,128)(2,1)S(1)}, bf16[256,384]{1,0:T(8,128)(2,1)S(1)}, u32[]{:S(2)}, u32[]{:S(2)}) collective-permute-start(bf16[256,384]{1,0:T(8,128)(2,1)S(1)} %get-tuple-element.53.refs_1_.refs_0_), channel_id=1, source_target_pairs={{0,1},{1,0},{2,3},{3,2},{4,5},{5,4},{6,7},{7,6},{8,9},{9,8},{10,11... | collective-permute-start | bytes 589832 | tf_op jit(solution)/shard_map/ppermute | solution.py:506
  102.0 2.9 %collective-permute-done.16.refs_3_ = bf16[256,384]{1,0:T(8,128)(2,1)S(1)} collective-permute-done((bf16[256,384]{1,0:T(8,128)(2,1)S(1)}, bf16[256,384]{1,0:T(8,128)(2,1)S(1)}, u32[]{:S(2)}, u32[]{:S(2)}) %collective-permute-start.16) | collective-permute-done | bytes 196640 | tf_op jit(solution)/shard_map/ppermute | solution.py:498
  105.4 3.0 %project_far.3 = bf16[512,1536]{1,0:T(8,128)(2,1)} custom-call(s32[2]{0:T(128)S(1)} %copy-done.4, bf16[512,384]{1,0:T(8,128)(2,1)S(1)} %collective-permute-done.8.piece, bf16[1536,1536]{1,0:T(8,128)(2,1)S(1)} %get-tuple-element.42.w_own.w, f32[512,1536]{1,0:T(8,128)S(1)} %get-tuple-element.47.refs_0_, bf16[512,1536]{1,0:T(8,128)(2,1)S(1)} %collective-permute-done.13.refs_1_), custom_call_target="tpu_custom_call" | custom-call | flops 500000000 | bytes 1000 | tf_op jit(solution)/shard_map/project_far/pallas_call | solution.py:425
  108.5 4.2 %project.1 = bf16[256,1536]{1,0:T(8,128)(2,1)} custom-call(s32[2]{0:T(128)S(1)} %copy-done.4, bf16[256,384]{1,0:T(8,128)(2,1)S(1)} %get-tuple-element.53.refs_1_.refs_0_, bf16[256,384]{1,0:T(8,128)(2,1)S(1)} %collective-permute-done.14.refs_1_, bf16[256,384]{1,0:T(8,128)(2,1)S(1)} %collective-permute-done.15.refs_2_, ...), custom_call_target="tpu_custom_call" | custom-call | flops 4000000000 | bytes 1000 | tf_op jit(solution)/shard_map/project/pallas_call | solution.py:471
  (45 shorter events, 3.0 us)
Async XLA Ops:
  2.8 16.0 %collective-permute-start = (bf16[2,256,384]{2,1,0:T(8,128)(2,1)}, bf16[2,256,384]{2,1,0:T(8,128)(2,1)S(1)}, u32[]{:S(2)}, u32[]{:S(2)}) collective-permute-start(bf16[2,256,384]{2,1,0:T(8,128)(2,1)} %get-tuple-element.30.refs_0_), channel_id=1, source_target_pairs={{0,2},{2,4},{4,6},{6,0},{8,10},{10,12},{12,14},{14,8},{16,18},{18,... | collective-permute-start | bytes 1179656 | tf_op jit(solution)/shard_map/ppermute | solution.py:498
  5.0 19.8 %collective-permute-start.1 = (bf16[2,256,384]{2,1,0:T(8,128)(2,1)}, bf16[2,256,384]{2,1,0:T(8,128)(2,1)S(1)}, u32[]{:S(2)}, u32[]{:S(2)}) collective-permute-start(bf16[2,256,384]{2,1,0:T(8,128)(2,1)} %get-tuple-element.31), channel_id=1, source_target_pairs={{0,4},{2,6},{4,0},{6,2},{8,12},{10,14},{12,8},{14,10},{16,20},{18,... | collective-permute-start | bytes 1179656 | tf_op jit(solution)/shard_map/ppermute | solution.py:498
  7.6 17.2 %collective-permute-start.2 = (bf16[2,256,384]{2,1,0:T(8,128)(2,1)}, bf16[2,256,384]{2,1,0:T(8,128)(2,1)S(1)}, u32[]{:S(2)}, u32[]{:S(2)}) collective-permute-start(bf16[2,256,384]{2,1,0:T(8,128)(2,1)} %get-tuple-element.32), channel_id=1, source_target_pairs={{0,6},{2,0},{4,2},{6,4},{8,14},{10,8},{12,10},{14,12},{16,22},{18,... | collective-permute-start | bytes 1179656 | tf_op jit(solution)/shard_map/ppermute | solution.py:498
  10.9 32.3 %collective-permute-start.6 = (bf16[2,512,384]{2,1,0:T(8,128)(2,1)}, bf16[2,512,384]{2,1,0:T(8,128)(2,1)S(1)}, u32[]{:S(2)}, u32[]{:S(2)}) collective-permute-start(bf16[2,512,384]{2,1,0:T(8,128)(2,1)} %get-tuple-element.33.after), channel_id=1, source_target_pairs={{0,2},{2,4},{4,6},{6,0},{8,10},{10,12},{12,14},{14,8},{16,18},{18,... | collective-permute-start | bytes 2359304 | tf_op jit(solution)/shard_map/ppermute | solution.py:498
  11.4 34.4 %collective-permute-start.7 = (bf16[2,512,384]{2,1,0:T(8,128)(2,1)}, bf16[2,512,384]{2,1,0:T(8,128)(2,1)}, u32[]{:S(2)}, u32[]{:S(2)}) collective-permute-start(bf16[2,512,384]{2,1,0:T(8,128)(2,1)} %get-tuple-element.37), channel_id=1, source_target_pairs={{0,6},{2,0},{4,2},{6,4},{8,14},{10,8},{12,10},{14,12},{16,22},{18,... | collective-permute-start | bytes 2359304 | tf_op jit(solution)/shard_map/ppermute | solution.py:498
  14.3 10.5 %copy-start.2 = (bf16[256,1536]{1,0:T(8,128)(2,1)S(1)}, bf16[256,1536]{1,0:T(8,128)(2,1)}, u32[]{:S(2)}) copy-start(bf16[256,1536]{1,0:T(8,128)(2,1)} %k.1) | copy-start | bytes 2359300
  14.3 10.5 %copy-start.3 = (bf16[256,1536]{1,0:T(8,128)(2,1)S(1)}, bf16[256,1536]{1,0:T(8,128)(2,1)}, u32[]{:S(2)}) copy-start(bf16[256,1536]{1,0:T(8,128)(2,1)} %v.2) | copy-start | bytes 2359300
  18.8 15.9 %copy-start.4 = (s32[2]{0:T(128)S(1)}, s32[2]{0:T(128)}, u32[]{:S(2)}) copy-start(s32[2]{0:T(128)} %pad_add_fusion.place) | copy-start | bytes 28
  25.6 21.3 %collective-permute-start.4 = (bf16[2,2,256,384]{3,2,1,0:T(8,128)(2,1)S(1)}, bf16[2,2,256,384]{3,2,1,0:T(8,128)(2,1)}, u32[]{:S(2)}, u32[]{:S(2)}) collective-permute-start(bf16[2,2,256,384]{3,2,1,0:T(8,128)(2,1)S(1)} %get-tuple-element.35.refs_5_), channel_id=1, source_target_pairs={{0,8},{2,10},{4,12},{6,14},{8,16},{10,18},{12,20},{14,22},{16,24},... | collective-permute-start | bytes 2359304 | tf_op jit(solution)/shard_map/ppermute | solution.py:503
  27.3 15.3 %copy-start = (bf16[512,1536]{1,0:T(8,128)(2,1)S(1)}, bf16[512,1536]{1,0:T(8,128)(2,1)}, u32[]{:S(2)}) copy-start(bf16[512,1536]{1,0:T(8,128)(2,1)} %refs_7_.1) | copy-start | bytes 4718596
  27.3 15.3 %copy-start.1 = (bf16[512,1536]{1,0:T(8,128)(2,1)S(1)}, bf16[512,1536]{1,0:T(8,128)(2,1)}, u32[]{:S(2)}) copy-start(bf16[512,1536]{1,0:T(8,128)(2,1)} %refs_8_.1) | copy-start | bytes 4718596
  27.3 19.6 %collective-permute-start.5 = (bf16[2,2,256,384]{3,2,1,0:T(8,128)(2,1)S(1)}, bf16[2,2,256,384]{3,2,1,0:T(8,128)(2,1)}, u32[]{:S(2)}, u32[]{:S(2)}) collective-permute-start(bf16[2,2,256,384]{3,2,1,0:T(8,128)(2,1)S(1)} %get-tuple-element.34.refs_0_.after.refs_4_), channel_id=1, source_target_pairs={{0,120},{2,122},{4,124},{6,126},{8,0},{10,2},{12,4},{14,6},{16,8},... | collective-permute-start | bytes 2359304 | tf_op jit(solution)/shard_map/ppermute | solution.py:503
  31.8 76.7 %collective-permute-start.21 = (bf16[1536,1536]{1,0:T(8,128)(2,1)}, bf16[1536,1536]{1,0:T(8,128)(2,1)S(1)}, u32[]{:S(2)}, u32[]{:S(2)}) collective-permute-start(bf16[1536,1536]{1,0:T(8,128)(2,1)} %half_to_send.1.after), channel_id=1, source_target_pairs={{0,1},{1,0},{2,3},{3,2},{4,5},{5,4},{6,7},{7,6},{8,9},{9,8},{10,11... | collective-permute-start | bytes 14155784 | tf_op jit(solution)/shard_map/ppermute | solution.py:506
  42.6 4.3 %copy-start.5 = (s32[64]{0:T(128)S(1)}, s32[64]{0:T(128)}, u32[]{:S(2)}) copy-start(s32[64]{0:T(128)} %refs_1_.3) | copy-start | bytes 772
  42.6 4.3 %copy-start.6 = (s32[64]{0:T(128)S(1)}, s32[64]{0:T(128)}, u32[]{:S(2)}) copy-start(s32[64]{0:T(128)} %refs_2_.3) | copy-start | bytes 772
  43.2 21.4 %collective-permute-start.3 = (bf16[2,512,384]{2,1,0:T(8,128)(2,1)S(1)}, bf16[2,512,384]{2,1,0:T(8,128)(2,1)S(1)}, u32[]{:S(2)}, u32[]{:S(2)}) collective-permute-start(bf16[2,512,384]{2,1,0:T(8,128)(2,1)S(1)} %pack.5.refs_9_), channel_id=1, source_target_pairs={{0,4},{2,6},{4,0},{6,2},{8,12},{10,14},{12,8},{14,10},{16,20},{18,... | collective-permute-start | bytes 2359304 | tf_op jit(solution)/shard_map/ppermute | solution.py:498
  59.4 14.8 %collective-permute-start.10 = (bf16[512,384]{1,0:T(8,128)(2,1)S(1)}, bf16[512,384]{1,0:T(8,128)(2,1)S(1)}, u32[]{:S(2)}, u32[]{:S(2)}) collective-permute-start(bf16[512,384]{1,0:T(8,128)(2,1)S(1)} %get-tuple-element.45), channel_id=1, source_target_pairs={{0,2},{2,4},{4,6},{6,0},{8,10},{10,12},{12,14},{14,8},{16,18},{18,... | collective-permute-start | bytes 1179656 | tf_op jit(solution)/shard_map/ppermute | solution.py:498
  60.2 16.4 %collective-permute-start.9 = (bf16[512,384]{1,0:T(8,128)(2,1)S(1)}, bf16[512,384]{1,0:T(8,128)(2,1)S(1)}, u32[]{:S(2)}, u32[]{:S(2)}) collective-permute-start(bf16[512,384]{1,0:T(8,128)(2,1)S(1)} %get-tuple-element.44), channel_id=1, source_target_pairs={{0,6},{2,0},{4,2},{6,4},{8,14},{10,8},{12,10},{14,12},{16,22},{18,... | collective-permute-start | bytes 1179656 | tf_op jit(solution)/shard_map/ppermute | solution.py:498
  69.3 13.5 %collective-permute-start.11 = (bf16[2,3,144,256]{3,2,1,0:T(8,128)(2,1)S(1)}, bf16[2,3,144,256]{3,2,1,0:T(8,128)(2,1)S(1)}, u32[]{:S(2)}, u32[]{:S(2)}) collective-permute-start(bf16[2,3,144,256]{3,2,1,0:T(8,128)(2,1)S(1)} %get-tuple-element.51), channel_id=1, source_target_pairs={{0,8},{2,10},{4,12},{6,14},{8,16},{10,18},{12,20},{14,22},{16,24},... | collective-permute-start | bytes 1327112 | tf_op jit(solution)/shard_map/ppermute | solution.py:503
  69.4 13.4 %collective-permute-start.12 = (bf16[2,3,144,256]{3,2,1,0:T(8,128)(2,1)S(1)}, bf16[2,3,144,256]{3,2,1,0:T(8,128)(2,1)S(1)}, u32[]{:S(2)}, u32[]{:S(2)}) collective-permute-start(bf16[2,3,144,256]{3,2,1,0:T(8,128)(2,1)S(1)} %get-tuple-element.52), channel_id=1, source_target_pairs={{0,120},{2,122},{4,124},{6,126},{8,0},{10,2},{12,4},{14,6},{16,8},... | collective-permute-start | bytes 1327112 | tf_op jit(solution)/shard_map/ppermute | solution.py:503
  74.2 9.3 %collective-permute-start.8 = (bf16[512,384]{1,0:T(8,128)(2,1)S(1)}, bf16[512,384]{1,0:T(8,128)(2,1)S(1)}, u32[]{:S(2)}, u32[]{:S(2)}) collective-permute-start(bf16[512,384]{1,0:T(8,128)(2,1)S(1)} %get-tuple-element.41), channel_id=1, source_target_pairs={{0,4},{2,6},{4,0},{6,2},{8,12},{10,14},{12,8},{14,10},{16,20},{18,... | collective-permute-start | bytes 1179656 | tf_op jit(solution)/shard_map/ppermute | solution.py:498
  83.5 25.0 %slice-start = ((s8[4718592]{0:T(1024)(128)(4,1)}), s8[4194304]{0:T(1024)(128)(4,1)S(1)}, s32[]{:S(2)}) async-start(s8[4718592]{0:T(1024)(128)(4,1)} %bitcast.3), calls=%async_computation | async-start | bytes 8388608
  86.3 19.1 %collective-permute-start.13 = (bf16[512,1536]{1,0:T(8,128)(2,1)S(1)}, bf16[512,1536]{1,0:T(8,128)(2,1)S(1)}, u32[]{:S(2)}, u32[]{:S(2)}) collective-permute-start(bf16[512,1536]{1,0:T(8,128)(2,1)S(1)} %project_far.2), channel_id=1, source_target_pairs={{0,1},{1,0},{2,3},{3,2},{4,5},{5,4},{6,7},{7,6},{8,9},{9,8},{10,11... | collective-permute-start | bytes 4718600 | tf_op jit(solution)/shard_map/ppermute | solution.py:506
  90.3 6.7 %collective-permute-start.14 = (bf16[256,384]{1,0:T(8,128)(2,1)S(1)}, bf16[256,384]{1,0:T(8,128)(2,1)S(1)}, u32[]{:S(2)}, u32[]{:S(2)}) collective-permute-start(bf16[256,384]{1,0:T(8,128)(2,1)S(1)} %get-tuple-element.54), channel_id=1, source_target_pairs={{0,6},{2,0},{4,2},{6,4},{8,14},{10,8},{12,10},{14,12},{16,22},{18,... | collective-permute-start | bytes 589832 | tf_op jit(solution)/shard_map/ppermute | solution.py:498
  92.4 9.4 %collective-permute-start.15 = (bf16[256,384]{1,0:T(8,128)(2,1)S(1)}, bf16[256,384]{1,0:T(8,128)(2,1)S(1)}, u32[]{:S(2)}, u32[]{:S(2)}) collective-permute-start(bf16[256,384]{1,0:T(8,128)(2,1)S(1)} %get-tuple-element.55), channel_id=1, source_target_pairs={{0,4},{2,6},{4,0},{6,2},{8,12},{10,14},{12,8},{14,10},{16,20},{18,... | collective-permute-start | bytes 589832 | tf_op jit(solution)/shard_map/ppermute | solution.py:498
  92.9 12.0 %collective-permute-start.16 = (bf16[256,384]{1,0:T(8,128)(2,1)S(1)}, bf16[256,384]{1,0:T(8,128)(2,1)S(1)}, u32[]{:S(2)}, u32[]{:S(2)}) collective-permute-start(bf16[256,384]{1,0:T(8,128)(2,1)S(1)} %get-tuple-element.56), channel_id=1, source_target_pairs={{0,2},{2,4},{4,6},{6,0},{8,10},{10,12},{12,14},{14,8},{16,18},{18,... | collective-permute-start | bytes 589832 | tf_op jit(solution)/shard_map/ppermute | solution.py:498
  97.0 11.5 %collective-permute-start.17 = (bf16[256,384]{1,0:T(8,128)(2,1)S(1)}, bf16[256,384]{1,0:T(8,128)(2,1)S(1)}, u32[]{:S(2)}, u32[]{:S(2)}) collective-permute-start(bf16[256,384]{1,0:T(8,128)(2,1)S(1)} %get-tuple-element.53.refs_1_.refs_0_), channel_id=1, source_target_pairs={{0,1},{1,0},{2,3},{3,2},{4,5},{5,4},{6,7},{7,6},{8,9},{9,8},{10,11... | collective-permute-start | bytes 589832 | tf_op jit(solution)/shard_map/ppermute | solution.py:506
  101.7 6.7 %collective-permute-start.18 = (bf16[256,384]{1,0:T(8,128)(2,1)S(1)}, bf16[256,384]{1,0:T(8,128)(2,1)S(1)}, u32[]{:S(2)}, u32[]{:S(2)}) collective-permute-start(bf16[256,384]{1,0:T(8,128)(2,1)S(1)} %collective-permute-done.14.refs_1_), channel_id=1, source_target_pairs={{0,1},{1,0},{2,3},{3,2},{4,5},{5,4},{6,7},{7,6},{8,9},{9,8},{10,11... | collective-permute-start | bytes 589832 | tf_op jit(solution)/shard_map/ppermute | solution.py:506
  104.9 3.5 %collective-permute-start.19 = (bf16[256,384]{1,0:T(8,128)(2,1)S(1)}, bf16[256,384]{1,0:T(8,128)(2,1)S(1)}, u32[]{:S(2)}, u32[]{:S(2)}) collective-permute-start(bf16[256,384]{1,0:T(8,128)(2,1)S(1)} %collective-permute-done.15.refs_2_), channel_id=1, source_target_pairs={{0,1},{1,0},{2,3},{3,2},{4,5},{5,4},{6,7},{7,6},{8,9},{9,8},{10,11... | collective-permute-start | bytes 589832 | tf_op jit(solution)/shard_map/ppermute | solution.py:506
  105.4 3.0 %collective-permute-start.20 = (bf16[256,384]{1,0:T(8,128)(2,1)S(1)}, bf16[256,384]{1,0:T(8,128)(2,1)S(1)}, u32[]{:S(2)}, u32[]{:S(2)}) collective-permute-start(bf16[256,384]{1,0:T(8,128)(2,1)S(1)} %collective-permute-done.16.refs_3_), channel_id=1, source_target_pairs={{0,1},{1,0},{2,3},{3,2},{4,5},{5,4},{6,7},{7,6},{8,9},{9,8},{10,11... | collective-permute-start | bytes 589832 | tf_op jit(solution)/shard_map/ppermute | solution.py:506
  105.4 3.1 %slice-start.1 = ((s8[4718592]{0:T(1024)(128)(4,1)}), s8[524288]{0:T(1024)(128)(4,1)S(1)}, s32[]{:S(2)}) async-start(s8[4718592]{0:T(1024)(128)(4,1)} %bitcast.3), calls=%async_computation.1 | async-start | bytes 1048576

commit v4 on v3

--- a/solution.py
+++ b/solution.py
@@ -183,7 +183,7 @@
         (kbuf,) = take(1)
     if last:
         before, after = take(2)
-    qbuf, obuf, tbuf, mbuf, cbuf, abuf, vtbuf, sem, qsem = refs
+    qbuf, tbuf, mbuf, cbuf, abuf, vtbuf, sem, qsem = refs
 
     y = lax.rem(me[0], LINE)
     base = me[0] - y
@@ -206,6 +206,9 @@
     for c in copies:
         c.wait()
 
+    diagonal = lax.broadcasted_iota(jnp.int32, (HD, HD), 0) == lax.broadcasted_iota(jnp.int32, (HD, HD), 1)
+    unit = jnp.where(diagonal, 1.0, 0.0).astype(BF)
+
     def video(i, carry):
         if own:
 
@@ -221,8 +224,6 @@
         v = lax.rem(y + LINE - step, LINE)
         lo = first[base + v] - base + 2
         hi = lo + count[base + v]
-        mbuf[...] = jnp.full_like(mbuf, NEG)
-
         def scores(a, carry):
             slot = a - lo
             for h in range(GH):
@@ -232,7 +233,8 @@
                 )
                 t = t * SCALE
                 tbuf[h, slot] = t
-                mbuf[h] = jnp.maximum(mbuf[h], jnp.maximum(t[:, :HD], t[:, HD:]))
+                top = jnp.maximum(t[:, :HD], t[:, HD:])
+                mbuf[h] = jnp.where(slot == 0, top, jnp.maximum(mbuf[h], top))
                 cbuf[h, slot] = jnp.broadcast_to(jnp.max(t, axis=0, keepdims=True), (8, AUD))
             return carry
 
@@ -241,7 +243,10 @@
             cols = slice(h * HD, (h + 1) * HD)
             mbuf[h] = jnp.broadcast_to(jnp.max(mbuf[h], axis=1, keepdims=True), (VID, HD))
             abuf[h] = jnp.zeros((VID, 2 * HD), F32)
-            vtbuf[h, :HD] = qbuf[i, 1, :, cols].T
+            turned = lax.dot_general(
+                unit, qbuf[i, 1, :, cols], (((1,), (1,)), ((), ())), preferred_element_type=F32
+            )
+            vtbuf[h, :HD] = turned.astype(BF)
             vtbuf[h, HD:] = jnp.ones((EXTRA, VID), BF)
 
         def weights(a, carry):
@@ -264,15 +269,17 @@
             return carry
 
         lax.fori_loop(lo, hi, weights, 0)
-        for h in range(GH):
-            obuf[i, :, h * HD : (h + 1) * HD] = (abuf[h, :, :HD] / abuf[h, :, HD:]).astype(BF)
+        for n, out in enumerate(outs):
+
+            @pl.when(i == n)
+            def _():
+                for h in range(GH):
+                    out[:, h * HD : (h + 1) * HD] = (abuf[h, :, :HD] / abuf[h, :, HD:]).astype(BF)
+
         return carry
 
     lax.fori_loop(0, len(steps), video, 0)
 
-    copies = [pltpu.make_async_copy(obuf.at[i], out, sem.at[i]) for i, out in enumerate(outs)]
-    for c in copies:
-        c.start()
     if last:
         row = lax.broadcasted_iota(jnp.int32, (EXTRA, AUD), 0)
         for place, out in ((0, before), (6, after)):
@@ -289,8 +296,6 @@
                     lo = level - hi - mid
                     parts = jnp.where(row == 0, hi, jnp.where(row == 1, mid, jnp.where(row == 2, lo, 0.0)))
                     out[j, h, HD:] = parts.astype(BF)
-    for c in copies:
-        c.wait()
 
 
 def attend(steps, info, kvs, own, arrived, sums, last):
@@ -301,7 +306,7 @@
         jax.ShapeDtypeStruct((GH, n_idx, 8, AUD), F32),
     ]
     out_shape = [jax.ShapeDtypeStruct((VID, GW), BF)] * n + sum_shapes
-    out_specs = [ANY] * n + [VMEM] * 2
+    out_specs = [VMEM] * (n + 2)
     if last:
         out_shape += [jax.ShapeDtypeStruct((2, GH, HD + EXTRA, AUD), BF)] * 2
         out_specs += [VMEM] * 2
@@ -318,7 +323,6 @@
         out_specs=tuple(out_specs),
         scratch_shapes=[
             pltpu.VMEM((n, 2, VID, GW), BF),
-            pltpu.VMEM((n, VID, GW), BF),
             pltpu.VMEM((GH, 5, VID, AUD), F32),
             pltpu.VMEM((GH, VID, HD), F32),
             pltpu.VMEM((GH, 5, 8, AUD), F32),
@@ -395,25 +399,21 @@
 
 def far_kernel(n_add, place, piece, w, *refs):
     adds = refs[:n_add]
-    out, held, sums, done, sem = refs[-5:]
+    out, done, sem = refs[-3:]
     base, received = adds[0], adds[1:]
     tiles, _, tile = done.shape
-    copies = [pltpu.make_async_copy(piece, held, sem.at[0, 0])]
-    if received:
-        copies.append(pltpu.make_async_copy(received[0], sums, sem.at[0, 1]))
-    for copy in copies:
-        copy.start()
-    for copy in copies:
-        copy.wait()
     rows = group_cols(lax.rem(place[0] + 2, LINE))
     outs = []
     for n in range(tiles):
         cols = slice(n * tile, (n + 1) * tile)
-        total = base[:, cols] + jnp.dot(held[...], w[rows, cols], preferred_element_type=F32)
+        total = base[:, cols] + jnp.dot(piece[...], w[rows, cols], preferred_element_type=F32)
         if received:
-            total += sums[:, cols].astype(F32)
+            total += received[0][:, cols].astype(F32)
+        if not received:
+            out[:, cols] = total.astype(BF)
+            continue
         done[n] = total.astype(BF)
-        outs.append(pltpu.make_async_copy(done.at[n], out.at[:, pl.ds(n * tile, tile)], sem.at[1, n]))
+        outs.append(pltpu.make_async_copy(done.at[n], out.at[:, pl.ds(n * tile, tile)], sem.at[n]))
         outs[-1].start()
     for copy in outs:
         copy.wait()
@@ -425,13 +425,11 @@
     return pl.pallas_call(
         functools.partial(far_kernel, 1 + len(received)),
         out_shape=jax.ShapeDtypeStruct((rows, width), BF),
-        in_specs=[SMEM, ANY, VMEM, VMEM] + [ANY] * (len(received) + len(after)),
-        out_specs=ANY,
+        in_specs=[SMEM, VMEM, VMEM, VMEM] + [VMEM] * len(received) + [ANY] * len(after),
+        out_specs=ANY if received else VMEM,
         scratch_shapes=[
-            pltpu.VMEM((rows, GW), BF),
-            pltpu.VMEM((rows, width), BF),
             pltpu.VMEM((width // tile, rows, tile), BF),
-            pltpu.SemaphoreType.DMA((2, 8)),
+            pltpu.SemaphoreType.DMA((8,)),
         ],
         compiler_params=pltpu.CompilerParams(vmem_limit_bytes=16 * MIB),
         cost_estimate=cost(0.5),

time: 113 us -> 111 us (0.982)
  Pallas kernels: 52.1 us -> 45.5 us
  waiting for transfers between devices: 13.6 us -> 18.7 us
    pallas_call x2, Pallas kernels: 17.2 us -> 12 us  [attend(): pl.pallas_call(functools.partial(attend_kernel, steps, bool(own), bool(su...]
    ppermute x12, waiting for transfers between devices: 12.4 us -> 17.5 us  [along_line(): lax.ppermute(x, 'seq', [(s, s // LINE * LINE + (s + d) % LINE) for s in r...]
    ppermute x4, starting transfers between devices: 11 us -> 14.6 us  [across_lines(): lax.ppermute(x, 'seq', [(s, (s + d * LINE) % nblocks) for s in range(nblo...]
    ppermute x12, starting transfers between devices: 21.9 us -> 19.3 us  [along_line(): lax.ppermute(x, 'seq', [(s, s // LINE * LINE + (s + d) % LINE) for s in r...]
    pallas_call x2, Pallas kernels: 5.82 us -> 4.32 us  [project_far(): pl.pallas_call(functools.partial(far_kernel, 1 + len(received)), out_shap...]
    ppermute x6, starting transfers between devices: 12.5 us -> 11.2 us  [swap(): return lax.ppermute(x, 'head', [(0, 1), (1, 0)])]
  transfers between devices with their start and end apart: 22 -> 22, of which waited for: 4 -> 7; matrix products, arithmetic and copies ran while one was open for 1% -> 1% of each run, Pallas kernels for 40% -> 35%
where the time goes in v4:
time: 111 us
  Pallas kernels  45.5 us (41%)
  starting transfers between devices  45.1 us (41%)
  waiting for transfers between devices  18.7 us (17%)
    ppermute x12, starting transfers between devices, along_line(): lax.ppermute(x, 'seq', [(s, s // LINE * LINE + (s + d) % LINE) for s in r...  19.3 us
    ppermute x12, waiting for transfers between devices, along_line(): lax.ppermute(x, 'seq', [(s, s // LINE * LINE + (s + d) % LINE) for s in r...  17.5 us
    ppermute x4, starting transfers between devices, across_lines(): lax.ppermute(x, 'seq', [(s, (s + d * LINE) % nblocks) for s in range(nblo...  14.6 us
    pallas_call x2, Pallas kernels, attend(): pl.pallas_call(functools.partial(attend_kernel, steps, bool(own), bool(su...  12 us
    ppermute x6, starting transfers between devices, swap(): return lax.ppermute(x, 'head', [(0, 1), (1, 0)])  11.2 us
    pallas_call x1, Pallas kernels, load_projections(): pl.pallas_call(load_kernel, out_shape=(half,) * 3 + (jax.ShapeDtypeStruct...  7.86 us
    pallas_call x1, Pallas kernels, project_near(): pl.pallas_call(near_kernel, out_shape=(jax.ShapeDtypeStruct((rows, width)...  6.26 us
    pallas_call x3, Pallas kernels, pack(): pl.pallas_call(functools.partial(pack_kernel, steps), out_shape=(jax.Shap...  4.88 us
  transfers between devices with their start and end apart: 22, of which 7 were waited for; matrix products, arithmetic and copies ran while one was open for 1% of the time, Pallas kernels for 35%

profile of v4, /device:TPU:1, one launch (start us, length us, event | category | flops | bytes accessed | tf_op | source)
XLA Modules:
  0.0 111.1 jit_solution(10961232764374700629)
XLA Ops:
  0.6 2.2 %pack.3 = (bf16[2,256,384]{2,1,0:T(8,128)(2,1)}, bf16[2,256,384]{2,1,0:T(8,128)(2,1)}, bf16[2,256,384]{2,1,0:T(8,128)(2,1)}) custom-call(s32[1]{0:T(128)} %bitcast.2.me.refs_0_, bf16[256,1536]{1,0:T(8,128)(2,1)} %k.1, bf16[256,1536]{1,0:T(8,128)(2,1)} %v.2), custom_call_target="tpu_custom_call" | custom-call | flops 1000000 | bytes 1000 | tf_op jit(solution)/shard_map/pack/pallas_call | solution.py:64
  2.8 2.2 %collective-permute-start = (bf16[2,256,384]{2,1,0:T(8,128)(2,1)}, bf16[2,256,384]{2,1,0:T(8,128)(2,1)S(1)}, u32[]{:S(2)}, u32[]{:S(2)}) collective-permute-start(bf16[2,256,384]{2,1,0:T(8,128)(2,1)} %get-tuple-element.30.refs_0_), channel_id=1, source_target_pairs={{0,2},{2,4},{4,6},{6,0},{8,10},{10,12},{12,14},{14,8},{16,18},{18,... | collective-permute-start | bytes 1179656 | tf_op jit(solution)/shard_map/ppermute | solution.py:496
  5.0 2.6 %collective-permute-start.1 = (bf16[2,256,384]{2,1,0:T(8,128)(2,1)}, bf16[2,256,384]{2,1,0:T(8,128)(2,1)S(1)}, u32[]{:S(2)}, u32[]{:S(2)}) collective-permute-start(bf16[2,256,384]{2,1,0:T(8,128)(2,1)} %get-tuple-element.31), channel_id=1, source_target_pairs={{0,4},{2,6},{4,0},{6,2},{8,12},{10,14},{12,8},{14,10},{16,20},{18,... | collective-permute-start | bytes 1179656 | tf_op jit(solution)/shard_map/ppermute | solution.py:496
  7.6 1.1 collective-permute-start.2
  8.7 2.2 %pack.4 = (bf16[2,512,384]{2,1,0:T(8,128)(2,1)}, bf16[2,512,384]{2,1,0:T(8,128)(2,1)}) custom-call(s32[1]{0:T(128)} %bitcast.2.me.refs_0_, bf16[512,1536]{1,0:T(8,128)(2,1)} %refs_7_.1, bf16[512,1536]{1,0:T(8,128)(2,1)} %refs_8_.1, bf16[2,256,384]{2,1,0:T(8,128)(2,1)} %get-tuple-element.30.refs_0_), custom_call_target="tpu_custom_call" | custom-call | flops 1000000 | bytes 1000 | tf_op jit(solution)/shard_map/pack/pallas_call | solution.py:64
  11.4 2.3 %collective-permute-start.7 = (bf16[2,512,384]{2,1,0:T(8,128)(2,1)}, bf16[2,512,384]{2,1,0:T(8,128)(2,1)}, u32[]{:S(2)}, u32[]{:S(2)}) collective-permute-start(bf16[2,512,384]{2,1,0:T(8,128)(2,1)} %get-tuple-element.37), channel_id=1, source_target_pairs={{0,6},{2,0},{4,2},{6,4},{8,14},{10,8},{12,10},{14,12},{16,22},{18,... | collective-permute-start | bytes 2359304 | tf_op jit(solution)/shard_map/ppermute | solution.py:496
  14.3 4.5 %half_to_send.1.after = bf16[1536,1536]{1,0:T(8,128)(2,1)} custom-call(s32[2]{0:T(128)} %pad_add_fusion.place, bf16[1536,3072]{1,0:T(8,128)(2,1)} %a.7, bf16[2,512,384]{2,1,0:T(8,128)(2,1)} %get-tuple-element.33.after), custom_call_target="tpu_custom_call" | custom-call | flops 4000000000 | bytes 1000 | tf_op jit(solution)/shard_map/half_to_send/pallas_call | solution.py:85
  18.9 6.0 %collective-permute-done.1.kv2 = bf16[2,256,384]{2,1,0:T(8,128)(2,1)S(1)} collective-permute-done((bf16[2,256,384]{2,1,0:T(8,128)(2,1)}, bf16[2,256,384]{2,1,0:T(8,128)(2,1)S(1)}, u32[]{:S(2)}, u32[]{:S(2)}) %collective-permute-start.1) | collective-permute-done | bytes 393248 | tf_op jit(solution)/shard_map/ppermute | solution.py:496
  25.6 1.7 %collective-permute-start.4 = (bf16[2,2,256,384]{3,2,1,0:T(8,128)(2,1)S(1)}, bf16[2,2,256,384]{3,2,1,0:T(8,128)(2,1)}, u32[]{:S(2)}, u32[]{:S(2)}) collective-permute-start(bf16[2,2,256,384]{3,2,1,0:T(8,128)(2,1)S(1)} %get-tuple-element.35.refs_5_), channel_id=1, source_target_pairs={{0,8},{2,10},{4,12},{6,14},{8,16},{10,18},{12,20},{14,22},{16,24},... | collective-permute-start | bytes 2359304 | tf_op jit(solution)/shard_map/ppermute | solution.py:501
  27.3 4.4 %collective-permute-start.5 = (bf16[2,2,256,384]{3,2,1,0:T(8,128)(2,1)S(1)}, bf16[2,2,256,384]{3,2,1,0:T(8,128)(2,1)}, u32[]{:S(2)}, u32[]{:S(2)}) collective-permute-start(bf16[2,2,256,384]{3,2,1,0:T(8,128)(2,1)S(1)} %get-tuple-element.34.refs_0_.after.refs_4_), channel_id=1, source_target_pairs={{0,120},{2,122},{4,124},{6,126},{8,0},{10,2},{12,4},{14,6},{16,8},... | collective-permute-start | bytes 2359304 | tf_op jit(solution)/shard_map/ppermute | solution.py:501
  31.8 3.0 %collective-permute-start.21 = (bf16[1536,1536]{1,0:T(8,128)(2,1)}, bf16[1536,1536]{1,0:T(8,128)(2,1)S(1)}, u32[]{:S(2)}, u32[]{:S(2)}) collective-permute-start(bf16[1536,1536]{1,0:T(8,128)(2,1)} %half_to_send.1.after), channel_id=1, source_target_pairs={{0,1},{1,0},{2,3},{3,2},{4,5},{5,4},{6,7},{7,6},{8,9},{9,8},{10,11... | collective-permute-start | bytes 14155784 | tf_op jit(solution)/shard_map/ppermute | solution.py:504
  34.7 7.9 %load_projections.1 = (bf16[1536,1536]{1,0:T(8,128)(2,1)S(1)}, bf16[1536,1536]{1,0:T(8,128)(2,1)S(1)}, bf16[1536,1536]{1,0:T(8,128)(2,1)}, f32[8,128]{1,0:T(8,128)S(1)}) custom-call(s32[2]{0:T(128)S(1)} %copy-done.4, bf16[1536,3072]{1,0:T(8,128)(2,1)} %v.3, bf16[1536,3072]{1,0:T(8,128)(2,1)} %a.7, ...), custom_call_target="tpu_custom_call" | custom-call | flops 8000000000 | bytes 1000 | tf_op jit(solution)/shard_map/load_projections/pallas_call | solution.py:116
  43.2 2.6 %collective-permute-start.3 = (bf16[2,512,384]{2,1,0:T(8,128)(2,1)S(1)}, bf16[2,512,384]{2,1,0:T(8,128)(2,1)S(1)}, u32[]{:S(2)}, u32[]{:S(2)}) collective-permute-start(bf16[2,512,384]{2,1,0:T(8,128)(2,1)S(1)} %pack.5.refs_9_), channel_id=1, source_target_pairs={{0,4},{2,6},{4,0},{6,2},{8,12},{10,14},{12,8},{14,10},{16,20},{18,... | collective-permute-start | bytes 2359304 | tf_op jit(solution)/shard_map/ppermute | solution.py:496
  45.8 1.2 %collective-permute-done.4.refs_3_ = bf16[2,2,256,384]{3,2,1,0:T(8,128)(2,1)} collective-permute-done((bf16[2,2,256,384]{3,2,1,0:T(8,128)(2,1)S(1)}, bf16[2,2,256,384]{3,2,1,0:T(8,128)(2,1)}, u32[]{:S(2)}, u32[]{:S(2)}) %collective-permute-start.4) | collective-permute-done | bytes 786464 | tf_op jit(solution)/shard_map/ppermute | solution.py:501
  46.9 9.6 %attend.1 = (bf16[512,384]{1,0:T(8,128)(2,1)S(1)}, bf16[512,384]{1,0:T(8,128)(2,1)S(1)}, bf16[512,384]{1,0:T(8,128)(2,1)S(1)}, f32[3,8,144,256]{3,2,1,0:T(8,128)...) custom-call(s32[1]{0:T(128)} %bitcast.2.me.refs_0_, s32[64]{0:T(128)S(1)} %copy-done.5, ...), custom_call_target="tpu_custom_call" | custom-call | flops 17999998976 | bytes 1000 | tf_op jit(solution)/shard_map/attend/pallas_call | solution.py:319
  56.6 4.1 %collective-permute-start.9 = (bf16[512,384]{1,0:T(8,128)(2,1)S(1)}, bf16[512,384]{1,0:T(8,128)(2,1)S(1)}, u32[]{:S(2)}, u32[]{:S(2)}) collective-permute-start(bf16[512,384]{1,0:T(8,128)(2,1)S(1)} %get-tuple-element.44), channel_id=1, source_target_pairs={{0,6},{2,0},{4,2},{6,4},{8,14},{10,8},{12,10},{14,12},{16,22},{18,... | collective-permute-start | bytes 1179656 | tf_op jit(solution)/shard_map/ppermute | solution.py:496
  60.8 3.2 %collective-permute-done.3.refs_3_ = bf16[2,512,384]{2,1,0:T(8,128)(2,1)S(1)} collective-permute-done((bf16[2,512,384]{2,1,0:T(8,128)(2,1)S(1)}, bf16[2,512,384]{2,1,0:T(8,128)(2,1)S(1)}, u32[]{:S(2)}, u32[]{:S(2)}) %collective-permute-start.3) | collective-permute-done | bytes 786464 | tf_op jit(solution)/shard_map/ppermute | solution.py:496
  64.0 2.4 %attend_last.1 = (bf16[512,384]{1,0:T(8,128)(2,1)S(1)}, f32[3,8,144,256]{3,2,1,0:T(8,128)S(1)}, f32[3,8,8,256]{3,2,1,0:T(8,128)S(1)}, bf16[2,3,144,256]{3,2,1,0:T(8,128)(2,1)S(1)}, bf16[2,3,144,256]{3,2,1,0:T(8,128)(2,1)S(1)}) custom-call(s32[1]{0:T(128)} %bitcast.2.me.refs_0_, s32[64]{0:T(128)S(1)} %copy-done.5, ...), custom_call_target="tpu_custom_call", output_to_operand_aliasing={{1}: (5, {}), {2}: (6, {})} | custom-call | flops 6000000000 | bytes 1000 | tf_op jit(solution)/shard_map/attend_last/pallas_call | solution.py:319
  66.5 8.4 %collective-permute-start.12 = (bf16[2,3,144,256]{3,2,1,0:T(8,128)(2,1)S(1)}, bf16[2,3,144,256]{3,2,1,0:T(8,128)(2,1)S(1)}, u32[]{:S(2)}, u32[]{:S(2)}) collective-permute-start(bf16[2,3,144,256]{3,2,1,0:T(8,128)(2,1)S(1)} %get-tuple-element.52), channel_id=1, source_target_pairs={{0,120},{2,122},{4,124},{6,126},{8,0},{10,2},{12,4},{14,6},{16,8},... | collective-permute-start | bytes 1327112 | tf_op jit(solution)/shard_map/ppermute | solution.py:501
  74.9 1.5 %collective-permute-start.8 = (bf16[512,384]{1,0:T(8,128)(2,1)S(1)}, bf16[512,384]{1,0:T(8,128)(2,1)S(1)}, u32[]{:S(2)}, u32[]{:S(2)}) collective-permute-start(bf16[512,384]{1,0:T(8,128)(2,1)S(1)} %get-tuple-element.41), channel_id=1, source_target_pairs={{0,4},{2,6},{4,0},{6,2},{8,12},{10,14},{12,8},{14,10},{16,20},{18,... | collective-permute-start | bytes 1179656 | tf_op jit(solution)/shard_map/ppermute | solution.py:496
  76.4 6.3 %project_near.1 = (f32[512,1536]{1,0:T(8,128)S(1)}, f32[512,1536]{1,0:T(8,128)S(1)}) custom-call(s32[2]{0:T(128)S(1)} %copy-done.4, bf16[512,384]{1,0:T(8,128)(2,1)S(1)} %get-tuple-element.43.o0, bf16[512,384]{1,0:T(8,128)(2,1)S(1)} %collective-permute-done.9.o1, bf16[512,384]{1,0:T(8,128)(2,1)S(1)} %collective-permute-done.10.o3, ...), custom_call_target="tpu_custom_call" | custom-call | flops 4000000000 | bytes 1000 | tf_op jit(solution)/shard_map/project_near/pallas_call | solution.py:388
  83.8 1.8 %project_far.2 = bf16[512,1536]{1,0:T(8,128)(2,1)S(1)} custom-call(s32[2]{0:T(128)S(1)} %copy-done.4, bf16[512,384]{1,0:T(8,128)(2,1)S(1)} %collective-permute-done.8.piece, bf16[1536,1536]{1,0:T(8,128)(2,1)S(1)} %get-tuple-element.46.w_other.w, f32[512,1536]{1,0:T(8,128)S(1)} %get-tuple-element.48.refs_0_, ...), custom_call_target="tpu_custom_call" | custom-call | flops 500000000 | bytes 1000 | tf_op jit(solution)/shard_map/project_far/pallas_call | solution.py:425
  85.5 4.3 %collective-permute-start.13 = (bf16[512,1536]{1,0:T(8,128)(2,1)S(1)}, bf16[512,1536]{1,0:T(8,128)(2,1)S(1)}, u32[]{:S(2)}, u32[]{:S(2)}) collective-permute-start(bf16[512,1536]{1,0:T(8,128)(2,1)S(1)} %project_far.2), channel_id=1, source_target_pairs={{0,1},{1,0},{2,3},{3,2},{4,5},{5,4},{6,7},{7,6},{8,9},{9,8},{10,11... | collective-permute-start | bytes 4718600 | tf_op jit(solution)/shard_map/ppermute | solution.py:504
  89.8 1.4 %collective-permute-start.14 = (bf16[256,384]{1,0:T(8,128)(2,1)S(1)}, bf16[256,384]{1,0:T(8,128)(2,1)S(1)}, u32[]{:S(2)}, u32[]{:S(2)}) collective-permute-start(bf16[256,384]{1,0:T(8,128)(2,1)S(1)} %get-tuple-element.54), channel_id=1, source_target_pairs={{0,6},{2,0},{4,2},{6,4},{8,14},{10,8},{12,10},{14,12},{16,22},{18,... | collective-permute-start | bytes 589832 | tf_op jit(solution)/shard_map/ppermute | solution.py:496
  91.3 0.9 collective-permute-start.16
  92.2 4.1 %collective-permute-done.14.refs_1_ = bf16[256,384]{1,0:T(8,128)(2,1)S(1)} collective-permute-done((bf16[256,384]{1,0:T(8,128)(2,1)S(1)}, bf16[256,384]{1,0:T(8,128)(2,1)S(1)}, u32[]{:S(2)}, u32[]{:S(2)}) %collective-permute-start.14) | collective-permute-done | bytes 196640 | tf_op jit(solution)/shard_map/ppermute | solution.py:496
  96.3 1.3 %collective-permute-start.17 = (bf16[256,384]{1,0:T(8,128)(2,1)S(1)}, bf16[256,384]{1,0:T(8,128)(2,1)S(1)}, u32[]{:S(2)}, u32[]{:S(2)}) collective-permute-start(bf16[256,384]{1,0:T(8,128)(2,1)S(1)} %get-tuple-element.53.refs_1_.refs_0_), channel_id=1, source_target_pairs={{0,1},{1,0},{2,3},{3,2},{4,5},{5,4},{6,7},{7,6},{8,9},{9,8},{10,11... | collective-permute-start | bytes 589832 | tf_op jit(solution)/shard_map/ppermute | solution.py:504
  97.6 1.3 %collective-permute-done.15.refs_2_ = bf16[256,384]{1,0:T(8,128)(2,1)S(1)} collective-permute-done((bf16[256,384]{1,0:T(8,128)(2,1)S(1)}, bf16[256,384]{1,0:T(8,128)(2,1)S(1)}, u32[]{:S(2)}, u32[]{:S(2)}) %collective-permute-start.15) | collective-permute-done | bytes 196640 | tf_op jit(solution)/shard_map/ppermute | solution.py:496
  98.9 2.0 %collective-permute-start.18 = (bf16[256,384]{1,0:T(8,128)(2,1)S(1)}, bf16[256,384]{1,0:T(8,128)(2,1)S(1)}, u32[]{:S(2)}, u32[]{:S(2)}) collective-permute-start(bf16[256,384]{1,0:T(8,128)(2,1)S(1)} %collective-permute-done.14.refs_1_), channel_id=1, source_target_pairs={{0,1},{1,0},{2,3},{3,2},{4,5},{5,4},{6,7},{7,6},{8,9},{9,8},{10,11... | collective-permute-start | bytes 589832 | tf_op jit(solution)/shard_map/ppermute | solution.py:504
  100.8 2.6 %collective-permute-done.16.refs_3_ = bf16[256,384]{1,0:T(8,128)(2,1)S(1)} collective-permute-done((bf16[256,384]{1,0:T(8,128)(2,1)S(1)}, bf16[256,384]{1,0:T(8,128)(2,1)S(1)}, u32[]{:S(2)}, u32[]{:S(2)}) %collective-permute-start.16) | collective-permute-done | bytes 196640 | tf_op jit(solution)/shard_map/ppermute | solution.py:496
  104.1 2.6 %project_far.3 = bf16[512,1536]{1,0:T(8,128)(2,1)} custom-call(s32[2]{0:T(128)S(1)} %copy-done.4, bf16[512,384]{1,0:T(8,128)(2,1)S(1)} %collective-permute-done.8.piece, bf16[1536,1536]{1,0:T(8,128)(2,1)S(1)} %get-tuple-element.42.w_own.w, f32[512,1536]{1,0:T(8,128)S(1)} %get-tuple-element.47.refs_0_, bf16[512,1536]{1,0:T(8,128)(2,1)S(1)} %collective-permute-done.13.refs_1_), custom_call_target="tpu_custom_call" | custom-call | flops 500000000 | bytes 1000 | tf_op jit(solution)/shard_map/project_far/pallas_call | solution.py:425
  106.7 4.2 %project.1 = bf16[256,1536]{1,0:T(8,128)(2,1)} custom-call(s32[2]{0:T(128)S(1)} %copy-done.4, bf16[256,384]{1,0:T(8,128)(2,1)S(1)} %get-tuple-element.53.refs_1_.refs_0_, bf16[256,384]{1,0:T(8,128)(2,1)S(1)} %collective-permute-done.14.refs_1_, bf16[256,384]{1,0:T(8,128)(2,1)S(1)} %collective-permute-done.15.refs_2_, ...), custom_call_target="tpu_custom_call" | custom-call | flops 4000000000 | bytes 1000 | tf_op jit(solution)/shard_map/project/pallas_call | solution.py:469
  (45 shorter events, 4.5 us)
Async XLA Ops:
  2.8 16.0 %collective-permute-start = (bf16[2,256,384]{2,1,0:T(8,128)(2,1)}, bf16[2,256,384]{2,1,0:T(8,128)(2,1)S(1)}, u32[]{:S(2)}, u32[]{:S(2)}) collective-permute-start(bf16[2,256,384]{2,1,0:T(8,128)(2,1)} %get-tuple-element.30.refs_0_), channel_id=1, source_target_pairs={{0,2},{2,4},{4,6},{6,0},{8,10},{10,12},{12,14},{14,8},{16,18},{18,... | collective-permute-start | bytes 1179656 | tf_op jit(solution)/shard_map/ppermute | solution.py:496
  5.0 19.8 %collective-permute-start.1 = (bf16[2,256,384]{2,1,0:T(8,128)(2,1)}, bf16[2,256,384]{2,1,0:T(8,128)(2,1)S(1)}, u32[]{:S(2)}, u32[]{:S(2)}) collective-permute-start(bf16[2,256,384]{2,1,0:T(8,128)(2,1)} %get-tuple-element.31), channel_id=1, source_target_pairs={{0,4},{2,6},{4,0},{6,2},{8,12},{10,14},{12,8},{14,10},{16,20},{18,... | collective-permute-start | bytes 1179656 | tf_op jit(solution)/shard_map/ppermute | solution.py:496
  7.6 17.2 %collective-permute-start.2 = (bf16[2,256,384]{2,1,0:T(8,128)(2,1)}, bf16[2,256,384]{2,1,0:T(8,128)(2,1)S(1)}, u32[]{:S(2)}, u32[]{:S(2)}) collective-permute-start(bf16[2,256,384]{2,1,0:T(8,128)(2,1)} %get-tuple-element.32), channel_id=1, source_target_pairs={{0,6},{2,0},{4,2},{6,4},{8,14},{10,8},{12,10},{14,12},{16,22},{18,... | collective-permute-start | bytes 1179656 | tf_op jit(solution)/shard_map/ppermute | solution.py:496
  10.9 32.3 %collective-permute-start.6 = (bf16[2,512,384]{2,1,0:T(8,128)(2,1)}, bf16[2,512,384]{2,1,0:T(8,128)(2,1)S(1)}, u32[]{:S(2)}, u32[]{:S(2)}) collective-permute-start(bf16[2,512,384]{2,1,0:T(8,128)(2,1)} %get-tuple-element.33.after), channel_id=1, source_target_pairs={{0,2},{2,4},{4,6},{6,0},{8,10},{10,12},{12,14},{14,8},{16,18},{18,... | collective-permute-start | bytes 2359304 | tf_op jit(solution)/shard_map/ppermute | solution.py:496
  11.4 34.4 %collective-permute-start.7 = (bf16[2,512,384]{2,1,0:T(8,128)(2,1)}, bf16[2,512,384]{2,1,0:T(8,128)(2,1)}, u32[]{:S(2)}, u32[]{:S(2)}) collective-permute-start(bf16[2,512,384]{2,1,0:T(8,128)(2,1)} %get-tuple-element.37), channel_id=1, source_target_pairs={{0,6},{2,0},{4,2},{6,4},{8,14},{10,8},{12,10},{14,12},{16,22},{18,... | collective-permute-start | bytes 2359304 | tf_op jit(solution)/shard_map/ppermute | solution.py:496
  14.3 10.5 %copy-start.2 = (bf16[256,1536]{1,0:T(8,128)(2,1)S(1)}, bf16[256,1536]{1,0:T(8,128)(2,1)}, u32[]{:S(2)}) copy-start(bf16[256,1536]{1,0:T(8,128)(2,1)} %k.1) | copy-start | bytes 2359300
  14.3 10.5 %copy-start.3 = (bf16[256,1536]{1,0:T(8,128)(2,1)S(1)}, bf16[256,1536]{1,0:T(8,128)(2,1)}, u32[]{:S(2)}) copy-start(bf16[256,1536]{1,0:T(8,128)(2,1)} %v.2) | copy-start | bytes 2359300
  18.8 15.9 %copy-start.4 = (s32[2]{0:T(128)S(1)}, s32[2]{0:T(128)}, u32[]{:S(2)}) copy-start(s32[2]{0:T(128)} %pad_add_fusion.place) | copy-start | bytes 28
  25.6 21.3 %collective-permute-start.4 = (bf16[2,2,256,384]{3,2,1,0:T(8,128)(2,1)S(1)}, bf16[2,2,256,384]{3,2,1,0:T(8,128)(2,1)}, u32[]{:S(2)}, u32[]{:S(2)}) collective-permute-start(bf16[2,2,256,384]{3,2,1,0:T(8,128)(2,1)S(1)} %get-tuple-element.35.refs_5_), channel_id=1, source_target_pairs={{0,8},{2,10},{4,12},{6,14},{8,16},{10,18},{12,20},{14,22},{16,24},... | collective-permute-start | bytes 2359304 | tf_op jit(solution)/shard_map/ppermute | solution.py:501
  27.3 15.3 %copy-start = (bf16[512,1536]{1,0:T(8,128)(2,1)S(1)}, bf16[512,1536]{1,0:T(8,128)(2,1)}, u32[]{:S(2)}) copy-start(bf16[512,1536]{1,0:T(8,128)(2,1)} %refs_7_.1) | copy-start | bytes 4718596
  27.3 15.3 %copy-start.1 = (bf16[512,1536]{1,0:T(8,128)(2,1)S(1)}, bf16[512,1536]{1,0:T(8,128)(2,1)}, u32[]{:S(2)}) copy-start(bf16[512,1536]{1,0:T(8,128)(2,1)} %refs_8_.1) | copy-start | bytes 4718596
  27.3 19.6 %collective-permute-start.5 = (bf16[2,2,256,384]{3,2,1,0:T(8,128)(2,1)S(1)}, bf16[2,2,256,384]{3,2,1,0:T(8,128)(2,1)}, u32[]{:S(2)}, u32[]{:S(2)}) collective-permute-start(bf16[2,2,256,384]{3,2,1,0:T(8,128)(2,1)S(1)} %get-tuple-element.34.refs_0_.after.refs_4_), channel_id=1, source_target_pairs={{0,120},{2,122},{4,124},{6,126},{8,0},{10,2},{12,4},{14,6},{16,8},... | collective-permute-start | bytes 2359304 | tf_op jit(solution)/shard_map/ppermute | solution.py:501
  31.8 74.9 %collective-permute-start.21 = (bf16[1536,1536]{1,0:T(8,128)(2,1)}, bf16[1536,1536]{1,0:T(8,128)(2,1)S(1)}, u32[]{:S(2)}, u32[]{:S(2)}) collective-permute-start(bf16[1536,1536]{1,0:T(8,128)(2,1)} %half_to_send.1.after), channel_id=1, source_target_pairs={{0,1},{1,0},{2,3},{3,2},{4,5},{5,4},{6,7},{7,6},{8,9},{9,8},{10,11... | collective-permute-start | bytes 14155784 | tf_op jit(solution)/shard_map/ppermute | solution.py:504
  42.6 4.3 %copy-start.5 = (s32[64]{0:T(128)S(1)}, s32[64]{0:T(128)}, u32[]{:S(2)}) copy-start(s32[64]{0:T(128)} %refs_1_.3) | copy-start | bytes 772
  42.6 4.3 %copy-start.6 = (s32[64]{0:T(128)S(1)}, s32[64]{0:T(128)}, u32[]{:S(2)}) copy-start(s32[64]{0:T(128)} %refs_2_.3) | copy-start | bytes 772
  43.2 20.8 %collective-permute-start.3 = (bf16[2,512,384]{2,1,0:T(8,128)(2,1)S(1)}, bf16[2,512,384]{2,1,0:T(8,128)(2,1)S(1)}, u32[]{:S(2)}, u32[]{:S(2)}) collective-permute-start(bf16[2,512,384]{2,1,0:T(8,128)(2,1)S(1)} %pack.5.refs_9_), channel_id=1, source_target_pairs={{0,4},{2,6},{4,0},{6,2},{8,12},{10,14},{12,8},{14,10},{16,20},{18,... | collective-permute-start | bytes 2359304 | tf_op jit(solution)/shard_map/ppermute | solution.py:496
  56.6 18.4 %collective-permute-start.10 = (bf16[512,384]{1,0:T(8,128)(2,1)S(1)}, bf16[512,384]{1,0:T(8,128)(2,1)S(1)}, u32[]{:S(2)}, u32[]{:S(2)}) collective-permute-start(bf16[512,384]{1,0:T(8,128)(2,1)S(1)} %get-tuple-element.45), channel_id=1, source_target_pairs={{0,2},{2,4},{4,6},{6,0},{8,10},{10,12},{12,14},{14,8},{16,18},{18,... | collective-permute-start | bytes 1179656 | tf_op jit(solution)/shard_map/ppermute | solution.py:496
  56.6 19.8 %collective-permute-start.9 = (bf16[512,384]{1,0:T(8,128)(2,1)S(1)}, bf16[512,384]{1,0:T(8,128)(2,1)S(1)}, u32[]{:S(2)}, u32[]{:S(2)}) collective-permute-start(bf16[512,384]{1,0:T(8,128)(2,1)S(1)} %get-tuple-element.44), channel_id=1, source_target_pairs={{0,6},{2,0},{4,2},{6,4},{8,14},{10,8},{12,10},{14,12},{16,22},{18,... | collective-permute-start | bytes 1179656 | tf_op jit(solution)/shard_map/ppermute | solution.py:496
  66.4 16.3 %collective-permute-start.11 = (bf16[2,3,144,256]{3,2,1,0:T(8,128)(2,1)S(1)}, bf16[2,3,144,256]{3,2,1,0:T(8,128)(2,1)S(1)}, u32[]{:S(2)}, u32[]{:S(2)}) collective-permute-start(bf16[2,3,144,256]{3,2,1,0:T(8,128)(2,1)S(1)} %get-tuple-element.51), channel_id=1, source_target_pairs={{0,8},{2,10},{4,12},{6,14},{8,16},{10,18},{12,20},{14,22},{16,24},... | collective-permute-start | bytes 1327112 | tf_op jit(solution)/shard_map/ppermute | solution.py:501
  66.5 16.2 %collective-permute-start.12 = (bf16[2,3,144,256]{3,2,1,0:T(8,128)(2,1)S(1)}, bf16[2,3,144,256]{3,2,1,0:T(8,128)(2,1)S(1)}, u32[]{:S(2)}, u32[]{:S(2)}) collective-permute-start(bf16[2,3,144,256]{3,2,1,0:T(8,128)(2,1)S(1)} %get-tuple-element.52), channel_id=1, source_target_pairs={{0,120},{2,122},{4,124},{6,126},{8,0},{10,2},{12,4},{14,6},{16,8},... | collective-permute-start | bytes 1327112 | tf_op jit(solution)/shard_map/ppermute | solution.py:501
  74.9 8.9 %collective-permute-start.8 = (bf16[512,384]{1,0:T(8,128)(2,1)S(1)}, bf16[512,384]{1,0:T(8,128)(2,1)S(1)}, u32[]{:S(2)}, u32[]{:S(2)}) collective-permute-start(bf16[512,384]{1,0:T(8,128)(2,1)S(1)} %get-tuple-element.41), channel_id=1, source_target_pairs={{0,4},{2,6},{4,0},{6,2},{8,12},{10,14},{12,8},{14,10},{16,20},{18,... | collective-permute-start | bytes 1179656 | tf_op jit(solution)/shard_map/ppermute | solution.py:496
  83.8 22.9 %slice-start = ((s8[4718592]{0:T(1024)(128)(4,1)}), s8[4194304]{0:T(1024)(128)(4,1)S(1)}, s32[]{:S(2)}) async-start(s8[4718592]{0:T(1024)(128)(4,1)} %bitcast.3), calls=%async_computation | async-start | bytes 8388608
  85.5 18.5 %collective-permute-start.13 = (bf16[512,1536]{1,0:T(8,128)(2,1)S(1)}, bf16[512,1536]{1,0:T(8,128)(2,1)S(1)}, u32[]{:S(2)}, u32[]{:S(2)}) collective-permute-start(bf16[512,1536]{1,0:T(8,128)(2,1)S(1)} %project_far.2), channel_id=1, source_target_pairs={{0,1},{1,0},{2,3},{3,2},{4,5},{5,4},{6,7},{7,6},{8,9},{9,8},{10,11... | collective-permute-start | bytes 4718600 | tf_op jit(solution)/shard_map/ppermute | solution.py:504
  89.8 6.5 %collective-permute-start.14 = (bf16[256,384]{1,0:T(8,128)(2,1)S(1)}, bf16[256,384]{1,0:T(8,128)(2,1)S(1)}, u32[]{:S(2)}, u32[]{:S(2)}) collective-permute-start(bf16[256,384]{1,0:T(8,128)(2,1)S(1)} %get-tuple-element.54), channel_id=1, source_target_pairs={{0,6},{2,0},{4,2},{6,4},{8,14},{10,8},{12,10},{14,12},{16,22},{18,... | collective-permute-start | bytes 589832 | tf_op jit(solution)/shard_map/ppermute | solution.py:496
  91.2 7.7 %collective-permute-start.15 = (bf16[256,384]{1,0:T(8,128)(2,1)S(1)}, bf16[256,384]{1,0:T(8,128)(2,1)S(1)}, u32[]{:S(2)}, u32[]{:S(2)}) collective-permute-start(bf16[256,384]{1,0:T(8,128)(2,1)S(1)} %get-tuple-element.55), channel_id=1, source_target_pairs={{0,4},{2,6},{4,0},{6,2},{8,12},{10,14},{12,8},{14,10},{16,20},{18,... | collective-permute-start | bytes 589832 | tf_op jit(solution)/shard_map/ppermute | solution.py:496
  91.3 12.1 %collective-permute-start.16 = (bf16[256,384]{1,0:T(8,128)(2,1)S(1)}, bf16[256,384]{1,0:T(8,128)(2,1)S(1)}, u32[]{:S(2)}, u32[]{:S(2)}) collective-permute-start(bf16[256,384]{1,0:T(8,128)(2,1)S(1)} %get-tuple-element.56), channel_id=1, source_target_pairs={{0,2},{2,4},{4,6},{6,0},{8,10},{10,12},{12,14},{14,8},{16,18},{18,... | collective-permute-start | bytes 589832 | tf_op jit(solution)/shard_map/ppermute | solution.py:496
  96.3 10.4 %collective-permute-start.17 = (bf16[256,384]{1,0:T(8,128)(2,1)S(1)}, bf16[256,384]{1,0:T(8,128)(2,1)S(1)}, u32[]{:S(2)}, u32[]{:S(2)}) collective-permute-start(bf16[256,384]{1,0:T(8,128)(2,1)S(1)} %get-tuple-element.53.refs_1_.refs_0_), channel_id=1, source_target_pairs={{0,1},{1,0},{2,3},{3,2},{4,5},{5,4},{6,7},{7,6},{8,9},{9,8},{10,11... | collective-permute-start | bytes 589832 | tf_op jit(solution)/shard_map/ppermute | solution.py:504
  98.9 7.8 %collective-permute-start.18 = (bf16[256,384]{1,0:T(8,128)(2,1)S(1)}, bf16[256,384]{1,0:T(8,128)(2,1)S(1)}, u32[]{:S(2)}, u32[]{:S(2)}) collective-permute-start(bf16[256,384]{1,0:T(8,128)(2,1)S(1)} %collective-permute-done.14.refs_1_), channel_id=1, source_target_pairs={{0,1},{1,0},{2,3},{3,2},{4,5},{5,4},{6,7},{7,6},{8,9},{9,8},{10,11... | collective-permute-start | bytes 589832 | tf_op jit(solution)/shard_map/ppermute | solution.py:504
  103.4 3.3 %collective-permute-start.19 = (bf16[256,384]{1,0:T(8,128)(2,1)S(1)}, bf16[256,384]{1,0:T(8,128)(2,1)S(1)}, u32[]{:S(2)}, u32[]{:S(2)}) collective-permute-start(bf16[256,384]{1,0:T(8,128)(2,1)S(1)} %collective-permute-done.15.refs_2_), channel_id=1, source_target_pairs={{0,1},{1,0},{2,3},{3,2},{4,5},{5,4},{6,7},{7,6},{8,9},{9,8},{10,11... | collective-permute-start | bytes 589832 | tf_op jit(solution)/shard_map/ppermute | solution.py:504
  104.1 2.6 %collective-permute-start.20 = (bf16[256,384]{1,0:T(8,128)(2,1)S(1)}, bf16[256,384]{1,0:T(8,128)(2,1)S(1)}, u32[]{:S(2)}, u32[]{:S(2)}) collective-permute-start(bf16[256,384]{1,0:T(8,128)(2,1)S(1)} %collective-permute-done.16.refs_3_), channel_id=1, source_target_pairs={{0,1},{1,0},{2,3},{3,2},{4,5},{5,4},{6,7},{7,6},{8,9},{9,8},{10,11... | collective-permute-start | bytes 589832 | tf_op jit(solution)/shard_map/ppermute | solution.py:504
  104.1 2.6 %slice-start.1 = ((s8[4718592]{0:T(1024)(128)(4,1)}), s8[524288]{0:T(1024)(128)(4,1)S(1)}, s32[]{:S(2)}) async-start(s8[4718592]{0:T(1024)(128)(4,1)} %bitcast.3), calls=%async_computation.1 | async-start | bytes 1048576

commit v5 on v4

--- a/solution.py
+++ b/solution.py
@@ -284,18 +284,19 @@
         row = lax.broadcasted_iota(jnp.int32, (EXTRA, AUD), 0)
         for place, out in ((0, before), (6, after)):
             for j in range(2):
+                levels = jnp.zeros((EXTRA, AUD), F32)
                 for h in range(GH):
                     top = csum[h, place + j, 0:1]
                     some = top > NEG
                     n = jnp.where(some, ubuf[h, place + j, HD : HD + 1], 1.0)
                     u = jnp.where(some, ubuf[h, place + j, :HD], 0.0)
-                    out[j, h, :HD] = (u / n).astype(BF)
+                    out[j, h * HD : (h + 1) * HD] = (u / n).astype(BF)
                     level = jnp.where(some, top + jnp.log2(n), NEG)
                     hi = level.astype(BF).astype(F32)
                     mid = (level - hi).astype(BF).astype(F32)
-                    lo = level - hi - mid
-                    parts = jnp.where(row == 0, hi, jnp.where(row == 1, mid, jnp.where(row == 2, lo, 0.0)))
-                    out[j, h, HD:] = parts.astype(BF)
+                    for k, part in enumerate((hi, mid, level - hi - mid)):
+                        levels = jnp.where(row == 3 * h + k, part, levels)
+                out[j, GW:] = levels.astype(BF)
 
 
 def attend(steps, info, kvs, own, arrived, sums, last):
@@ -308,7 +309,7 @@
     out_shape = [jax.ShapeDtypeStruct((VID, GW), BF)] * n + sum_shapes
     out_specs = [VMEM] * (n + 2)
     if last:
-        out_shape += [jax.ShapeDtypeStruct((2, GH, HD + EXTRA, AUD), BF)] * 2
+        out_shape += [jax.ShapeDtypeStruct((2, GW + EXTRA, AUD), BF)] * 2
         out_specs += [VMEM] * 2
     assert bool(own) != bool(sums)
     operands = [*info, *kvs, *own, *arrived, *sums]
@@ -345,15 +346,17 @@
         for h in range(GH):
             low = j < 2
             at = lax.rem(j, 2)
-            got = jnp.where(low, prev[at, h].astype(F32), nxt[at, h].astype(F32))
-            level = got[HD : HD + 1] + got[HD + 1 : HD + 2] + got[HD + 2 : HD + 3]
+            rows = slice(h * HD, (h + 1) * HD)
+            got = jnp.where(low, prev[at, rows].astype(F32), nxt[at, rows].astype(F32))
+            levels = jnp.where(low, prev[at, GW:].astype(F32), nxt[at, GW:].astype(F32))
+            level = levels[3 * h : 3 * h + 1] + levels[3 * h + 1 : 3 * h + 2] + levels[3 * h + 2 : 3 * h + 3]
             n = u[h, j + 2, HD : HD + 1]
             own = c[h, j + 2, 0:1] + jnp.log2(n)
             top = jnp.maximum(own, level)
             own_w = jnp.exp2(own - top)
             got_w = jnp.exp2(level - top)
             total = own_w + got_w
-            mixed = u[h, j + 2, :HD] * (own_w / (n * total)) + got[:HD] * (got_w / total)
+            mixed = u[h, j + 2, :HD] * (own_w / (n * total)) + got * (got_w / total)
             out[:, h * HD : (h + 1) * HD] = mixed.T.astype(BF)
 
 

time: 111 us -> 110 us (level)
  starting transfers between devices: 45.1 us -> 39 us
  Pallas kernels: 45.5 us -> 50.5 us
    pallas_call x2, Pallas kernels: 12 us -> 17 us  [attend(): pl.pallas_call(functools.partial(attend_kernel, steps, bool(own), bool(su...]
    ppermute x4, starting transfers between devices: 14.6 us -> 11 us  [across_lines(): lax.ppermute(x, 'seq', [(s, (s + d * LINE) % nblocks) for s in range(nblo...]
    ppermute x4, waiting for transfers between devices: 1.17 us -> 3.11 us  [across_lines(): lax.ppermute(x, 'seq', [(s, (s + d * LINE) % nblocks) for s in range(nblo...]
    ppermute x12, waiting for transfers between devices: 17.5 us -> 16 us  [along_line(): lax.ppermute(x, 'seq', [(s, s // LINE * LINE + (s + d) % LINE) for s in r...]
    ppermute x6, starting transfers between devices: 11.2 us -> 9.75 us  [swap(): return lax.ppermute(x, 'head', [(0, 1), (1, 0)])]
  transfers between devices with their start and end apart: 22 -> 22, of which waited for: 7 -> 8; matrix products, arithmetic and copies ran while one was open for 1% -> 1% of each run, Pallas kernels for 35% -> 40%
where the time goes in v5:
time: 110 us
  Pallas kernels  50.5 us (46%)
  starting transfers between devices  39 us (35%)
  waiting for transfers between devices  19.1 us (17%)
    ppermute x12, starting transfers between devices, along_line(): lax.ppermute(x, 'seq', [(s, s // LINE * LINE + (s + d) % LINE) for s in r...  18.3 us
    pallas_call x2, Pallas kernels, attend(): pl.pallas_call(functools.partial(attend_kernel, steps, bool(own), bool(su...  17 us
    ppermute x12, waiting for transfers between devices, along_line(): lax.ppermute(x, 'seq', [(s, s // LINE * LINE + (s + d) % LINE) for s in r...  16 us
    ppermute x4, starting transfers between devices, across_lines(): lax.ppermute(x, 'seq', [(s, (s + d * LINE) % nblocks) for s in range(nblo...  11 us
    ppermute x6, starting transfers between devices, swap(): return lax.ppermute(x, 'head', [(0, 1), (1, 0)])  9.75 us
    pallas_call x1, Pallas kernels, load_projections(): pl.pallas_call(load_kernel, out_shape=(half,) * 3 + (jax.ShapeDtypeStruct...  7.86 us
    pallas_call x1, Pallas kernels, project_near(): pl.pallas_call(near_kernel, out_shape=(jax.ShapeDtypeStruct((rows, width)...  6.26 us
    pallas_call x3, Pallas kernels, pack(): pl.pallas_call(functools.partial(pack_kernel, steps), out_shape=(jax.Shap...  4.88 us
  transfers between devices with their start and end apart: 22, of which 8 were waited for; matrix products, arithmetic and copies ran while one was open for 1% of the time, Pallas kernels for 40%

profile of v5, /device:TPU:1, one launch (start us, length us, event | category | flops | bytes accessed | tf_op | source)
XLA Modules:
  0.0 110.3 jit_solution(14242953285107704157)
XLA Ops:
  0.6 2.2 %pack.3 = (bf16[2,256,384]{2,1,0:T(8,128)(2,1)}, bf16[2,256,384]{2,1,0:T(8,128)(2,1)}, bf16[2,256,384]{2,1,0:T(8,128)(2,1)}) custom-call(s32[1]{0:T(128)} %bitcast.2.me.refs_0_, bf16[256,1536]{1,0:T(8,128)(2,1)} %k.1, bf16[256,1536]{1,0:T(8,128)(2,1)} %v.2), custom_call_target="tpu_custom_call" | custom-call | flops 1000000 | bytes 1000 | tf_op jit(solution)/shard_map/pack/pallas_call | solution.py:64
  2.8 2.2 %collective-permute-start = (bf16[2,256,384]{2,1,0:T(8,128)(2,1)}, bf16[2,256,384]{2,1,0:T(8,128)(2,1)S(1)}, u32[]{:S(2)}, u32[]{:S(2)}) collective-permute-start(bf16[2,256,384]{2,1,0:T(8,128)(2,1)} %get-tuple-element.30.refs_0_), channel_id=1, source_target_pairs={{0,2},{2,4},{4,6},{6,0},{8,10},{10,12},{12,14},{14,8},{16,18},{18,... | collective-permute-start | bytes 1179656 | tf_op jit(solution)/shard_map/ppermute | solution.py:499
  5.0 2.6 %collective-permute-start.1 = (bf16[2,256,384]{2,1,0:T(8,128)(2,1)}, bf16[2,256,384]{2,1,0:T(8,128)(2,1)S(1)}, u32[]{:S(2)}, u32[]{:S(2)}) collective-permute-start(bf16[2,256,384]{2,1,0:T(8,128)(2,1)} %get-tuple-element.31), channel_id=1, source_target_pairs={{0,4},{2,6},{4,0},{6,2},{8,12},{10,14},{12,8},{14,10},{16,20},{18,... | collective-permute-start | bytes 1179656 | tf_op jit(solution)/shard_map/ppermute | solution.py:499
  7.6 1.1 collective-permute-start.2
  8.7 2.2 %pack.4 = (bf16[2,512,384]{2,1,0:T(8,128)(2,1)}, bf16[2,512,384]{2,1,0:T(8,128)(2,1)}) custom-call(s32[1]{0:T(128)} %bitcast.2.me.refs_0_, bf16[512,1536]{1,0:T(8,128)(2,1)} %refs_7_.1, bf16[512,1536]{1,0:T(8,128)(2,1)} %refs_8_.1, bf16[2,256,384]{2,1,0:T(8,128)(2,1)} %get-tuple-element.30.refs_0_), custom_call_target="tpu_custom_call" | custom-call | flops 1000000 | bytes 1000 | tf_op jit(solution)/shard_map/pack/pallas_call | solution.py:64
  11.4 2.3 %collective-permute-start.7 = (bf16[2,512,384]{2,1,0:T(8,128)(2,1)}, bf16[2,512,384]{2,1,0:T(8,128)(2,1)}, u32[]{:S(2)}, u32[]{:S(2)}) collective-permute-start(bf16[2,512,384]{2,1,0:T(8,128)(2,1)} %get-tuple-element.37), channel_id=1, source_target_pairs={{0,6},{2,0},{4,2},{6,4},{8,14},{10,8},{12,10},{14,12},{16,22},{18,... | collective-permute-start | bytes 2359304 | tf_op jit(solution)/shard_map/ppermute | solution.py:499
  14.3 4.5 %half_to_send.1.after = bf16[1536,1536]{1,0:T(8,128)(2,1)} custom-call(s32[2]{0:T(128)} %pad_add_fusion.place, bf16[1536,3072]{1,0:T(8,128)(2,1)} %a.7, bf16[2,512,384]{2,1,0:T(8,128)(2,1)} %get-tuple-element.33.after), custom_call_target="tpu_custom_call" | custom-call | flops 4000000000 | bytes 1000 | tf_op jit(solution)/shard_map/half_to_send/pallas_call | solution.py:85
  18.9 6.0 %collective-permute-done.1.kv2 = bf16[2,256,384]{2,1,0:T(8,128)(2,1)S(1)} collective-permute-done((bf16[2,256,384]{2,1,0:T(8,128)(2,1)}, bf16[2,256,384]{2,1,0:T(8,128)(2,1)S(1)}, u32[]{:S(2)}, u32[]{:S(2)}) %collective-permute-start.1) | collective-permute-done | bytes 393248 | tf_op jit(solution)/shard_map/ppermute | solution.py:499
  25.6 1.7 %collective-permute-start.4 = (bf16[2,2,256,384]{3,2,1,0:T(8,128)(2,1)S(1)}, bf16[2,2,256,384]{3,2,1,0:T(8,128)(2,1)}, u32[]{:S(2)}, u32[]{:S(2)}) collective-permute-start(bf16[2,2,256,384]{3,2,1,0:T(8,128)(2,1)S(1)} %get-tuple-element.35.refs_5_), channel_id=1, source_target_pairs={{0,8},{2,10},{4,12},{6,14},{8,16},{10,18},{12,20},{14,22},{16,24},... | collective-permute-start | bytes 2359304 | tf_op jit(solution)/shard_map/ppermute | solution.py:504
  27.3 4.4 %collective-permute-start.5 = (bf16[2,2,256,384]{3,2,1,0:T(8,128)(2,1)S(1)}, bf16[2,2,256,384]{3,2,1,0:T(8,128)(2,1)}, u32[]{:S(2)}, u32[]{:S(2)}) collective-permute-start(bf16[2,2,256,384]{3,2,1,0:T(8,128)(2,1)S(1)} %get-tuple-element.34.refs_0_.after.refs_4_), channel_id=1, source_target_pairs={{0,120},{2,122},{4,124},{6,126},{8,0},{10,2},{12,4},{14,6},{16,8},... | collective-permute-start | bytes 2359304 | tf_op jit(solution)/shard_map/ppermute | solution.py:504
  31.8 3.0 %collective-permute-start.21 = (bf16[1536,1536]{1,0:T(8,128)(2,1)}, bf16[1536,1536]{1,0:T(8,128)(2,1)S(1)}, u32[]{:S(2)}, u32[]{:S(2)}) collective-permute-start(bf16[1536,1536]{1,0:T(8,128)(2,1)} %half_to_send.1.after), channel_id=1, source_target_pairs={{0,1},{1,0},{2,3},{3,2},{4,5},{5,4},{6,7},{7,6},{8,9},{9,8},{10,11... | collective-permute-start | bytes 14155784 | tf_op jit(solution)/shard_map/ppermute | solution.py:507
  34.7 7.9 %load_projections.1 = (bf16[1536,1536]{1,0:T(8,128)(2,1)S(1)}, bf16[1536,1536]{1,0:T(8,128)(2,1)S(1)}, bf16[1536,1536]{1,0:T(8,128)(2,1)}, f32[8,128]{1,0:T(8,128)S(1)}) custom-call(s32[2]{0:T(128)S(1)} %copy-done.4, bf16[1536,3072]{1,0:T(8,128)(2,1)} %v.3, bf16[1536,3072]{1,0:T(8,128)(2,1)} %a.7, ...), custom_call_target="tpu_custom_call" | custom-call | flops 8000000000 | bytes 1000 | tf_op jit(solution)/shard_map/load_projections/pallas_call | solution.py:116
  43.2 2.6 %collective-permute-start.3 = (bf16[2,512,384]{2,1,0:T(8,128)(2,1)S(1)}, bf16[2,512,384]{2,1,0:T(8,128)(2,1)S(1)}, u32[]{:S(2)}, u32[]{:S(2)}) collective-permute-start(bf16[2,512,384]{2,1,0:T(8,128)(2,1)S(1)} %pack.5.refs_9_), channel_id=1, source_target_pairs={{0,4},{2,6},{4,0},{6,2},{8,12},{10,14},{12,8},{14,10},{16,20},{18,... | collective-permute-start | bytes 2359304 | tf_op jit(solution)/shard_map/ppermute | solution.py:499
  45.8 1.2 %collective-permute-done.4.refs_3_ = bf16[2,2,256,384]{3,2,1,0:T(8,128)(2,1)} collective-permute-done((bf16[2,2,256,384]{3,2,1,0:T(8,128)(2,1)S(1)}, bf16[2,2,256,384]{3,2,1,0:T(8,128)(2,1)}, u32[]{:S(2)}, u32[]{:S(2)}) %collective-permute-start.4) | collective-permute-done | bytes 786464 | tf_op jit(solution)/shard_map/ppermute | solution.py:504
  46.9 11.6 %attend.1 = (bf16[512,384]{1,0:T(8,128)(2,1)S(1)}, bf16[512,384]{1,0:T(8,128)(2,1)S(1)}, bf16[512,384]{1,0:T(8,128)(2,1)S(1)}, f32[3,8,144,256]{3,2,1,0:T(8,128)...) custom-call(s32[1]{0:T(128)} %bitcast.2.me.refs_0_, s32[64]{0:T(128)S(1)} %copy-done.5, ...), custom_call_target="tpu_custom_call" | custom-call | flops 17999998976 | bytes 1000 | tf_op jit(solution)/shard_map/attend/pallas_call | solution.py:320
  58.6 2.8 %collective-permute-start.10 = (bf16[512,384]{1,0:T(8,128)(2,1)S(1)}, bf16[512,384]{1,0:T(8,128)(2,1)S(1)}, u32[]{:S(2)}, u32[]{:S(2)}) collective-permute-start(bf16[512,384]{1,0:T(8,128)(2,1)S(1)} %get-tuple-element.45), channel_id=1, source_target_pairs={{0,2},{2,4},{4,6},{6,0},{8,10},{10,12},{12,14},{14,8},{16,18},{18,... | collective-permute-start | bytes 1179656 | tf_op jit(solution)/shard_map/ppermute | solution.py:499
  61.4 2.4 %collective-permute-start.9 = (bf16[512,384]{1,0:T(8,128)(2,1)S(1)}, bf16[512,384]{1,0:T(8,128)(2,1)S(1)}, u32[]{:S(2)}, u32[]{:S(2)}) collective-permute-start(bf16[512,384]{1,0:T(8,128)(2,1)S(1)} %get-tuple-element.44), channel_id=1, source_target_pairs={{0,6},{2,0},{4,2},{6,4},{8,14},{10,8},{12,10},{14,12},{16,22},{18,... | collective-permute-start | bytes 1179656 | tf_op jit(solution)/shard_map/ppermute | solution.py:499
  63.9 5.4 %attend_last.1 = (bf16[512,384]{1,0:T(8,128)(2,1)S(1)}, f32[3,8,144,256]{3,2,1,0:T(8,128)S(1)}, f32[3,8,8,256]{3,2,1,0:T(8,128)S(1)}, bf16[2,400,256]{2,1,0:T(8,128)(2,1)S(1)}, bf16[2,400,256]{2,1,0:T(8,128)(2,1)S(1)}) custom-call(s32[1]{0:T(128)} %bitcast.2.me.refs_0_, s32[64]{0:T(128)S(1)} %copy-done.5, ...), custom_call_target="tpu_custom_call", output_to_operand_aliasing={{1}: (5, {}), {2}: (6, {})} | custom-call | flops 6000000000 | bytes 1000 | tf_op jit(solution)/shard_map/attend_last/pallas_call | solution.py:320
  69.4 4.8 %collective-permute-start.12 = (bf16[2,400,256]{2,1,0:T(8,128)(2,1)S(1)}, bf16[2,400,256]{2,1,0:T(8,128)(2,1)S(1)}, u32[]{:S(2)}, u32[]{:S(2)}) collective-permute-start(bf16[2,400,256]{2,1,0:T(8,128)(2,1)S(1)} %get-tuple-element.52), channel_id=1, source_target_pairs={{0,120},{2,122},{4,124},{6,126},{8,0},{10,2},{12,4},{14,6},{16,8},... | collective-permute-start | bytes 1228808 | tf_op jit(solution)/shard_map/ppermute | solution.py:504
  74.2 6.3 %project_near.1 = (f32[512,1536]{1,0:T(8,128)S(1)}, f32[512,1536]{1,0:T(8,128)S(1)}) custom-call(s32[2]{0:T(128)S(1)} %copy-done.4, bf16[512,384]{1,0:T(8,128)(2,1)S(1)} %get-tuple-element.43.o0, bf16[512,384]{1,0:T(8,128)(2,1)S(1)} %collective-permute-done.9.o1, bf16[512,384]{1,0:T(8,128)(2,1)S(1)} %collective-permute-done.10.o3, ...), custom_call_target="tpu_custom_call" | custom-call | flops 4000000000 | bytes 1000 | tf_op jit(solution)/shard_map/project_near/pallas_call | solution.py:391
  80.5 1.9 %collective-permute-done.11.prev = bf16[2,400,256]{2,1,0:T(8,128)(2,1)S(1)} collective-permute-done((bf16[2,400,256]{2,1,0:T(8,128)(2,1)S(1)}, bf16[2,400,256]{2,1,0:T(8,128)(2,1)S(1)}, u32[]{:S(2)}, u32[]{:S(2)}) %collective-permute-start.11) | collective-permute-done | bytes 409632 | tf_op jit(solution)/shard_map/ppermute | solution.py:504
  83.0 1.5 %collective-permute-done.8.piece = bf16[512,384]{1,0:T(8,128)(2,1)S(1)} collective-permute-done((bf16[512,384]{1,0:T(8,128)(2,1)S(1)}, bf16[512,384]{1,0:T(8,128)(2,1)S(1)}, u32[]{:S(2)}, u32[]{:S(2)}) %collective-permute-start.8) | collective-permute-done | bytes 393248 | tf_op jit(solution)/shard_map/ppermute | solution.py:499
  84.5 1.8 %project_far.2 = bf16[512,1536]{1,0:T(8,128)(2,1)S(1)} custom-call(s32[2]{0:T(128)S(1)} %copy-done.4, bf16[512,384]{1,0:T(8,128)(2,1)S(1)} %collective-permute-done.8.piece, bf16[1536,1536]{1,0:T(8,128)(2,1)S(1)} %get-tuple-element.46.w_other.w, f32[512,1536]{1,0:T(8,128)S(1)} %get-tuple-element.48.refs_0_, ...), custom_call_target="tpu_custom_call" | custom-call | flops 500000000 | bytes 1000 | tf_op jit(solution)/shard_map/project_far/pallas_call | solution.py:428
  86.2 2.8 %collective-permute-start.13 = (bf16[512,1536]{1,0:T(8,128)(2,1)S(1)}, bf16[512,1536]{1,0:T(8,128)(2,1)S(1)}, u32[]{:S(2)}, u32[]{:S(2)}) collective-permute-start(bf16[512,1536]{1,0:T(8,128)(2,1)S(1)} %project_far.2), channel_id=1, source_target_pairs={{0,1},{1,0},{2,3},{3,2},{4,5},{5,4},{6,7},{7,6},{8,9},{9,8},{10,11... | collective-permute-start | bytes 4718600 | tf_op jit(solution)/shard_map/ppermute | solution.py:507
  89.1 1.3 %collective-permute-start.14 = (bf16[256,384]{1,0:T(8,128)(2,1)S(1)}, bf16[256,384]{1,0:T(8,128)(2,1)S(1)}, u32[]{:S(2)}, u32[]{:S(2)}) collective-permute-start(bf16[256,384]{1,0:T(8,128)(2,1)S(1)} %get-tuple-element.54), channel_id=1, source_target_pairs={{0,6},{2,0},{4,2},{6,4},{8,14},{10,8},{12,10},{14,12},{16,22},{18,... | collective-permute-start | bytes 589832 | tf_op jit(solution)/shard_map/ppermute | solution.py:499
  90.9 4.6 %collective-permute-done.14.refs_1_ = bf16[256,384]{1,0:T(8,128)(2,1)S(1)} collective-permute-done((bf16[256,384]{1,0:T(8,128)(2,1)S(1)}, bf16[256,384]{1,0:T(8,128)(2,1)S(1)}, u32[]{:S(2)}, u32[]{:S(2)}) %collective-permute-start.14) | collective-permute-done | bytes 196640 | tf_op jit(solution)/shard_map/ppermute | solution.py:499
  95.5 1.3 %collective-permute-start.17 = (bf16[256,384]{1,0:T(8,128)(2,1)S(1)}, bf16[256,384]{1,0:T(8,128)(2,1)S(1)}, u32[]{:S(2)}, u32[]{:S(2)}) collective-permute-start(bf16[256,384]{1,0:T(8,128)(2,1)S(1)} %get-tuple-element.53.refs_1_.refs_0_), channel_id=1, source_target_pairs={{0,1},{1,0},{2,3},{3,2},{4,5},{5,4},{6,7},{7,6},{8,9},{9,8},{10,11... | collective-permute-start | bytes 589832 | tf_op jit(solution)/shard_map/ppermute | solution.py:507
  96.9 1.2 %collective-permute-done.15.refs_2_ = bf16[256,384]{1,0:T(8,128)(2,1)S(1)} collective-permute-done((bf16[256,384]{1,0:T(8,128)(2,1)S(1)}, bf16[256,384]{1,0:T(8,128)(2,1)S(1)}, u32[]{:S(2)}, u32[]{:S(2)}) %collective-permute-start.15) | collective-permute-done | bytes 196640 | tf_op jit(solution)/shard_map/ppermute | solution.py:499
  98.0 2.0 %collective-permute-start.18 = (bf16[256,384]{1,0:T(8,128)(2,1)S(1)}, bf16[256,384]{1,0:T(8,128)(2,1)S(1)}, u32[]{:S(2)}, u32[]{:S(2)}) collective-permute-start(bf16[256,384]{1,0:T(8,128)(2,1)S(1)} %collective-permute-done.14.refs_1_), channel_id=1, source_target_pairs={{0,1},{1,0},{2,3},{3,2},{4,5},{5,4},{6,7},{7,6},{8,9},{9,8},{10,11... | collective-permute-start | bytes 589832 | tf_op jit(solution)/shard_map/ppermute | solution.py:507
  100.0 2.6 %collective-permute-done.16.refs_3_ = bf16[256,384]{1,0:T(8,128)(2,1)S(1)} collective-permute-done((bf16[256,384]{1,0:T(8,128)(2,1)S(1)}, bf16[256,384]{1,0:T(8,128)(2,1)S(1)}, u32[]{:S(2)}, u32[]{:S(2)}) %collective-permute-start.16) | collective-permute-done | bytes 196640 | tf_op jit(solution)/shard_map/ppermute | solution.py:499
  103.2 2.6 %project_far.3 = bf16[512,1536]{1,0:T(8,128)(2,1)} custom-call(s32[2]{0:T(128)S(1)} %copy-done.4, bf16[512,384]{1,0:T(8,128)(2,1)S(1)} %collective-permute-done.8.piece, bf16[1536,1536]{1,0:T(8,128)(2,1)S(1)} %get-tuple-element.42.w_own.w, f32[512,1536]{1,0:T(8,128)S(1)} %get-tuple-element.47.refs_0_, bf16[512,1536]{1,0:T(8,128)(2,1)S(1)} %collective-permute-done.13.refs_1_), custom_call_target="tpu_custom_call" | custom-call | flops 500000000 | bytes 1000 | tf_op jit(solution)/shard_map/project_far/pallas_call | solution.py:428
  105.9 4.2 %project.1 = bf16[256,1536]{1,0:T(8,128)(2,1)} custom-call(s32[2]{0:T(128)S(1)} %copy-done.4, bf16[256,384]{1,0:T(8,128)(2,1)S(1)} %get-tuple-element.53.refs_1_.refs_0_, bf16[256,384]{1,0:T(8,128)(2,1)S(1)} %collective-permute-done.14.refs_1_, bf16[256,384]{1,0:T(8,128)(2,1)S(1)} %collective-permute-done.15.refs_2_, ...), custom_call_target="tpu_custom_call" | custom-call | flops 4000000000 | bytes 1000 | tf_op jit(solution)/shard_map/project/pallas_call | solution.py:472
  (45 shorter events, 4.5 us)
Async XLA Ops:
  2.8 16.0 %collective-permute-start = (bf16[2,256,384]{2,1,0:T(8,128)(2,1)}, bf16[2,256,384]{2,1,0:T(8,128)(2,1)S(1)}, u32[]{:S(2)}, u32[]{:S(2)}) collective-permute-start(bf16[2,256,384]{2,1,0:T(8,128)(2,1)} %get-tuple-element.30.refs_0_), channel_id=1, source_target_pairs={{0,2},{2,4},{4,6},{6,0},{8,10},{10,12},{12,14},{14,8},{16,18},{18,... | collective-permute-start | bytes 1179656 | tf_op jit(solution)/shard_map/ppermute | solution.py:499
  5.0 19.8 %collective-permute-start.1 = (bf16[2,256,384]{2,1,0:T(8,128)(2,1)}, bf16[2,256,384]{2,1,0:T(8,128)(2,1)S(1)}, u32[]{:S(2)}, u32[]{:S(2)}) collective-permute-start(bf16[2,256,384]{2,1,0:T(8,128)(2,1)} %get-tuple-element.31), channel_id=1, source_target_pairs={{0,4},{2,6},{4,0},{6,2},{8,12},{10,14},{12,8},{14,10},{16,20},{18,... | collective-permute-start | bytes 1179656 | tf_op jit(solution)/shard_map/ppermute | solution.py:499
  7.6 17.2 %collective-permute-start.2 = (bf16[2,256,384]{2,1,0:T(8,128)(2,1)}, bf16[2,256,384]{2,1,0:T(8,128)(2,1)S(1)}, u32[]{:S(2)}, u32[]{:S(2)}) collective-permute-start(bf16[2,256,384]{2,1,0:T(8,128)(2,1)} %get-tuple-element.32), channel_id=1, source_target_pairs={{0,6},{2,0},{4,2},{6,4},{8,14},{10,8},{12,10},{14,12},{16,22},{18,... | collective-permute-start | bytes 1179656 | tf_op jit(solution)/shard_map/ppermute | solution.py:499
  10.9 32.3 %collective-permute-start.6 = (bf16[2,512,384]{2,1,0:T(8,128)(2,1)}, bf16[2,512,384]{2,1,0:T(8,128)(2,1)S(1)}, u32[]{:S(2)}, u32[]{:S(2)}) collective-permute-start(bf16[2,512,384]{2,1,0:T(8,128)(2,1)} %get-tuple-element.33.after), channel_id=1, source_target_pairs={{0,2},{2,4},{4,6},{6,0},{8,10},{10,12},{12,14},{14,8},{16,18},{18,... | collective-permute-start | bytes 2359304 | tf_op jit(solution)/shard_map/ppermute | solution.py:499
  11.4 34.4 %collective-permute-start.7 = (bf16[2,512,384]{2,1,0:T(8,128)(2,1)}, bf16[2,512,384]{2,1,0:T(8,128)(2,1)}, u32[]{:S(2)}, u32[]{:S(2)}) collective-permute-start(bf16[2,512,384]{2,1,0:T(8,128)(2,1)} %get-tuple-element.37), channel_id=1, source_target_pairs={{0,6},{2,0},{4,2},{6,4},{8,14},{10,8},{12,10},{14,12},{16,22},{18,... | collective-permute-start | bytes 2359304 | tf_op jit(solution)/shard_map/ppermute | solution.py:499
  14.3 10.5 %copy-start.2 = (bf16[256,1536]{1,0:T(8,128)(2,1)S(1)}, bf16[256,1536]{1,0:T(8,128)(2,1)}, u32[]{:S(2)}) copy-start(bf16[256,1536]{1,0:T(8,128)(2,1)} %k.1) | copy-start | bytes 2359300
  14.3 10.5 %copy-start.3 = (bf16[256,1536]{1,0:T(8,128)(2,1)S(1)}, bf16[256,1536]{1,0:T(8,128)(2,1)}, u32[]{:S(2)}) copy-start(bf16[256,1536]{1,0:T(8,128)(2,1)} %v.2) | copy-start | bytes 2359300
  18.8 15.9 %copy-start.4 = (s32[2]{0:T(128)S(1)}, s32[2]{0:T(128)}, u32[]{:S(2)}) copy-start(s32[2]{0:T(128)} %pad_add_fusion.place) | copy-start | bytes 28
  25.6 21.3 %collective-permute-start.4 = (bf16[2,2,256,384]{3,2,1,0:T(8,128)(2,1)S(1)}, bf16[2,2,256,384]{3,2,1,0:T(8,128)(2,1)}, u32[]{:S(2)}, u32[]{:S(2)}) collective-permute-start(bf16[2,2,256,384]{3,2,1,0:T(8,128)(2,1)S(1)} %get-tuple-element.35.refs_5_), channel_id=1, source_target_pairs={{0,8},{2,10},{4,12},{6,14},{8,16},{10,18},{12,20},{14,22},{16,24},... | collective-permute-start | bytes 2359304 | tf_op jit(solution)/shard_map/ppermute | solution.py:504
  27.3 15.3 %copy-start = (bf16[512,1536]{1,0:T(8,128)(2,1)S(1)}, bf16[512,1536]{1,0:T(8,128)(2,1)}, u32[]{:S(2)}) copy-start(bf16[512,1536]{1,0:T(8,128)(2,1)} %refs_7_.1) | copy-start | bytes 4718596
  27.3 15.3 %copy-start.1 = (bf16[512,1536]{1,0:T(8,128)(2,1)S(1)}, bf16[512,1536]{1,0:T(8,128)(2,1)}, u32[]{:S(2)}) copy-start(bf16[512,1536]{1,0:T(8,128)(2,1)} %refs_8_.1) | copy-start | bytes 4718596
  27.3 19.6 %collective-permute-start.5 = (bf16[2,2,256,384]{3,2,1,0:T(8,128)(2,1)S(1)}, bf16[2,2,256,384]{3,2,1,0:T(8,128)(2,1)}, u32[]{:S(2)}, u32[]{:S(2)}) collective-permute-start(bf16[2,2,256,384]{3,2,1,0:T(8,128)(2,1)S(1)} %get-tuple-element.34.refs_0_.after.refs_4_), channel_id=1, source_target_pairs={{0,120},{2,122},{4,124},{6,126},{8,0},{10,2},{12,4},{14,6},{16,8},... | collective-permute-start | bytes 2359304 | tf_op jit(solution)/shard_map/ppermute | solution.py:504
  31.8 74.1 %collective-permute-start.21 = (bf16[1536,1536]{1,0:T(8,128)(2,1)}, bf16[1536,1536]{1,0:T(8,128)(2,1)S(1)}, u32[]{:S(2)}, u32[]{:S(2)}) collective-permute-start(bf16[1536,1536]{1,0:T(8,128)(2,1)} %half_to_send.1.after), channel_id=1, source_target_pairs={{0,1},{1,0},{2,3},{3,2},{4,5},{5,4},{6,7},{7,6},{8,9},{9,8},{10,11... | collective-permute-start | bytes 14155784 | tf_op jit(solution)/shard_map/ppermute | solution.py:507
  42.6 4.3 %copy-start.5 = (s32[64]{0:T(128)S(1)}, s32[64]{0:T(128)}, u32[]{:S(2)}) copy-start(s32[64]{0:T(128)} %refs_1_.3) | copy-start | bytes 772
  42.6 4.3 %copy-start.6 = (s32[64]{0:T(128)S(1)}, s32[64]{0:T(128)}, u32[]{:S(2)}) copy-start(s32[64]{0:T(128)} %refs_2_.3) | copy-start | bytes 772
  43.2 20.8 %collective-permute-start.3 = (bf16[2,512,384]{2,1,0:T(8,128)(2,1)S(1)}, bf16[2,512,384]{2,1,0:T(8,128)(2,1)S(1)}, u32[]{:S(2)}, u32[]{:S(2)}) collective-permute-start(bf16[2,512,384]{2,1,0:T(8,128)(2,1)S(1)} %pack.5.refs_9_), channel_id=1, source_target_pairs={{0,4},{2,6},{4,0},{6,2},{8,12},{10,14},{12,8},{14,10},{16,20},{18,... | collective-permute-start | bytes 2359304 | tf_op jit(solution)/shard_map/ppermute | solution.py:499
  58.6 15.6 %collective-permute-start.10 = (bf16[512,384]{1,0:T(8,128)(2,1)S(1)}, bf16[512,384]{1,0:T(8,128)(2,1)S(1)}, u32[]{:S(2)}, u32[]{:S(2)}) collective-permute-start(bf16[512,384]{1,0:T(8,128)(2,1)S(1)} %get-tuple-element.45), channel_id=1, source_target_pairs={{0,2},{2,4},{4,6},{6,0},{8,10},{10,12},{12,14},{14,8},{16,18},{18,... | collective-permute-start | bytes 1179656 | tf_op jit(solution)/shard_map/ppermute | solution.py:499
  61.4 12.8 %collective-permute-start.9 = (bf16[512,384]{1,0:T(8,128)(2,1)S(1)}, bf16[512,384]{1,0:T(8,128)(2,1)S(1)}, u32[]{:S(2)}, u32[]{:S(2)}) collective-permute-start(bf16[512,384]{1,0:T(8,128)(2,1)S(1)} %get-tuple-element.44), channel_id=1, source_target_pairs={{0,6},{2,0},{4,2},{6,4},{8,14},{10,8},{12,10},{14,12},{16,22},{18,... | collective-permute-start | bytes 1179656 | tf_op jit(solution)/shard_map/ppermute | solution.py:499
  69.3 13.1 %collective-permute-start.11 = (bf16[2,400,256]{2,1,0:T(8,128)(2,1)S(1)}, bf16[2,400,256]{2,1,0:T(8,128)(2,1)S(1)}, u32[]{:S(2)}, u32[]{:S(2)}) collective-permute-start(bf16[2,400,256]{2,1,0:T(8,128)(2,1)S(1)} %get-tuple-element.51), channel_id=1, source_target_pairs={{0,8},{2,10},{4,12},{6,14},{8,16},{10,18},{12,20},{14,22},{16,24},... | collective-permute-start | bytes 1228808 | tf_op jit(solution)/shard_map/ppermute | solution.py:504
  69.4 13.0 %collective-permute-start.12 = (bf16[2,400,256]{2,1,0:T(8,128)(2,1)S(1)}, bf16[2,400,256]{2,1,0:T(8,128)(2,1)S(1)}, u32[]{:S(2)}, u32[]{:S(2)}) collective-permute-start(bf16[2,400,256]{2,1,0:T(8,128)(2,1)S(1)} %get-tuple-element.52), channel_id=1, source_target_pairs={{0,120},{2,122},{4,124},{6,126},{8,0},{10,2},{12,4},{14,6},{16,8},... | collective-permute-start | bytes 1228808 | tf_op jit(solution)/shard_map/ppermute | solution.py:504
  74.2 10.3 %collective-permute-start.8 = (bf16[512,384]{1,0:T(8,128)(2,1)S(1)}, bf16[512,384]{1,0:T(8,128)(2,1)S(1)}, u32[]{:S(2)}, u32[]{:S(2)}) collective-permute-start(bf16[512,384]{1,0:T(8,128)(2,1)S(1)} %get-tuple-element.41), channel_id=1, source_target_pairs={{0,4},{2,6},{4,0},{6,2},{8,12},{10,14},{12,8},{14,10},{16,20},{18,... | collective-permute-start | bytes 1179656 | tf_op jit(solution)/shard_map/ppermute | solution.py:499
  84.5 21.4 %slice-start = ((s8[4718592]{0:T(1024)(128)(4,1)}), s8[4194304]{0:T(1024)(128)(4,1)S(1)}, s32[]{:S(2)}) async-start(s8[4718592]{0:T(1024)(128)(4,1)} %bitcast.3), calls=%async_computation | async-start | bytes 8388608
  86.2 17.0 %collective-permute-start.13 = (bf16[512,1536]{1,0:T(8,128)(2,1)S(1)}, bf16[512,1536]{1,0:T(8,128)(2,1)S(1)}, u32[]{:S(2)}, u32[]{:S(2)}) collective-permute-start(bf16[512,1536]{1,0:T(8,128)(2,1)S(1)} %project_far.2), channel_id=1, source_target_pairs={{0,1},{1,0},{2,3},{3,2},{4,5},{5,4},{6,7},{7,6},{8,9},{9,8},{10,11... | collective-permute-start | bytes 4718600 | tf_op jit(solution)/shard_map/ppermute | solution.py:507
  89.1 6.5 %collective-permute-start.14 = (bf16[256,384]{1,0:T(8,128)(2,1)S(1)}, bf16[256,384]{1,0:T(8,128)(2,1)S(1)}, u32[]{:S(2)}, u32[]{:S(2)}) collective-permute-start(bf16[256,384]{1,0:T(8,128)(2,1)S(1)} %get-tuple-element.54), channel_id=1, source_target_pairs={{0,6},{2,0},{4,2},{6,4},{8,14},{10,8},{12,10},{14,12},{16,22},{18,... | collective-permute-start | bytes 589832 | tf_op jit(solution)/shard_map/ppermute | solution.py:499
  90.3 7.7 %collective-permute-start.15 = (bf16[256,384]{1,0:T(8,128)(2,1)S(1)}, bf16[256,384]{1,0:T(8,128)(2,1)S(1)}, u32[]{:S(2)}, u32[]{:S(2)}) collective-permute-start(bf16[256,384]{1,0:T(8,128)(2,1)S(1)} %get-tuple-element.55), channel_id=1, source_target_pairs={{0,4},{2,6},{4,0},{6,2},{8,12},{10,14},{12,8},{14,10},{16,20},{18,... | collective-permute-start | bytes 589832 | tf_op jit(solution)/shard_map/ppermute | solution.py:499
  90.5 12.1 %collective-permute-start.16 = (bf16[256,384]{1,0:T(8,128)(2,1)S(1)}, bf16[256,384]{1,0:T(8,128)(2,1)S(1)}, u32[]{:S(2)}, u32[]{:S(2)}) collective-permute-start(bf16[256,384]{1,0:T(8,128)(2,1)S(1)} %get-tuple-element.56), channel_id=1, source_target_pairs={{0,2},{2,4},{4,6},{6,0},{8,10},{10,12},{12,14},{14,8},{16,18},{18,... | collective-permute-start | bytes 589832 | tf_op jit(solution)/shard_map/ppermute | solution.py:499
  95.5 10.3 %collective-permute-start.17 = (bf16[256,384]{1,0:T(8,128)(2,1)S(1)}, bf16[256,384]{1,0:T(8,128)(2,1)S(1)}, u32[]{:S(2)}, u32[]{:S(2)}) collective-permute-start(bf16[256,384]{1,0:T(8,128)(2,1)S(1)} %get-tuple-element.53.refs_1_.refs_0_), channel_id=1, source_target_pairs={{0,1},{1,0},{2,3},{3,2},{4,5},{5,4},{6,7},{7,6},{8,9},{9,8},{10,11... | collective-permute-start | bytes 589832 | tf_op jit(solution)/shard_map/ppermute | solution.py:507
  98.0 7.8 %collective-permute-start.18 = (bf16[256,384]{1,0:T(8,128)(2,1)S(1)}, bf16[256,384]{1,0:T(8,128)(2,1)S(1)}, u32[]{:S(2)}, u32[]{:S(2)}) collective-permute-start(bf16[256,384]{1,0:T(8,128)(2,1)S(1)} %collective-permute-done.14.refs_1_), channel_id=1, source_target_pairs={{0,1},{1,0},{2,3},{3,2},{4,5},{5,4},{6,7},{7,6},{8,9},{9,8},{10,11... | collective-permute-start | bytes 589832 | tf_op jit(solution)/shard_map/ppermute | solution.py:507
  102.6 3.3 %collective-permute-start.19 = (bf16[256,384]{1,0:T(8,128)(2,1)S(1)}, bf16[256,384]{1,0:T(8,128)(2,1)S(1)}, u32[]{:S(2)}, u32[]{:S(2)}) collective-permute-start(bf16[256,384]{1,0:T(8,128)(2,1)S(1)} %collective-permute-done.15.refs_2_), channel_id=1, source_target_pairs={{0,1},{1,0},{2,3},{3,2},{4,5},{5,4},{6,7},{7,6},{8,9},{9,8},{10,11... | collective-permute-start | bytes 589832 | tf_op jit(solution)/shard_map/ppermute | solution.py:507
  103.2 2.6 %collective-permute-start.20 = (bf16[256,384]{1,0:T(8,128)(2,1)S(1)}, bf16[256,384]{1,0:T(8,128)(2,1)S(1)}, u32[]{:S(2)}, u32[]{:S(2)}) collective-permute-start(bf16[256,384]{1,0:T(8,128)(2,1)S(1)} %collective-permute-done.16.refs_3_), channel_id=1, source_target_pairs={{0,1},{1,0},{2,3},{3,2},{4,5},{5,4},{6,7},{7,6},{8,9},{9,8},{10,11... | collective-permute-start | bytes 589832 | tf_op jit(solution)/shard_map/ppermute | solution.py:507
  103.2 2.6 %slice-start.1 = ((s8[4718592]{0:T(1024)(128)(4,1)}), s8[524288]{0:T(1024)(128)(4,1)S(1)}, s32[]{:S(2)}) async-start(s8[4718592]{0:T(1024)(128)(4,1)} %bitcast.3), calls=%async_computation.1 | async-start | bytes 1048576

commit v6 on v5

--- a/solution.py
+++ b/solution.py
@@ -424,7 +424,7 @@
 
 def project_far(place, piece, w, base, received=(), after=()):
     rows, width = piece.shape[0], w.shape[1]
-    tile = 384
+    tile = 512
     return pl.pallas_call(
         functools.partial(far_kernel, 1 + len(received)),
         out_shape=jax.ShapeDtypeStruct((rows, width), BF),
@@ -468,7 +468,7 @@
 
 def project(place, mine, theirs, w, w_theirs):
     rows, width = mine[0].shape[0], w.shape[1]
-    tile = 256
+    tile = 512
     return pl.pallas_call(
         project_kernel,
         out_shape=jax.ShapeDtypeStruct((rows, width), BF),

time: 110 us -> 110 us (level)
  the two profiles are of different devices: /device:TPU:1 before, /device:TPU:5 now
where the time goes in v6:
time: 110 us
  Pallas kernels  50.1 us (46%)
  starting transfers between devices  40.1 us (36%)
  waiting for transfers between devices  18.3 us (17%)
    ppermute x12, starting transfers between devices, along_line(): lax.ppermute(x, 'seq', [(s, s // LINE * LINE + (s + d) % LINE) for s in r...  17.2 us
    pallas_call x2, Pallas kernels, attend(): pl.pallas_call(functools.partial(attend_kernel, steps, bool(own), bool(su...  17 us
    ppermute x12, waiting for transfers between devices, along_line(): lax.ppermute(x, 'seq', [(s, s // LINE * LINE + (s + d) % LINE) for s in r...  15.7 us
    ppermute x4, starting transfers between devices, across_lines(): lax.ppermute(x, 'seq', [(s, (s + d * LINE) % nblocks) for s in range(nblo...  13.5 us
    ppermute x6, starting transfers between devices, swap(): return lax.ppermute(x, 'head', [(0, 1), (1, 0)])  9.41 us
    pallas_call x1, Pallas kernels, load_projections(): pl.pallas_call(load_kernel, out_shape=(half,) * 3 + (jax.ShapeDtypeStruct...  7.86 us
    pallas_call x1, Pallas kernels, project_near(): pl.pallas_call(near_kernel, out_shape=(jax.ShapeDtypeStruct((rows, width)...  6.25 us
    pallas_call x3, Pallas kernels, pack(): pl.pallas_call(functools.partial(pack_kernel, steps), out_shape=(jax.Shap...  4.88 us
  transfers between devices with their start and end apart: 22, of which 7 were waited for; matrix products, arithmetic and copies ran while one was open for 1% of the time, Pallas kernels for 40%

profile of v6, /device:TPU:5, one launch (start us, length us, event | category | flops | bytes accessed | tf_op | source)
XLA Modules:
  0.0 110.3 jit_solution(16072736962019866532)
XLA Ops:
  0.6 2.2 %pack.3 = (bf16[2,256,384]{2,1,0:T(8,128)(2,1)}, bf16[2,256,384]{2,1,0:T(8,128)(2,1)}, bf16[2,256,384]{2,1,0:T(8,128)(2,1)}) custom-call(s32[1]{0:T(128)} %bitcast.2.me.refs_0_, bf16[256,1536]{1,0:T(8,128)(2,1)} %k.1, bf16[256,1536]{1,0:T(8,128)(2,1)} %v.2), custom_call_target="tpu_custom_call" | custom-call | flops 1000000 | bytes 1000 | tf_op jit(solution)/shard_map/pack/pallas_call | solution.py:64
  2.8 1.4 %collective-permute-start = (bf16[2,256,384]{2,1,0:T(8,128)(2,1)}, bf16[2,256,384]{2,1,0:T(8,128)(2,1)S(1)}, u32[]{:S(2)}, u32[]{:S(2)}) collective-permute-start(bf16[2,256,384]{2,1,0:T(8,128)(2,1)} %get-tuple-element.30.refs_0_), channel_id=1, source_target_pairs={{0,2},{2,4},{4,6},{6,0},{8,10},{10,12},{12,14},{14,8},{16,18},{18,... | collective-permute-start | bytes 1179656 | tf_op jit(solution)/shard_map/ppermute | solution.py:499
  4.2 2.6 %collective-permute-start.1 = (bf16[2,256,384]{2,1,0:T(8,128)(2,1)}, bf16[2,256,384]{2,1,0:T(8,128)(2,1)S(1)}, u32[]{:S(2)}, u32[]{:S(2)}) collective-permute-start(bf16[2,256,384]{2,1,0:T(8,128)(2,1)} %get-tuple-element.31), channel_id=1, source_target_pairs={{0,4},{2,6},{4,0},{6,2},{8,12},{10,14},{12,8},{14,10},{16,20},{18,... | collective-permute-start | bytes 1179656 | tf_op jit(solution)/shard_map/ppermute | solution.py:499
  6.8 1.1 collective-permute-start.2
  7.9 2.2 %pack.4 = (bf16[2,512,384]{2,1,0:T(8,128)(2,1)}, bf16[2,512,384]{2,1,0:T(8,128)(2,1)}) custom-call(s32[1]{0:T(128)} %bitcast.2.me.refs_0_, bf16[512,1536]{1,0:T(8,128)(2,1)} %refs_7_.1, bf16[512,1536]{1,0:T(8,128)(2,1)} %refs_8_.1, bf16[2,256,384]{2,1,0:T(8,128)(2,1)} %get-tuple-element.30.refs_0_), custom_call_target="tpu_custom_call" | custom-call | flops 1000000 | bytes 1000 | tf_op jit(solution)/shard_map/pack/pallas_call | solution.py:64
  10.5 2.3 %collective-permute-start.7 = (bf16[2,512,384]{2,1,0:T(8,128)(2,1)}, bf16[2,512,384]{2,1,0:T(8,128)(2,1)}, u32[]{:S(2)}, u32[]{:S(2)}) collective-permute-start(bf16[2,512,384]{2,1,0:T(8,128)(2,1)} %get-tuple-element.37), channel_id=1, source_target_pairs={{0,6},{2,0},{4,2},{6,4},{8,14},{10,8},{12,10},{14,12},{16,22},{18,... | collective-permute-start | bytes 2359304 | tf_op jit(solution)/shard_map/ppermute | solution.py:499
  13.5 4.5 %half_to_send.1.after = bf16[1536,1536]{1,0:T(8,128)(2,1)} custom-call(s32[2]{0:T(128)} %pad_add_fusion.place, bf16[1536,3072]{1,0:T(8,128)(2,1)} %a.7, bf16[2,512,384]{2,1,0:T(8,128)(2,1)} %get-tuple-element.33.after), custom_call_target="tpu_custom_call" | custom-call | flops 4000000000 | bytes 1000 | tf_op jit(solution)/shard_map/half_to_send/pallas_call | solution.py:85
  18.0 6.0 %collective-permute-done.1.kv2 = bf16[2,256,384]{2,1,0:T(8,128)(2,1)S(1)} collective-permute-done((bf16[2,256,384]{2,1,0:T(8,128)(2,1)}, bf16[2,256,384]{2,1,0:T(8,128)(2,1)S(1)}, u32[]{:S(2)}, u32[]{:S(2)}) %collective-permute-start.1) | collective-permute-done | bytes 393248 | tf_op jit(solution)/shard_map/ppermute | solution.py:499
  24.0 0.8 line_blocks.1
  24.8 1.7 %collective-permute-start.4 = (bf16[2,2,256,384]{3,2,1,0:T(8,128)(2,1)S(1)}, bf16[2,2,256,384]{3,2,1,0:T(8,128)(2,1)}, u32[]{:S(2)}, u32[]{:S(2)}) collective-permute-start(bf16[2,2,256,384]{3,2,1,0:T(8,128)(2,1)S(1)} %get-tuple-element.35.refs_5_), channel_id=1, source_target_pairs={{0,8},{2,10},{4,12},{6,14},{8,16},{10,18},{12,20},{14,22},{16,24},... | collective-permute-start | bytes 2359304 | tf_op jit(solution)/shard_map/ppermute | solution.py:504
  26.5 2.2 %collective-permute-start.5 = (bf16[2,2,256,384]{3,2,1,0:T(8,128)(2,1)S(1)}, bf16[2,2,256,384]{3,2,1,0:T(8,128)(2,1)}, u32[]{:S(2)}, u32[]{:S(2)}) collective-permute-start(bf16[2,2,256,384]{3,2,1,0:T(8,128)(2,1)S(1)} %get-tuple-element.34.refs_0_.after.refs_4_), channel_id=1, source_target_pairs={{0,120},{2,122},{4,124},{6,126},{8,0},{10,2},{12,4},{14,6},{16,8},... | collective-permute-start | bytes 2359304 | tf_op jit(solution)/shard_map/ppermute | solution.py:504
  28.7 3.0 %collective-permute-start.21 = (bf16[1536,1536]{1,0:T(8,128)(2,1)}, bf16[1536,1536]{1,0:T(8,128)(2,1)S(1)}, u32[]{:S(2)}, u32[]{:S(2)}) collective-permute-start(bf16[1536,1536]{1,0:T(8,128)(2,1)} %half_to_send.1.after), channel_id=1, source_target_pairs={{0,1},{1,0},{2,3},{3,2},{4,5},{5,4},{6,7},{7,6},{8,9},{9,8},{10,11... | collective-permute-start | bytes 14155784 | tf_op jit(solution)/shard_map/ppermute | solution.py:507
  31.7 7.9 %load_projections.1 = (bf16[1536,1536]{1,0:T(8,128)(2,1)S(1)}, bf16[1536,1536]{1,0:T(8,128)(2,1)S(1)}, bf16[1536,1536]{1,0:T(8,128)(2,1)}, f32[8,128]{1,0:T(8,128)S(1)}) custom-call(s32[2]{0:T(128)S(1)} %copy-done.4, bf16[1536,3072]{1,0:T(8,128)(2,1)} %v.3, bf16[1536,3072]{1,0:T(8,128)(2,1)} %a.7, ...), custom_call_target="tpu_custom_call" | custom-call | flops 8000000000 | bytes 1000 | tf_op jit(solution)/shard_map/load_projections/pallas_call | solution.py:116
  40.1 2.6 %collective-permute-start.3 = (bf16[2,512,384]{2,1,0:T(8,128)(2,1)S(1)}, bf16[2,512,384]{2,1,0:T(8,128)(2,1)S(1)}, u32[]{:S(2)}, u32[]{:S(2)}) collective-permute-start(bf16[2,512,384]{2,1,0:T(8,128)(2,1)S(1)} %pack.5.refs_9_), channel_id=1, source_target_pairs={{0,4},{2,6},{4,0},{6,2},{8,12},{10,14},{12,8},{14,10},{16,20},{18,... | collective-permute-start | bytes 2359304 | tf_op jit(solution)/shard_map/ppermute | solution.py:499
  42.7 1.0 collective-permute-done.4.refs_3_
  43.8 12.6 %attend.1 = (bf16[512,384]{1,0:T(8,128)(2,1)S(1)}, bf16[512,384]{1,0:T(8,128)(2,1)S(1)}, bf16[512,384]{1,0:T(8,128)(2,1)S(1)}, f32[3,8,144,256]{3,2,1,0:T(8,128)...) custom-call(s32[1]{0:T(128)} %bitcast.2.me.refs_0_, s32[64]{0:T(128)S(1)} %copy-done.5, ...), custom_call_target="tpu_custom_call" | custom-call | flops 17999998976 | bytes 1000 | tf_op jit(solution)/shard_map/attend/pallas_call | solution.py:320
  56.4 3.8 %collective-permute-start.10 = (bf16[512,384]{1,0:T(8,128)(2,1)S(1)}, bf16[512,384]{1,0:T(8,128)(2,1)S(1)}, u32[]{:S(2)}, u32[]{:S(2)}) collective-permute-start(bf16[512,384]{1,0:T(8,128)(2,1)S(1)} %get-tuple-element.45), channel_id=1, source_target_pairs={{0,2},{2,4},{4,6},{6,0},{8,10},{10,12},{12,14},{14,8},{16,18},{18,... | collective-permute-start | bytes 1179656 | tf_op jit(solution)/shard_map/ppermute | solution.py:499
  60.2 1.4 %collective-permute-start.9 = (bf16[512,384]{1,0:T(8,128)(2,1)S(1)}, bf16[512,384]{1,0:T(8,128)(2,1)S(1)}, u32[]{:S(2)}, u32[]{:S(2)}) collective-permute-start(bf16[512,384]{1,0:T(8,128)(2,1)S(1)} %get-tuple-element.44), channel_id=1, source_target_pairs={{0,6},{2,0},{4,2},{6,4},{8,14},{10,8},{12,10},{14,12},{16,22},{18,... | collective-permute-start | bytes 1179656 | tf_op jit(solution)/shard_map/ppermute | solution.py:499
  61.6 4.4 %attend_last.1 = (bf16[512,384]{1,0:T(8,128)(2,1)S(1)}, f32[3,8,144,256]{3,2,1,0:T(8,128)S(1)}, f32[3,8,8,256]{3,2,1,0:T(8,128)S(1)}, bf16[2,400,256]{2,1,0:T(8,128)(2,1)S(1)}, bf16[2,400,256]{2,1,0:T(8,128)(2,1)S(1)}) custom-call(s32[1]{0:T(128)} %bitcast.2.me.refs_0_, s32[64]{0:T(128)S(1)} %copy-done.5, ...), custom_call_target="tpu_custom_call", output_to_operand_aliasing={{1}: (5, {}), {2}: (6, {})} | custom-call | flops 6000000000 | bytes 1000 | tf_op jit(solution)/shard_map/attend_last/pallas_call | solution.py:320
  66.6 9.0 %collective-permute-start.12 = (bf16[2,400,256]{2,1,0:T(8,128)(2,1)S(1)}, bf16[2,400,256]{2,1,0:T(8,128)(2,1)S(1)}, u32[]{:S(2)}, u32[]{:S(2)}) collective-permute-start(bf16[2,400,256]{2,1,0:T(8,128)(2,1)S(1)} %get-tuple-element.52), channel_id=1, source_target_pairs={{0,120},{2,122},{4,124},{6,126},{8,0},{10,2},{12,4},{14,6},{16,8},... | collective-permute-start | bytes 1228808 | tf_op jit(solution)/shard_map/ppermute | solution.py:504
  75.7 6.3 %project_near.1 = (f32[512,1536]{1,0:T(8,128)S(1)}, f32[512,1536]{1,0:T(8,128)S(1)}) custom-call(s32[2]{0:T(128)S(1)} %copy-done.4, bf16[512,384]{1,0:T(8,128)(2,1)S(1)} %get-tuple-element.43.o0, bf16[512,384]{1,0:T(8,128)(2,1)S(1)} %collective-permute-done.9.o1, bf16[512,384]{1,0:T(8,128)(2,1)S(1)} %collective-permute-done.10.o3, ...), custom_call_target="tpu_custom_call" | custom-call | flops 4000000000 | bytes 1000 | tf_op jit(solution)/shard_map/project_near/pallas_call | solution.py:391
  82.0 1.6 %collective-permute-done.11.prev = bf16[2,400,256]{2,1,0:T(8,128)(2,1)S(1)} collective-permute-done((bf16[2,400,256]{2,1,0:T(8,128)(2,1)S(1)}, bf16[2,400,256]{2,1,0:T(8,128)(2,1)S(1)}, u32[]{:S(2)}, u32[]{:S(2)}) %collective-permute-start.11) | collective-permute-done | bytes 409632 | tf_op jit(solution)/shard_map/ppermute | solution.py:504
  84.1 1.6 %collective-permute-done.8.piece = bf16[512,384]{1,0:T(8,128)(2,1)S(1)} collective-permute-done((bf16[512,384]{1,0:T(8,128)(2,1)S(1)}, bf16[512,384]{1,0:T(8,128)(2,1)S(1)}, u32[]{:S(2)}, u32[]{:S(2)}) %collective-permute-start.8) | collective-permute-done | bytes 393248 | tf_op jit(solution)/shard_map/ppermute | solution.py:499
  85.7 1.6 %project_far.2 = bf16[512,1536]{1,0:T(8,128)(2,1)S(1)} custom-call(s32[2]{0:T(128)S(1)} %copy-done.4, bf16[512,384]{1,0:T(8,128)(2,1)S(1)} %collective-permute-done.8.piece, bf16[1536,1536]{1,0:T(8,128)(2,1)S(1)} %get-tuple-element.46.w_other.w, f32[512,1536]{1,0:T(8,128)S(1)} %get-tuple-element.48.refs_0_, ...), custom_call_target="tpu_custom_call" | custom-call | flops 500000000 | bytes 1000 | tf_op jit(solution)/shard_map/project_far/pallas_call | solution.py:428
  87.3 3.0 %collective-permute-start.13 = (bf16[512,1536]{1,0:T(8,128)(2,1)S(1)}, bf16[512,1536]{1,0:T(8,128)(2,1)S(1)}, u32[]{:S(2)}, u32[]{:S(2)}) collective-permute-start(bf16[512,1536]{1,0:T(8,128)(2,1)S(1)} %project_far.2), channel_id=1, source_target_pairs={{0,1},{1,0},{2,3},{3,2},{4,5},{5,4},{6,7},{7,6},{8,9},{9,8},{10,11... | collective-permute-start | bytes 4718600 | tf_op jit(solution)/shard_map/ppermute | solution.py:507
  90.4 1.4 %collective-permute-start.16 = (bf16[256,384]{1,0:T(8,128)(2,1)S(1)}, bf16[256,384]{1,0:T(8,128)(2,1)S(1)}, u32[]{:S(2)}, u32[]{:S(2)}) collective-permute-start(bf16[256,384]{1,0:T(8,128)(2,1)S(1)} %get-tuple-element.56), channel_id=1, source_target_pairs={{0,2},{2,4},{4,6},{6,0},{8,10},{10,12},{12,14},{14,8},{16,18},{18,... | collective-permute-start | bytes 589832 | tf_op jit(solution)/shard_map/ppermute | solution.py:499
  91.8 5.0 %collective-permute-done.14.refs_1_ = bf16[256,384]{1,0:T(8,128)(2,1)S(1)} collective-permute-done((bf16[256,384]{1,0:T(8,128)(2,1)S(1)}, bf16[256,384]{1,0:T(8,128)(2,1)S(1)}, u32[]{:S(2)}, u32[]{:S(2)}) %collective-permute-start.14) | collective-permute-done | bytes 196640 | tf_op jit(solution)/shard_map/ppermute | solution.py:499
  96.8 1.3 %collective-permute-start.17 = (bf16[256,384]{1,0:T(8,128)(2,1)S(1)}, bf16[256,384]{1,0:T(8,128)(2,1)S(1)}, u32[]{:S(2)}, u32[]{:S(2)}) collective-permute-start(bf16[256,384]{1,0:T(8,128)(2,1)S(1)} %get-tuple-element.53.refs_1_.refs_0_), channel_id=1, source_target_pairs={{0,1},{1,0},{2,3},{3,2},{4,5},{5,4},{6,7},{7,6},{8,9},{9,8},{10,11... | collective-permute-start | bytes 589832 | tf_op jit(solution)/shard_map/ppermute | solution.py:507
  98.2 1.6 %collective-permute-start.18 = (bf16[256,384]{1,0:T(8,128)(2,1)S(1)}, bf16[256,384]{1,0:T(8,128)(2,1)S(1)}, u32[]{:S(2)}, u32[]{:S(2)}) collective-permute-start(bf16[256,384]{1,0:T(8,128)(2,1)S(1)} %collective-permute-done.14.refs_1_), channel_id=1, source_target_pairs={{0,1},{1,0},{2,3},{3,2},{4,5},{5,4},{6,7},{7,6},{8,9},{9,8},{10,11... | collective-permute-start | bytes 589832 | tf_op jit(solution)/shard_map/ppermute | solution.py:507
  99.8 3.1 %collective-permute-done.16.refs_3_ = bf16[256,384]{1,0:T(8,128)(2,1)S(1)} collective-permute-done((bf16[256,384]{1,0:T(8,128)(2,1)S(1)}, bf16[256,384]{1,0:T(8,128)(2,1)S(1)}, u32[]{:S(2)}, u32[]{:S(2)}) %collective-permute-start.16) | collective-permute-done | bytes 196640 | tf_op jit(solution)/shard_map/ppermute | solution.py:499
  103.4 2.4 %project_far.3 = bf16[512,1536]{1,0:T(8,128)(2,1)} custom-call(s32[2]{0:T(128)S(1)} %copy-done.4, bf16[512,384]{1,0:T(8,128)(2,1)S(1)} %collective-permute-done.8.piece, bf16[1536,1536]{1,0:T(8,128)(2,1)S(1)} %get-tuple-element.42.w_own.w, f32[512,1536]{1,0:T(8,128)S(1)} %get-tuple-element.47.refs_0_, bf16[512,1536]{1,0:T(8,128)(2,1)S(1)} %collective-permute-done.13.refs_1_), custom_call_target="tpu_custom_call" | custom-call | flops 500000000 | bytes 1000 | tf_op jit(solution)/shard_map/project_far/pallas_call | solution.py:428
  105.9 4.3 %project.1 = bf16[256,1536]{1,0:T(8,128)(2,1)} custom-call(s32[2]{0:T(128)S(1)} %copy-done.4, bf16[256,384]{1,0:T(8,128)(2,1)S(1)} %get-tuple-element.53.refs_1_.refs_0_, bf16[256,384]{1,0:T(8,128)(2,1)S(1)} %collective-permute-done.14.refs_1_, bf16[256,384]{1,0:T(8,128)(2,1)S(1)} %collective-permute-done.15.refs_2_, ...), custom_call_target="tpu_custom_call" | custom-call | flops 4000000000 | bytes 1000 | tf_op jit(solution)/shard_map/project/pallas_call | solution.py:472
  (45 shorter events, 3.7 us)
Async XLA Ops:
  2.8 15.2 %collective-permute-start = (bf16[2,256,384]{2,1,0:T(8,128)(2,1)}, bf16[2,256,384]{2,1,0:T(8,128)(2,1)S(1)}, u32[]{:S(2)}, u32[]{:S(2)}) collective-permute-start(bf16[2,256,384]{2,1,0:T(8,128)(2,1)} %get-tuple-element.30.refs_0_), channel_id=1, source_target_pairs={{0,2},{2,4},{4,6},{6,0},{8,10},{10,12},{12,14},{14,8},{16,18},{18,... | collective-permute-start | bytes 1179656 | tf_op jit(solution)/shard_map/ppermute | solution.py:499
  4.2 19.8 %collective-permute-start.1 = (bf16[2,256,384]{2,1,0:T(8,128)(2,1)}, bf16[2,256,384]{2,1,0:T(8,128)(2,1)S(1)}, u32[]{:S(2)}, u32[]{:S(2)}) collective-permute-start(bf16[2,256,384]{2,1,0:T(8,128)(2,1)} %get-tuple-element.31), channel_id=1, source_target_pairs={{0,4},{2,6},{4,0},{6,2},{8,12},{10,14},{12,8},{14,10},{16,20},{18,... | collective-permute-start | bytes 1179656 | tf_op jit(solution)/shard_map/ppermute | solution.py:499
  6.8 17.2 %collective-permute-start.2 = (bf16[2,256,384]{2,1,0:T(8,128)(2,1)}, bf16[2,256,384]{2,1,0:T(8,128)(2,1)S(1)}, u32[]{:S(2)}, u32[]{:S(2)}) collective-permute-start(bf16[2,256,384]{2,1,0:T(8,128)(2,1)} %get-tuple-element.32), channel_id=1, source_target_pairs={{0,6},{2,0},{4,2},{6,4},{8,14},{10,8},{12,10},{14,12},{16,22},{18,... | collective-permute-start | bytes 1179656 | tf_op jit(solution)/shard_map/ppermute | solution.py:499
  10.1 30.1 %collective-permute-start.6 = (bf16[2,512,384]{2,1,0:T(8,128)(2,1)}, bf16[2,512,384]{2,1,0:T(8,128)(2,1)S(1)}, u32[]{:S(2)}, u32[]{:S(2)}) collective-permute-start(bf16[2,512,384]{2,1,0:T(8,128)(2,1)} %get-tuple-element.33.after), channel_id=1, source_target_pairs={{0,2},{2,4},{4,6},{6,0},{8,10},{10,12},{12,14},{14,8},{16,18},{18,... | collective-permute-start | bytes 2359304 | tf_op jit(solution)/shard_map/ppermute | solution.py:499
  10.5 32.2 %collective-permute-start.7 = (bf16[2,512,384]{2,1,0:T(8,128)(2,1)}, bf16[2,512,384]{2,1,0:T(8,128)(2,1)}, u32[]{:S(2)}, u32[]{:S(2)}) collective-permute-start(bf16[2,512,384]{2,1,0:T(8,128)(2,1)} %get-tuple-element.37), channel_id=1, source_target_pairs={{0,6},{2,0},{4,2},{6,4},{8,14},{10,8},{12,10},{14,12},{16,22},{18,... | collective-permute-start | bytes 2359304 | tf_op jit(solution)/shard_map/ppermute | solution.py:499
  13.5 10.5 %copy-start.2 = (bf16[256,1536]{1,0:T(8,128)(2,1)S(1)}, bf16[256,1536]{1,0:T(8,128)(2,1)}, u32[]{:S(2)}) copy-start(bf16[256,1536]{1,0:T(8,128)(2,1)} %k.1) | copy-start | bytes 2359300
  13.5 10.5 %copy-start.3 = (bf16[256,1536]{1,0:T(8,128)(2,1)S(1)}, bf16[256,1536]{1,0:T(8,128)(2,1)}, u32[]{:S(2)}) copy-start(bf16[256,1536]{1,0:T(8,128)(2,1)} %v.2) | copy-start | bytes 2359300
  18.0 13.7 %copy-start.4 = (s32[2]{0:T(128)S(1)}, s32[2]{0:T(128)}, u32[]{:S(2)}) copy-start(s32[2]{0:T(128)} %pad_add_fusion.place) | copy-start | bytes 28
  24.8 18.9 %collective-permute-start.4 = (bf16[2,2,256,384]{3,2,1,0:T(8,128)(2,1)S(1)}, bf16[2,2,256,384]{3,2,1,0:T(8,128)(2,1)}, u32[]{:S(2)}, u32[]{:S(2)}) collective-permute-start(bf16[2,2,256,384]{3,2,1,0:T(8,128)(2,1)S(1)} %get-tuple-element.35.refs_5_), channel_id=1, source_target_pairs={{0,8},{2,10},{4,12},{6,14},{8,16},{10,18},{12,20},{14,22},{16,24},... | collective-permute-start | bytes 2359304 | tf_op jit(solution)/shard_map/ppermute | solution.py:504
  26.5 13.1 %copy-start = (bf16[512,1536]{1,0:T(8,128)(2,1)S(1)}, bf16[512,1536]{1,0:T(8,128)(2,1)}, u32[]{:S(2)}) copy-start(bf16[512,1536]{1,0:T(8,128)(2,1)} %refs_7_.1) | copy-start | bytes 4718596
  26.5 13.1 %copy-start.1 = (bf16[512,1536]{1,0:T(8,128)(2,1)S(1)}, bf16[512,1536]{1,0:T(8,128)(2,1)}, u32[]{:S(2)}) copy-start(bf16[512,1536]{1,0:T(8,128)(2,1)} %refs_8_.1) | copy-start | bytes 4718596
  26.5 17.2 %collective-permute-start.5 = (bf16[2,2,256,384]{3,2,1,0:T(8,128)(2,1)S(1)}, bf16[2,2,256,384]{3,2,1,0:T(8,128)(2,1)}, u32[]{:S(2)}, u32[]{:S(2)}) collective-permute-start(bf16[2,2,256,384]{3,2,1,0:T(8,128)(2,1)S(1)} %get-tuple-element.34.refs_0_.after.refs_4_), channel_id=1, source_target_pairs={{0,120},{2,122},{4,124},{6,126},{8,0},{10,2},{12,4},{14,6},{16,8},... | collective-permute-start | bytes 2359304 | tf_op jit(solution)/shard_map/ppermute | solution.py:504
  28.7 77.1 %collective-permute-start.21 = (bf16[1536,1536]{1,0:T(8,128)(2,1)}, bf16[1536,1536]{1,0:T(8,128)(2,1)S(1)}, u32[]{:S(2)}, u32[]{:S(2)}) collective-permute-start(bf16[1536,1536]{1,0:T(8,128)(2,1)} %half_to_send.1.after), channel_id=1, source_target_pairs={{0,1},{1,0},{2,3},{3,2},{4,5},{5,4},{6,7},{7,6},{8,9},{9,8},{10,11... | collective-permute-start | bytes 14155784 | tf_op jit(solution)/shard_map/ppermute | solution.py:507
  39.6 4.2 %copy-start.5 = (s32[64]{0:T(128)S(1)}, s32[64]{0:T(128)}, u32[]{:S(2)}) copy-start(s32[64]{0:T(128)} %refs_1_.3) | copy-start | bytes 772
  39.6 4.1 %copy-start.6 = (s32[64]{0:T(128)S(1)}, s32[64]{0:T(128)}, u32[]{:S(2)}) copy-start(s32[64]{0:T(128)} %refs_2_.3) | copy-start | bytes 772
  40.1 21.4 %collective-permute-start.3 = (bf16[2,512,384]{2,1,0:T(8,128)(2,1)S(1)}, bf16[2,512,384]{2,1,0:T(8,128)(2,1)S(1)}, u32[]{:S(2)}, u32[]{:S(2)}) collective-permute-start(bf16[2,512,384]{2,1,0:T(8,128)(2,1)S(1)} %pack.5.refs_9_), channel_id=1, source_target_pairs={{0,4},{2,6},{4,0},{6,2},{8,12},{10,14},{12,8},{14,10},{16,20},{18,... | collective-permute-start | bytes 2359304 | tf_op jit(solution)/shard_map/ppermute | solution.py:499
  56.4 19.2 %collective-permute-start.10 = (bf16[512,384]{1,0:T(8,128)(2,1)S(1)}, bf16[512,384]{1,0:T(8,128)(2,1)S(1)}, u32[]{:S(2)}, u32[]{:S(2)}) collective-permute-start(bf16[512,384]{1,0:T(8,128)(2,1)S(1)} %get-tuple-element.45), channel_id=1, source_target_pairs={{0,2},{2,4},{4,6},{6,0},{8,10},{10,12},{12,14},{14,8},{16,18},{18,... | collective-permute-start | bytes 1179656 | tf_op jit(solution)/shard_map/ppermute | solution.py:499
  60.2 15.5 %collective-permute-start.9 = (bf16[512,384]{1,0:T(8,128)(2,1)S(1)}, bf16[512,384]{1,0:T(8,128)(2,1)S(1)}, u32[]{:S(2)}, u32[]{:S(2)}) collective-permute-start(bf16[512,384]{1,0:T(8,128)(2,1)S(1)} %get-tuple-element.44), channel_id=1, source_target_pairs={{0,6},{2,0},{4,2},{6,4},{8,14},{10,8},{12,10},{14,12},{16,22},{18,... | collective-permute-start | bytes 1179656 | tf_op jit(solution)/shard_map/ppermute | solution.py:499
  66.0 17.5 %collective-permute-start.11 = (bf16[2,400,256]{2,1,0:T(8,128)(2,1)S(1)}, bf16[2,400,256]{2,1,0:T(8,128)(2,1)S(1)}, u32[]{:S(2)}, u32[]{:S(2)}) collective-permute-start(bf16[2,400,256]{2,1,0:T(8,128)(2,1)S(1)} %get-tuple-element.51), channel_id=1, source_target_pairs={{0,8},{2,10},{4,12},{6,14},{8,16},{10,18},{12,20},{14,22},{16,24},... | collective-permute-start | bytes 1228808 | tf_op jit(solution)/shard_map/ppermute | solution.py:504
  66.6 17.0 %collective-permute-start.12 = (bf16[2,400,256]{2,1,0:T(8,128)(2,1)S(1)}, bf16[2,400,256]{2,1,0:T(8,128)(2,1)S(1)}, u32[]{:S(2)}, u32[]{:S(2)}) collective-permute-start(bf16[2,400,256]{2,1,0:T(8,128)(2,1)S(1)} %get-tuple-element.52), channel_id=1, source_target_pairs={{0,120},{2,122},{4,124},{6,126},{8,0},{10,2},{12,4},{14,6},{16,8},... | collective-permute-start | bytes 1228808 | tf_op jit(solution)/shard_map/ppermute | solution.py:504
  75.6 10.1 %collective-permute-start.8 = (bf16[512,384]{1,0:T(8,128)(2,1)S(1)}, bf16[512,384]{1,0:T(8,128)(2,1)S(1)}, u32[]{:S(2)}, u32[]{:S(2)}) collective-permute-start(bf16[512,384]{1,0:T(8,128)(2,1)S(1)} %get-tuple-element.41), channel_id=1, source_target_pairs={{0,4},{2,6},{4,0},{6,2},{8,12},{10,14},{12,8},{14,10},{16,20},{18,... | collective-permute-start | bytes 1179656 | tf_op jit(solution)/shard_map/ppermute | solution.py:499
  85.7 20.2 %slice-start = ((s8[4718592]{0:T(1024)(128)(4,1)}), s8[4194304]{0:T(1024)(128)(4,1)S(1)}, s32[]{:S(2)}) async-start(s8[4718592]{0:T(1024)(128)(4,1)} %bitcast.3), calls=%async_computation | async-start | bytes 8388608
  87.3 16.1 %collective-permute-start.13 = (bf16[512,1536]{1,0:T(8,128)(2,1)S(1)}, bf16[512,1536]{1,0:T(8,128)(2,1)S(1)}, u32[]{:S(2)}, u32[]{:S(2)}) collective-permute-start(bf16[512,1536]{1,0:T(8,128)(2,1)S(1)} %project_far.2), channel_id=1, source_target_pairs={{0,1},{1,0},{2,3},{3,2},{4,5},{5,4},{6,7},{7,6},{8,9},{9,8},{10,11... | collective-permute-start | bytes 4718600 | tf_op jit(solution)/shard_map/ppermute | solution.py:507
  90.3 6.5 %collective-permute-start.14 = (bf16[256,384]{1,0:T(8,128)(2,1)S(1)}, bf16[256,384]{1,0:T(8,128)(2,1)S(1)}, u32[]{:S(2)}, u32[]{:S(2)}) collective-permute-start(bf16[256,384]{1,0:T(8,128)(2,1)S(1)} %get-tuple-element.54), channel_id=1, source_target_pairs={{0,6},{2,0},{4,2},{6,4},{8,14},{10,8},{12,10},{14,12},{16,22},{18,... | collective-permute-start | bytes 589832 | tf_op jit(solution)/shard_map/ppermute | solution.py:499
  90.3 7.9 %collective-permute-start.15 = (bf16[256,384]{1,0:T(8,128)(2,1)S(1)}, bf16[256,384]{1,0:T(8,128)(2,1)S(1)}, u32[]{:S(2)}, u32[]{:S(2)}) collective-permute-start(bf16[256,384]{1,0:T(8,128)(2,1)S(1)} %get-tuple-element.55), channel_id=1, source_target_pairs={{0,4},{2,6},{4,0},{6,2},{8,12},{10,14},{12,8},{14,10},{16,20},{18,... | collective-permute-start | bytes 589832 | tf_op jit(solution)/shard_map/ppermute | solution.py:499
  90.4 12.5 %collective-permute-start.16 = (bf16[256,384]{1,0:T(8,128)(2,1)S(1)}, bf16[256,384]{1,0:T(8,128)(2,1)S(1)}, u32[]{:S(2)}, u32[]{:S(2)}) collective-permute-start(bf16[256,384]{1,0:T(8,128)(2,1)S(1)} %get-tuple-element.56), channel_id=1, source_target_pairs={{0,2},{2,4},{4,6},{6,0},{8,10},{10,12},{12,14},{14,8},{16,18},{18,... | collective-permute-start | bytes 589832 | tf_op jit(solution)/shard_map/ppermute | solution.py:499
  96.8 9.0 %collective-permute-start.17 = (bf16[256,384]{1,0:T(8,128)(2,1)S(1)}, bf16[256,384]{1,0:T(8,128)(2,1)S(1)}, u32[]{:S(2)}, u32[]{:S(2)}) collective-permute-start(bf16[256,384]{1,0:T(8,128)(2,1)S(1)} %get-tuple-element.53.refs_1_.refs_0_), channel_id=1, source_target_pairs={{0,1},{1,0},{2,3},{3,2},{4,5},{5,4},{6,7},{7,6},{8,9},{9,8},{10,11... | collective-permute-start | bytes 589832 | tf_op jit(solution)/shard_map/ppermute | solution.py:507
  98.2 7.6 %collective-permute-start.18 = (bf16[256,384]{1,0:T(8,128)(2,1)S(1)}, bf16[256,384]{1,0:T(8,128)(2,1)S(1)}, u32[]{:S(2)}, u32[]{:S(2)}) collective-permute-start(bf16[256,384]{1,0:T(8,128)(2,1)S(1)} %collective-permute-done.14.refs_1_), channel_id=1, source_target_pairs={{0,1},{1,0},{2,3},{3,2},{4,5},{5,4},{6,7},{7,6},{8,9},{9,8},{10,11... | collective-permute-start | bytes 589832 | tf_op jit(solution)/shard_map/ppermute | solution.py:507
  102.9 2.9 %collective-permute-start.19 = (bf16[256,384]{1,0:T(8,128)(2,1)S(1)}, bf16[256,384]{1,0:T(8,128)(2,1)S(1)}, u32[]{:S(2)}, u32[]{:S(2)}) collective-permute-start(bf16[256,384]{1,0:T(8,128)(2,1)S(1)} %collective-permute-done.15.refs_2_), channel_id=1, source_target_pairs={{0,1},{1,0},{2,3},{3,2},{4,5},{5,4},{6,7},{7,6},{8,9},{9,8},{10,11... | collective-permute-start | bytes 589832 | tf_op jit(solution)/shard_map/ppermute | solution.py:507
  103.4 2.5 %collective-permute-start.20 = (bf16[256,384]{1,0:T(8,128)(2,1)S(1)}, bf16[256,384]{1,0:T(8,128)(2,1)S(1)}, u32[]{:S(2)}, u32[]{:S(2)}) collective-permute-start(bf16[256,384]{1,0:T(8,128)(2,1)S(1)} %collective-permute-done.16.refs_3_), channel_id=1, source_target_pairs={{0,1},{1,0},{2,3},{3,2},{4,5},{5,4},{6,7},{7,6},{8,9},{9,8},{10,11... | collective-permute-start | bytes 589832 | tf_op jit(solution)/shard_map/ppermute | solution.py:507
  103.4 2.5 %slice-start.1 = ((s8[4718592]{0:T(1024)(128)(4,1)}), s8[524288]{0:T(1024)(128)(4,1)S(1)}, s32[]{:S(2)}) async-start(s8[4718592]{0:T(1024)(128)(4,1)} %bitcast.3), calls=%async_computation.1 | async-start | bytes 1048576
